TPU v7x, 32 devices: a whole 2x2x4 slice. The times are simulated.
32 devices in a mesh: dom: 32 (over z, y, x, core).
Axes of the slice: x: 2, y: 2, z: 4, core: 2. Of those that a mesh axis runs over, the one named last changes fastest.
Arguments:
- right_side: float32 [512, 320], P('dom'), may hold values from -6 to 6
- start_state: float32 [512, 320], P('dom'), may hold values from -6 to 6
- pivot_inverse: bfloat16 [512, 320, 320], P('dom')
- lower_block: bfloat16 [512, 320, 320], P('dom'), may hold values from -0.15625 to 0.15625
- upper_block: bfloat16 [512, 320, 320], P('dom'), may hold values from -0.15625 to 0.15625
- face_blocks: bfloat16 [512, 4, 320, 320], P('dom'), may hold values from -0.15625 to 0.15625
- neighbours: int32 [4, 512], P(None, 'dom'), may hold values from -1 to 511, as said below
- element_slot: int32 [512], P('dom'), may hold values from 0 to 1023, as said below
Outputs:
- new_state: float32 [512, 320], P('dom')
Inputs may be any that keep to these rules, and one draw needn't show every extreme that they name: `neighbours`: an entry -1 marks a boundary face; any other entry n of element e satisfies |n // 16 - e // 16| <= 1. Distinct elements have distinct values. The owner element_slot[e] // 32 differs from e // 16 by at most one. At most 8 elements of one partition have the owner below it and at most 8 the owner above it; in every draw some partition sends 8 each way, and some owner has all 32 slots taken.
All inputs are finite; a program needn't handle non-finite values.
Results may differ from a plain program's by a relative error of at most 0.0095.
Values may be sent and summed in bfloat16 or wider, within the bound.
No kernel may reach another device: no remote copies, remote signals or barrier semaphores. Data moves between devices by JAX's collectives and lax.ppermute only.
A program may use at most 128 MiB of HBM per device.

v0:
```python
import jax
import jax.numpy as jnp
import numpy as np
from jax import lax
from jax.sharding import PartitionSpec as P

LMAX = 8
SWEEPS = 2


def with_halo(array, sides, width):
    for axis, dim in sides:
        devices, length = (lax.axis_size(axis), array.shape[dim])
        up = [(i, (i + 1) % devices) for i in range(devices - 1)]
        down = [(j, i) for i, j in up]
        last = lax.slice_in_dim(array, length - width, length, axis=dim)
        initial = lax.slice_in_dim(array, 0, width, axis=dim)
        before = lax.ppermute(last, axis, up)
        after = lax.ppermute(initial, axis, down)
        array = jnp.concatenate([before, array, after], axis=dim)
    return array


def pack_order(selected, bucket):
    ordering = jnp.cumsum(selected.astype(jnp.int32)) - 1
    positions = jnp.arange(bucket, dtype=jnp.int32)[:, None]
    matches = selected[None, :] & (ordering[None, :] == positions)
    members = jnp.arange(selected.shape[0], dtype=jnp.int32)[None, :]
    picked = jnp.sum(jnp.where(matches, members, 0), axis=1)
    return (picked, jnp.any(matches, axis=1), jnp.maximum(ordering, 0))


def premultiply(first_block, second_block):
    return jnp.einsum(
        "eij,ejk->eik", first_block, second_block, preferred_element_type=jnp.float32
    ).astype(jnp.bfloat16)


def apply_blocks(blocks, vectors):
    return jnp.einsum("eij,ej->ei", blocks, vectors, preferred_element_type=jnp.float32)


def split_rims(arrived, bucket, elem_count):
    return (arrived[:bucket], arrived[bucket + elem_count :])


def body(
    right_side,
    start_state,
    pivot_inverse,
    lower_block,
    upper_block,
    face_blocks,
    neighbours,
    element_slot,
):
    elem_count = right_side.shape[0]
    bucket = elem_count // 2
    slot_count = 2 * elem_count
    line_count = slot_count // LMAX
    device_index = lax.axis_index("dom")
    slot_rim = with_halo(element_slot, (("dom", 0),), elem_count)
    rim_below = slot_rim[:elem_count]
    own_slots = slot_rim[elem_count : 2 * elem_count]
    rim_above = slot_rim[2 * elem_count :]
    own_owner = own_slots // slot_count
    goes_down = own_owner == device_index - 1
    goes_up = own_owner == device_index + 1
    stays = own_owner == device_index
    down_index, down_valid, down_rank = pack_order(goes_down, bucket)
    up_index, up_valid, up_rank = pack_order(goes_up, bucket)
    send_index = jnp.concatenate([down_index, up_index])
    from_below = (rim_below // slot_count == device_index) & (device_index > 0)
    from_above = rim_above // slot_count == device_index
    below_index, below_valid, below_rank = pack_order(from_below, bucket)
    above_index, above_valid, above_rank = pack_order(from_above, bucket)
    item_slot = jnp.concatenate(
        [
            jnp.where(below_valid, rim_below[below_index] % slot_count, -1),
            jnp.where(stays, own_slots % slot_count, -1),
            jnp.where(above_valid, rim_above[above_index] % slot_count, -1),
        ]
    )
    slot_matches = item_slot[None, :] == jnp.arange(slot_count, dtype=jnp.int32)[:, None]
    slot_item = jnp.sum(
        jnp.where(slot_matches, jnp.arange(slot_count, dtype=jnp.int32)[None, :], 0), axis=1
    )
    slot_live = jnp.any(slot_matches, axis=1)
    outgoing = jnp.stack(
        [pivot_inverse[send_index], lower_block[send_index], upper_block[send_index]], axis=1
    )
    arrived = with_halo(outgoing, (("dom", 0),), bucket)
    low_rim, high_rim = split_rims(arrived, bucket, elem_count)
    item_lower = jnp.concatenate(
        [
            premultiply(low_rim[:, 0], low_rim[:, 1]),
            premultiply(pivot_inverse, lower_block),
            premultiply(high_rim[:, 0], high_rim[:, 1]),
        ]
    )
    item_upper = jnp.concatenate(
        [
            premultiply(low_rim[:, 0], low_rim[:, 2]),
            premultiply(pivot_inverse, upper_block),
            premultiply(high_rim[:, 0], high_rim[:, 2]),
        ]
    )
    across = neighbours.T
    face_live = across >= 0
    local_face = jnp.clip(across - (device_index - 1) * elem_count, 0, 3 * elem_count - 1)
    row_starts = np.arange(line_count) * LMAX
    width = right_side.shape[1]
    current = start_state
    for sweep_step in range(SWEEPS):
        rounded = current.astype(jnp.bfloat16)
        extended = with_halo(rounded, (("dom", 0),), elem_count)
        neighbour_states = jnp.where(
            face_live[:, :, None], extended[local_face], jnp.zeros((), jnp.bfloat16)
        )
        face_sum = jnp.einsum(
            "efij,efj->ei", face_blocks, neighbour_states, preferred_element_type=jnp.float32
        )
        residual = (right_side - face_sum).astype(jnp.bfloat16)
        arrived_residual = with_halo(residual[send_index], (("dom", 0),), bucket)
        low_residual, high_residual = split_rims(arrived_residual, bucket, elem_count)
        item_scaled = jnp.concatenate(
            [
                apply_blocks(low_rim[:, 0], low_residual),
                apply_blocks(pivot_inverse, residual),
                apply_blocks(high_rim[:, 0], high_residual),
            ]
        )
        previous = jnp.zeros((line_count, width), jnp.bfloat16)
        forward = []
        for position in range(LMAX):
            items_here = slot_item[row_starts + position]
            live = slot_live[row_starts + position][:, None]
            carried = jnp.einsum(
                "rij,rj->ri", item_lower[items_here], previous, preferred_element_type=jnp.float32
            )
            value = jnp.where(live, item_scaled[items_here] - carried, jnp.zeros((), jnp.float32))
            forward.append(value)
            previous = value.astype(jnp.bfloat16)
        following = jnp.zeros((line_count, width), jnp.bfloat16)
        backward = [None] * LMAX
        for position in reversed(range(LMAX)):
            items_here = slot_item[row_starts + position]
            live = slot_live[row_starts + position][:, None]
            carried = jnp.einsum(
                "rij,rj->ri", item_upper[items_here], following, preferred_element_type=jnp.float32
            )
            value = jnp.where(live, forward[position] - carried, jnp.zeros((), jnp.float32))
            backward[position] = value
            following = value.astype(jnp.bfloat16)
        solved_slots = jnp.stack(backward, axis=1).reshape(slot_count, width)
        solved_items = solved_slots[jnp.maximum(item_slot, 0)]
        going_back = jnp.concatenate([solved_items[:bucket], solved_items[bucket + elem_count :]])
        returned = with_halo(going_back, (("dom", 0),), bucket)
        low_solved, high_solved = split_rims(returned, bucket, elem_count)
        own_solved = solved_items[bucket : bucket + elem_count]
        current = jnp.where(
            stays[:, None],
            own_solved,
            jnp.where(
                goes_down[:, None],
                low_solved[jnp.minimum(down_rank, bucket - 1)],
                high_solved[jnp.minimum(up_rank, bucket - 1)],
            ),
        )
    return current


def solution(mesh):
    placed = (
        P("dom", None),
        P("dom", None),
        P("dom", None, None),
        P("dom", None, None),
        P("dom", None, None),
        P("dom", None, None, None),
        P(None, "dom"),
        P("dom"),
    )
    return jax.shard_map(
        body, mesh=mesh, in_specs=placed, out_specs=P("dom", None), check_vma=False
    )
```

profile of v0, /device:TPU:23, one launch (start us, length us, event | category | flops | bytes accessed | tf_op | source)
XLA Modules:
  0.0 360.1 jit_solution(10052630943697925046)
XLA Ops:
  0.0 2.6 collective-permute-start.1
  2.6 4.8 %collective-permute-start = (s32[16]{0:T(128)}, s32[16]{0:T(128)S(1)}, u32[]{:S(2)}, u32[]{:S(2)}) collective-permute-start(s32[16]{0:T(128)} %param.143), channel_id=1, source_target_pairs={{0,1},{1,2},{2,3},{3,4},{4,5},{5,6},{6,7},{7,8},{8,9},{9,10},{10,1... | collective-permute-start | bytes 200 | tf_op jit(solution)/shard_map/ppermute | solution.py:18
  10.0 5.4 %collective-permute-start.3 = (bf16[16,320]{1,0:T(8,128)(2,1)S(1)}, bf16[16,320]{1,0:T(8,128)(2,1)S(1)}, u32[]{:S(2)}, u32[]{:S(2)}) collective-permute-start(bf16[16,320]{1,0:T(8,128)(2,1)S(1)} %convert_element_type.118), channel_id=1, source_target_pairs={{0,1},{1,2},{2,3},{3,4},{4,5},{5,6},{6,7},{7,8},{8,9},{9,10},{10,1... | collective-permute-start | bytes 30728 | tf_op jit(solution)/shard_map/ppermute | solution.py:18
  17.1 5.1 %gather_fusion.5 = bf16[16,320,320]{2,1,0:T(8,128)(2,1)} fusion(bf16[16,320,320]{2,1,0:T(8,128)(2,1)} %param.140, s32[1024]{0:T(1024)S(1)} %pad_clamp_fusion.19), kind=kCustom, calls=%fused_computation.5 | custom fusion | bytes 6553664 | tf_op jit(solution)/shard_map/gather | solution.py:90
  22.2 5.1 %gather_fusion.4 = bf16[16,320,320]{2,1,0:T(8,128)(2,1)} fusion(bf16[16,320,320]{2,1,0:T(8,128)(2,1)} %param.139, s32[1024]{0:T(1024)S(1)} %pad_clamp_fusion.19), kind=kCustom, calls=%fused_computation.4 | custom fusion | bytes 6553664 | tf_op jit(solution)/shard_map/gather | solution.py:90
  27.3 5.2 %gather_fusion.3 = bf16[16,320,320]{2,1,0:T(8,128)(2,1)} fusion(bf16[16,320,320]{2,1,0:T(8,128)(2,1)} %param.138, s32[1024]{0:T(1024)S(1)} %pad_clamp_fusion.19), kind=kCustom, calls=%fused_computation.3 | custom fusion | bytes 6553664 | tf_op jit(solution)/shard_map/gather | solution.py:90
  32.5 7.4 %pad_maximum_fusion = bf16[16,3,320,320]{3,2,0,1:T(8,128)(2,1)S(1)} fusion(bf16[16,1,320,320]{3,2,0,1:T(8,128)(2,1)} %bitcast.473, bf16[16,1,320,320]{3,2,0,1:T(8,128)(2,1)} %bitcast.474, bf16[16,1,320,320]{3,2,0,1:T(8,128)(2,1)} %bitcast.475), kind=kLoop, calls=%fused_computation.63 | loop fusion | flops 9830400 | bytes 19660800 | tf_op jit(solution)/shard_map/stack | solution.py:89
  39.8 4.8 %fusion.157 = (bf16[8,3,320,320]{3,2,0,1:T(8,128)(2,1)}, bf16[8,3,320,320]{3,2,0,1:T(8,128)(2,1)}) fusion(bf16[16,3,320,320]{3,2,0,1:T(8,128)(2,1)S(1)} %pad_maximum_fusion), kind=kLoop, calls=%fused_computation.399 | loop fusion | bytes 19660800 | tf_op jit(solution)/shard_map/slice | solution.py:16
  46.6 7.9 %convolution_convert_fusion.1 = bf16[16,320,320]{2,1,0:T(8,128)(2,1)} fusion(bf16[16,320,320]{2,1,0:T(8,128)(2,1)} %param.138, bf16[16,320,320]{2,1,0:T(8,128)(2,1)} %param.139), kind=kOutput, calls=%fused_computation.67 | convolution fusion | flops 1050214400 | bytes 9830400 | tf_op jit(solution)/shard_map/eij,ejk->eik/dot_general | solution.py:34
  54.6 4.0 %convolution_convert_fusion = bf16[16,320,320]{2,1,0:T(8,128)(2,1)} fusion(bf16[16,320,320]{2,1,0:T(8,128)(2,1)S(1)} %copy-done, bf16[16,320,320]{2,1,0:T(8,128)(2,1)S(1)} %copy-done.1), kind=kOutput, calls=%fused_computation.66 | convolution fusion | flops 1050214400 | bytes 9830400 | tf_op jit(solution)/shard_map/eij,ejk->eik/dot_general | solution.py:34
  59.1 2.4 collective-permute-start.6
  75.5 7.6 %fusion.14 = f32[16,1,320,1]{2,1,3,0:T(1,128)S(1)} fusion(bf16[16,4,320,320]{3,2,1,0:T(8,128)(2,1)} %param.141, bf16[16,4,320,1]{2,1,0,3:T(4,128)(2,1)S(1)} %select_bitcast_fusion.1), kind=kOutput, calls=%fused_computation.88 | convolution fusion | flops 13107200 | bytes 13168640 | tf_op jit(solution)/shard_map/efij,efj->ei/dot_general | solution.py:120
  83.8 4.9 %collective-permute-start.5 = (bf16[8,320]{1,0:T(8,128)(2,1)S(1)}, bf16[8,320]{1,0:T(8,128)(2,1)S(1)}, u32[]{:S(2)}, u32[]{:S(2)}) collective-permute-start(bf16[8,320]{1,0:T(8,128)(2,1)S(1)} %get-tuple-element.42), channel_id=1, source_target_pairs={{0,1},{1,2},{2,3},{3,4},{4,5},{5,6},{6,7},{7,8},{8,9},{9,10},{10,1... | collective-permute-start | bytes 15368 | tf_op jit(solution)/shard_map/ppermute | solution.py:18
  90.8 3.3 fusion.21
  94.1 16.4 %collective-permute-done.5 = bf16[8,320]{1,0:T(8,128)(2,1)S(1)} collective-permute-done((bf16[8,320]{1,0:T(8,128)(2,1)S(1)}, bf16[8,320]{1,0:T(8,128)(2,1)S(1)}, u32[]{:S(2)}, u32[]{:S(2)}) %collective-permute-start.5) | collective-permute-done | bytes 5152 | tf_op jit(solution)/shard_map/ppermute | solution.py:18
  112.8 16.6 %collective-permute-done.7 = bf16[8,320]{1,0:T(8,128)(2,1)S(1)} collective-permute-done((bf16[8,320]{1,0:T(8,128)(2,1)S(1)}, bf16[8,320]{1,0:T(8,128)(2,1)S(1)}, u32[]{:S(2)}, u32[]{:S(2)}) %collective-permute-start.7) | collective-permute-done | bytes 5152 | tf_op jit(solution)/shard_map/ppermute | solution.py:19
  129.4 2.2 fusion.11
  132.7 3.5 fusion.6
  136.2 3.6 %fusion.7 = bf16[8,320,320]{2,1,0:T(8,128)(2,1)S(1)} fusion(bf16[8,3,320,320]{3,2,0,1:T(8,128)(2,1)} %collective-permute-done.6), kind=kOutput, calls=%fused_computation.81 | convolution fusion | flops 525107200 | bytes 5570560 | tf_op jit(solution)/shard_map/eij,ejk->eik/dot_general | solution.py:34
  139.9 4.2 %pad_maximum_fusion.2 = bf16[32,320,320]{2,1,0:T(8,128)(2,1)} fusion(bf16[8,320,320]{2,1,0:T(8,128)(2,1)S(1)} %fusion.7, bf16[16,320,320]{2,1,0:T(8,128)(2,1)S(1)} %copy-done.3, bf16[8,320,320]{2,1,0:T(8,128)(2,1)S(1)} %fusion.6), kind=kLoop, calls=%fused_computation.65 | loop fusion | flops 6553600 | bytes 13107200 | tf_op jit(solution)/shard_map/concatenate | solution.py:101
  144.0 4.9 %gather_fusion.41 = bf16[4,320,320]{2,1,0:T(8,128)(2,1)} fusion(bf16[32,320,320]{2,1,0:T(8,128)(2,1)} %pad_maximum_fusion.2, s32[1024]{0:T(1024)S(1)} %get-tuple-element.52), kind=kCustom, calls=%fused_computation.41 | custom fusion | bytes 1638416 | tf_op jit(solution)/shard_map/gather | solution.py:150
  148.9 4.9 %gather_fusion.36 = bf16[4,320,320]{2,1,0:T(8,128)(2,1)} fusion(bf16[32,320,320]{2,1,0:T(8,128)(2,1)} %pad_maximum_fusion.2, s32[1024]{0:T(1024)S(1)} %get-tuple-element.53), kind=kCustom, calls=%fused_computation.36 | custom fusion | bytes 1638416 | tf_op jit(solution)/shard_map/gather | solution.py:150
  154.3 4.9 %gather_fusion.31 = bf16[4,320,320]{2,1,0:T(8,128)(2,1)} fusion(bf16[32,320,320]{2,1,0:T(8,128)(2,1)} %pad_maximum_fusion.2, s32[1024]{0:T(1024)S(1)} %get-tuple-element.54), kind=kCustom, calls=%fused_computation.31 | custom fusion | bytes 1638416 | tf_op jit(solution)/shard_map/gather | solution.py:150
  159.8 4.9 %gather_fusion.26 = bf16[4,320,320]{2,1,0:T(8,128)(2,1)} fusion(bf16[32,320,320]{2,1,0:T(8,128)(2,1)} %pad_maximum_fusion.2, s32[1024]{0:T(1024)S(1)} %get-tuple-element.55), kind=kCustom, calls=%fused_computation.26 | custom fusion | bytes 1638416 | tf_op jit(solution)/shard_map/gather | solution.py:150
  165.2 4.0 %gather_fusion.21 = bf16[4,320,320]{2,1,0:T(8,128)(2,1)S(1)} fusion(bf16[32,320,320]{2,1,0:T(8,128)(2,1)} %pad_maximum_fusion.2, s32[1024]{0:T(1024)S(1)} %get-tuple-element.56), kind=kCustom, calls=%fused_computation.21 | custom fusion | bytes 1638416 | tf_op jit(solution)/shard_map/gather | solution.py:150
  169.8 4.0 %gather_fusion.16 = bf16[4,320,320]{2,1,0:T(8,128)(2,1)S(1)} fusion(bf16[32,320,320]{2,1,0:T(8,128)(2,1)} %pad_maximum_fusion.2, s32[1024]{0:T(1024)S(1)} %get-tuple-element.57), kind=kCustom, calls=%fused_computation.16 | custom fusion | bytes 1638416 | tf_op jit(solution)/shard_map/gather | solution.py:150
  174.4 4.0 %gather_fusion.11 = bf16[4,320,320]{2,1,0:T(8,128)(2,1)S(1)} fusion(bf16[32,320,320]{2,1,0:T(8,128)(2,1)} %pad_maximum_fusion.2, s32[1024]{0:T(1024)S(1)} %pad_clamp_fusion.17), kind=kCustom, calls=%fused_computation.11 | custom fusion | bytes 1638416 | tf_op jit(solution)/shard_map/gather | solution.py:150
  178.9 4.9 %gather_fusion.46 = bf16[4,320,320]{2,1,0:T(8,128)(2,1)} fusion(bf16[32,320,320]{2,1,0:T(8,128)(2,1)} %pad_maximum_fusion.2, s32[1024]{0:T(1024)S(1)} %get-tuple-element.51), kind=kCustom, calls=%fused_computation.46 | custom fusion | bytes 1638416 | tf_op jit(solution)/shard_map/gather | solution.py:150
  183.8 3.5 fusion.4
  187.3 3.6 %fusion.5 = bf16[8,320,320]{2,1,0:T(8,128)(2,1)S(1)} fusion(bf16[8,3,320,320]{3,2,0,1:T(8,128)(2,1)} %collective-permute-done.6), kind=kOutput, calls=%fused_computation.79 | convolution fusion | flops 525107200 | bytes 5570560 | tf_op jit(solution)/shard_map/eij,ejk->eik/dot_general | solution.py:34
  191.0 4.1 %pad_maximum_fusion.1 = bf16[32,320,320]{2,1,0:T(8,128)(2,1)} fusion(bf16[8,320,320]{2,1,0:T(8,128)(2,1)S(1)} %fusion.5, bf16[16,320,320]{2,1,0:T(8,128)(2,1)S(1)} %copy-done.2, bf16[8,320,320]{2,1,0:T(8,128)(2,1)S(1)} %fusion.4), kind=kLoop, calls=%fused_computation.64 | loop fusion | flops 6553600 | bytes 13107200 | tf_op jit(solution)/shard_map/concatenate | solution.py:94
  195.1 4.9 %gather_fusion.45 = bf16[4,320,320]{2,1,0:T(8,128)(2,1)} fusion(bf16[32,320,320]{2,1,0:T(8,128)(2,1)} %pad_maximum_fusion.1, s32[1024]{0:T(1024)S(1)} %get-tuple-element.51), kind=kCustom, calls=%fused_computation.45 | custom fusion | bytes 1638416 | tf_op jit(solution)/shard_map/gather | solution.py:139
  199.9 4.9 %gather_fusion.40 = bf16[4,320,320]{2,1,0:T(8,128)(2,1)} fusion(bf16[32,320,320]{2,1,0:T(8,128)(2,1)} %pad_maximum_fusion.1, s32[1024]{0:T(1024)S(1)} %get-tuple-element.52), kind=kCustom, calls=%fused_computation.40 | custom fusion | bytes 1638416 | tf_op jit(solution)/shard_map/gather | solution.py:139
  204.8 4.9 %gather_fusion.35 = bf16[4,320,320]{2,1,0:T(8,128)(2,1)} fusion(bf16[32,320,320]{2,1,0:T(8,128)(2,1)} %pad_maximum_fusion.1, s32[1024]{0:T(1024)S(1)} %get-tuple-element.53), kind=kCustom, calls=%fused_computation.35 | custom fusion | bytes 1638416 | tf_op jit(solution)/shard_map/gather | solution.py:139
  209.7 4.9 %gather_fusion.30 = bf16[4,320,320]{2,1,0:T(8,128)(2,1)} fusion(bf16[32,320,320]{2,1,0:T(8,128)(2,1)} %pad_maximum_fusion.1, s32[1024]{0:T(1024)S(1)} %get-tuple-element.54), kind=kCustom, calls=%fused_computation.30 | custom fusion | bytes 1638416 | tf_op jit(solution)/shard_map/gather | solution.py:139
  214.6 4.9 %gather_fusion.25 = bf16[4,320,320]{2,1,0:T(8,128)(2,1)} fusion(bf16[32,320,320]{2,1,0:T(8,128)(2,1)} %pad_maximum_fusion.1, s32[1024]{0:T(1024)S(1)} %get-tuple-element.55), kind=kCustom, calls=%fused_computation.25 | custom fusion | bytes 1638416 | tf_op jit(solution)/shard_map/gather | solution.py:139
  219.5 4.9 %gather_fusion.20 = bf16[4,320,320]{2,1,0:T(8,128)(2,1)} fusion(bf16[32,320,320]{2,1,0:T(8,128)(2,1)} %pad_maximum_fusion.1, s32[1024]{0:T(1024)S(1)} %get-tuple-element.56), kind=kCustom, calls=%fused_computation.20 | custom fusion | bytes 1638416 | tf_op jit(solution)/shard_map/gather | solution.py:139
  224.4 4.9 %gather_fusion.15 = bf16[4,320,320]{2,1,0:T(8,128)(2,1)} fusion(bf16[32,320,320]{2,1,0:T(8,128)(2,1)} %pad_maximum_fusion.1, s32[1024]{0:T(1024)S(1)} %get-tuple-element.57), kind=kCustom, calls=%fused_computation.15 | custom fusion | bytes 1638416 | tf_op jit(solution)/shard_map/gather | solution.py:139
  229.3 4.9 %gather_fusion.10 = bf16[4,320,320]{2,1,0:T(8,128)(2,1)} fusion(bf16[32,320,320]{2,1,0:T(8,128)(2,1)} %pad_maximum_fusion.1, s32[1024]{0:T(1024)S(1)} %pad_clamp_fusion.17), kind=kCustom, calls=%fused_computation.10 | custom fusion | bytes 1638416 | tf_op jit(solution)/shard_map/gather | solution.py:139
  248.8 46.6 %collective-permute-start.9 = (bf16[8,320]{1,0:T(8,128)(2,1)S(1)}, bf16[8,320]{1,0:T(8,128)(2,1)S(1)}, u32[]{:S(2)}, u32[]{:S(2)}) collective-permute-start(bf16[8,320]{1,0:T(8,128)(2,1)S(1)} %get-tuple-element.38), channel_id=1, source_target_pairs={{1,0},{2,1},{3,2},{4,3},{5,4},{6,5},{7,6},{8,7},{9,8},{10,9},{11,1... | collective-permute-start | bytes 15368 | tf_op jit(solution)/shard_map/ppermute | solution.py:19
  300.6 4.3 %collective-permute-start.11 = (bf16[16,320]{1,0:T(8,128)(2,1)S(1)}, bf16[16,320]{1,0:T(8,128)(2,1)S(1)}, u32[]{:S(2)}, u32[]{:S(2)}) collective-permute-start(bf16[16,320]{1,0:T(8,128)(2,1)S(1)} %fusion.16), channel_id=1, source_target_pairs={{1,0},{2,1},{3,2},{4,3},{5,4},{6,5},{7,6},{8,7},{9,8},{10,9},{11,1... | collective-permute-start | bytes 30728 | tf_op jit(solution)/shard_map/ppermute | solution.py:19
  304.8 3.1 collective-permute-start.10
  309.6 7.6 %fusion.12 = f32[16,1,320,1]{2,1,3,0:T(1,128)S(1)} fusion(bf16[16,4,320,320]{3,2,1,0:T(8,128)(2,1)} %param.141, bf16[16,4,320,1]{2,1,0,3:T(4,128)(2,1)S(1)} %select_bitcast_fusion), kind=kOutput, calls=%fused_computation.86 | convolution fusion | flops 13107200 | bytes 13168640 | tf_op jit(solution)/shard_map/efij,efj->ei/dot_general | solution.py:120
  317.8 6.0 %collective-permute-start.12 = (bf16[8,320]{1,0:T(8,128)(2,1)S(1)}, bf16[8,320]{1,0:T(8,128)(2,1)S(1)}, u32[]{:S(2)}, u32[]{:S(2)}) collective-permute-start(bf16[8,320]{1,0:T(8,128)(2,1)S(1)} %get-tuple-element.40), channel_id=1, source_target_pairs={{0,1},{1,2},{2,3},{3,4},{4,5},{5,6},{6,7},{7,8},{8,9},{9,10},{10,1... | collective-permute-start | bytes 15368 | tf_op jit(solution)/shard_map/ppermute | solution.py:18
  326.0 3.3 fusion.19
  329.3 2.2 fusion.8
  331.5 2.2 fusion.10
  352.6 5.4 %collective-permute-start.14 = (f32[8,320]{1,0:T(8,128)S(1)}, f32[8,320]{1,0:T(8,128)S(1)}, u32[]{:S(2)}, u32[]{:S(2)}) collective-permute-start(f32[8,320]{1,0:T(8,128)S(1)} %get-tuple-element.37), channel_id=1, source_target_pairs={{0,1},{1,2},{2,3},{3,4},{4,5},{5,6},{6,7},{7,8},{8,9},{9,10},{10,1... | collective-permute-start | bytes 30728 | tf_op jit(solution)/shard_map/ppermute | solution.py:18
  (284 shorter events, 74.8 us)
Async XLA Ops:
  0.0 59.1 %collective-permute-start.1 = (s32[16]{0:T(128)}, s32[16]{0:T(128)S(1)}, u32[]{:S(2)}, u32[]{:S(2)}) collective-permute-start(s32[16]{0:T(128)} %param.143), channel_id=1, source_target_pairs={{1,0},{2,1},{3,2},{4,3},{5,4},{6,5},{7,6},{8,7},{9,8},{10,9},{11,1... | collective-permute-start | bytes 200 | tf_op jit(solution)/shard_map/ppermute | solution.py:19
  2.6 59.4 %collective-permute-start = (s32[16]{0:T(128)}, s32[16]{0:T(128)S(1)}, u32[]{:S(2)}, u32[]{:S(2)}) collective-permute-start(s32[16]{0:T(128)} %param.143), channel_id=1, source_target_pairs={{0,1},{1,2},{2,3},{3,4},{4,5},{5,6},{6,7},{7,8},{8,9},{9,10},{10,1... | collective-permute-start | bytes 200 | tf_op jit(solution)/shard_map/ppermute | solution.py:18
  8.1 66.5 %collective-permute-start.4 = (bf16[16,320]{1,0:T(8,128)(2,1)S(1)}, bf16[16,320]{1,0:T(8,128)(2,1)S(1)}, u32[]{:S(2)}, u32[]{:S(2)}) collective-permute-start(bf16[16,320]{1,0:T(8,128)(2,1)S(1)} %convert_element_type.118), channel_id=1, source_target_pairs={{1,0},{2,1},{3,2},{4,3},{5,4},{6,5},{7,6},{8,7},{9,8},{10,9},{11,1... | collective-permute-start | bytes 30728 | tf_op jit(solution)/shard_map/ppermute | solution.py:19
  10.0 64.6 %collective-permute-start.3 = (bf16[16,320]{1,0:T(8,128)(2,1)S(1)}, bf16[16,320]{1,0:T(8,128)(2,1)S(1)}, u32[]{:S(2)}, u32[]{:S(2)}) collective-permute-start(bf16[16,320]{1,0:T(8,128)(2,1)S(1)} %convert_element_type.118), channel_id=1, source_target_pairs={{0,1},{1,2},{2,3},{3,4},{4,5},{5,6},{6,7},{7,8},{8,9},{9,10},{10,1... | collective-permute-start | bytes 30728 | tf_op jit(solution)/shard_map/ppermute | solution.py:18
  44.6 66.0 %collective-permute-start.2 = (bf16[8,3,320,320]{3,2,0,1:T(8,128)(2,1)}, bf16[8,3,320,320]{3,2,0,1:T(8,128)(2,1)}, u32[]{:S(2)}, u32[]{:S(2)}) collective-permute-start(bf16[8,3,320,320]{3,2,0,1:T(8,128)(2,1)} %get-tuple-element.34), channel_id=1, source_target_pairs={{0,1},{1,2},{2,3},{3,4},{4,5},{5,6},{6,7},{7,8},{8,9},{9,10},{10,1... | collective-permute-start | bytes 14745608 | tf_op jit(solution)/shard_map/ppermute | solution.py:18
  46.6 7.9 %copy-start = (bf16[16,320,320]{2,1,0:T(8,128)(2,1)S(1)}, bf16[16,320,320]{2,1,0:T(8,128)(2,1)}, u32[]{:S(2)}) copy-start(bf16[16,320,320]{2,1,0:T(8,128)(2,1)} %param.138) | copy-start | bytes 9830404
  46.6 7.9 %copy-start.1 = (bf16[16,320,320]{2,1,0:T(8,128)(2,1)S(1)}, bf16[16,320,320]{2,1,0:T(8,128)(2,1)}, u32[]{:S(2)}) copy-start(bf16[16,320,320]{2,1,0:T(8,128)(2,1)} %param.140) | copy-start | bytes 9830404
  54.5 4.1 %copy-start.20 = (s32[4,16]{1,0:T(4,128)S(1)}, s32[4,16]{1,0:T(4,128)}, u32[]{:S(2)}) copy-start(s32[4,16]{1,0:T(4,128)} %param.142) | copy-start | bytes 772
  54.5 4.1 %copy-start.27 = (s32[4]{0:T(128)S(1)}, s32[4]{0:T(128)}, u32[]{:S(2)}) copy-start(s32[4]{0:T(128)} %constant.144) | copy-start | bytes 52
  54.5 4.1 %copy-start.26 = (s32[4]{0:T(128)S(1)}, s32[4]{0:T(128)}, u32[]{:S(2)}) copy-start(s32[4]{0:T(128)} %constant.146) | copy-start | bytes 52
  54.5 4.2 %copy-start.25 = (s32[4]{0:T(128)S(1)}, s32[4]{0:T(128)}, u32[]{:S(2)}) copy-start(s32[4]{0:T(128)} %constant.148) | copy-start | bytes 52
  54.5 4.2 %copy-start.24 = (s32[4]{0:T(128)S(1)}, s32[4]{0:T(128)}, u32[]{:S(2)}) copy-start(s32[4]{0:T(128)} %constant.150) | copy-start | bytes 52
  54.5 4.2 %copy-start.23 = (s32[4]{0:T(128)S(1)}, s32[4]{0:T(128)}, u32[]{:S(2)}) copy-start(s32[4]{0:T(128)} %constant.152) | copy-start | bytes 52
  54.5 4.2 %copy-start.22 = (s32[4]{0:T(128)S(1)}, s32[4]{0:T(128)}, u32[]{:S(2)}) copy-start(s32[4]{0:T(128)} %constant.154) | copy-start | bytes 52
  54.6 4.2 %copy-start.21 = (s32[4]{0:T(128)S(1)}, s32[4]{0:T(128)}, u32[]{:S(2)}) copy-start(s32[4]{0:T(128)} %constant.156) | copy-start | bytes 52
  59.1 70.3 %collective-permute-start.6 = (bf16[8,3,320,320]{3,2,0,1:T(8,128)(2,1)}, bf16[8,3,320,320]{3,2,0,1:T(8,128)(2,1)}, u32[]{:S(2)}, u32[]{:S(2)}) collective-permute-start(bf16[8,3,320,320]{3,2,0,1:T(8,128)(2,1)} %get-tuple-element.35), channel_id=1, source_target_pairs={{1,0},{2,1},{3,2},{4,3},{5,4},{6,5},{7,6},{8,7},{9,8},{10,9},{11,1... | collective-permute-start | bytes 14745608 | tf_op jit(solution)/shard_map/ppermute | solution.py:19
  75.5 7.6 %copy-start.19 = (f32[16,320]{1,0:T(8,128)S(1)}, f32[16,320]{1,0:T(8,128)}, u32[]{:S(2)}) copy-start(f32[16,320]{1,0:T(8,128)} %param.136) | copy-start | bytes 61444
  83.8 26.8 %collective-permute-start.5 = (bf16[8,320]{1,0:T(8,128)(2,1)S(1)}, bf16[8,320]{1,0:T(8,128)(2,1)S(1)}, u32[]{:S(2)}, u32[]{:S(2)}) collective-permute-start(bf16[8,320]{1,0:T(8,128)(2,1)S(1)} %get-tuple-element.42), channel_id=1, source_target_pairs={{0,1},{1,2},{2,3},{3,4},{4,5},{5,6},{6,7},{7,8},{8,9},{9,10},{10,1... | collective-permute-start | bytes 15368 | tf_op jit(solution)/shard_map/ppermute | solution.py:18
  88.7 40.6 %collective-permute-start.7 = (bf16[8,320]{1,0:T(8,128)(2,1)S(1)}, bf16[8,320]{1,0:T(8,128)(2,1)S(1)}, u32[]{:S(2)}, u32[]{:S(2)}) collective-permute-start(bf16[8,320]{1,0:T(8,128)(2,1)S(1)} %get-tuple-element.43), channel_id=1, source_target_pairs={{1,0},{2,1},{3,2},{4,3},{5,4},{6,5},{7,6},{8,7},{9,8},{10,9},{11,1... | collective-permute-start | bytes 15368 | tf_op jit(solution)/shard_map/ppermute | solution.py:19
  136.2 3.7 %copy-start.3 = (bf16[16,320,320]{2,1,0:T(8,128)(2,1)S(1)}, bf16[16,320,320]{2,1,0:T(8,128)(2,1)}, u32[]{:S(2)}) copy-start(bf16[16,320,320]{2,1,0:T(8,128)(2,1)} %convolution_convert_fusion) | copy-start | bytes 9830404
  187.3 3.7 %copy-start.2 = (bf16[16,320,320]{2,1,0:T(8,128)(2,1)S(1)}, bf16[16,320,320]{2,1,0:T(8,128)(2,1)}, u32[]{:S(2)}) copy-start(bf16[16,320,320]{2,1,0:T(8,128)(2,1)} %convolution_convert_fusion.1) | copy-start | bytes 9830404
  234.2 8.7 %copy-start.18 = (bf16[4,320,320]{2,1,0:T(8,128)(2,1)S(1)}, bf16[4,320,320]{2,1,0:T(8,128)(2,1)}, u32[]{:S(2)}) copy-start(bf16[4,320,320]{2,1,0:T(8,128)(2,1)} %gather_fusion.30) | copy-start | bytes 2457604
  234.2 9.2 %copy-start.16 = (bf16[4,320,320]{2,1,0:T(8,128)(2,1)S(1)}, bf16[4,320,320]{2,1,0:T(8,128)(2,1)}, u32[]{:S(2)}) copy-start(bf16[4,320,320]{2,1,0:T(8,128)(2,1)} %gather_fusion.35) | copy-start | bytes 2457604
  234.2 9.7 %copy-start.14 = (bf16[4,320,320]{2,1,0:T(8,128)(2,1)S(1)}, bf16[4,320,320]{2,1,0:T(8,128)(2,1)}, u32[]{:S(2)}) copy-start(bf16[4,320,320]{2,1,0:T(8,128)(2,1)} %gather_fusion.40) | copy-start | bytes 2457604
  234.2 10.1 %copy-start.12 = (bf16[4,320,320]{2,1,0:T(8,128)(2,1)S(1)}, bf16[4,320,320]{2,1,0:T(8,128)(2,1)}, u32[]{:S(2)}) copy-start(bf16[4,320,320]{2,1,0:T(8,128)(2,1)} %gather_fusion.45) | copy-start | bytes 2457604
  235.9 8.9 %copy-start.10 = (bf16[4,320,320]{2,1,0:T(8,128)(2,1)S(1)}, bf16[4,320,320]{2,1,0:T(8,128)(2,1)}, u32[]{:S(2)}) copy-start(bf16[4,320,320]{2,1,0:T(8,128)(2,1)} %gather_fusion.41) | copy-start | bytes 2457604
  237.7 7.6 %copy-start.8 = (bf16[4,320,320]{2,1,0:T(8,128)(2,1)S(1)}, bf16[4,320,320]{2,1,0:T(8,128)(2,1)}, u32[]{:S(2)}) copy-start(bf16[4,320,320]{2,1,0:T(8,128)(2,1)} %gather_fusion.36) | copy-start | bytes 2457604
  239.4 6.3 %copy-start.6 = (bf16[4,320,320]{2,1,0:T(8,128)(2,1)S(1)}, bf16[4,320,320]{2,1,0:T(8,128)(2,1)}, u32[]{:S(2)}) copy-start(bf16[4,320,320]{2,1,0:T(8,128)(2,1)} %gather_fusion.31) | copy-start | bytes 2457604
  241.2 5.0 %copy-start.4 = (bf16[4,320,320]{2,1,0:T(8,128)(2,1)S(1)}, bf16[4,320,320]{2,1,0:T(8,128)(2,1)}, u32[]{:S(2)}) copy-start(bf16[4,320,320]{2,1,0:T(8,128)(2,1)} %gather_fusion.26) | copy-start | bytes 2457604
  248.8 48.6 %collective-permute-start.9 = (bf16[8,320]{1,0:T(8,128)(2,1)S(1)}, bf16[8,320]{1,0:T(8,128)(2,1)S(1)}, u32[]{:S(2)}, u32[]{:S(2)}) collective-permute-start(bf16[8,320]{1,0:T(8,128)(2,1)S(1)} %get-tuple-element.38), channel_id=1, source_target_pairs={{1,0},{2,1},{3,2},{4,3},{5,4},{6,5},{7,6},{8,7},{9,8},{10,9},{11,1... | collective-permute-start | bytes 15368 | tf_op jit(solution)/shard_map/ppermute | solution.py:19
  295.4 4.5 %collective-permute-start.8 = (bf16[8,320]{1,0:T(8,128)(2,1)S(1)}, bf16[8,320]{1,0:T(8,128)(2,1)S(1)}, u32[]{:S(2)}, u32[]{:S(2)}) collective-permute-start(bf16[8,320]{1,0:T(8,128)(2,1)S(1)} %get-tuple-element.39), channel_id=1, source_target_pairs={{0,1},{1,2},{2,3},{3,4},{4,5},{5,6},{6,7},{7,8},{8,9},{9,10},{10,1... | collective-permute-start | bytes 15368 | tf_op jit(solution)/shard_map/ppermute | solution.py:18
  300.6 7.4 %collective-permute-start.11 = (bf16[16,320]{1,0:T(8,128)(2,1)S(1)}, bf16[16,320]{1,0:T(8,128)(2,1)S(1)}, u32[]{:S(2)}, u32[]{:S(2)}) collective-permute-start(bf16[16,320]{1,0:T(8,128)(2,1)S(1)} %fusion.16), channel_id=1, source_target_pairs={{1,0},{2,1},{3,2},{4,3},{5,4},{6,5},{7,6},{8,7},{9,8},{10,9},{11,1... | collective-permute-start | bytes 30728 | tf_op jit(solution)/shard_map/ppermute | solution.py:19
  304.8 3.9 %collective-permute-start.10 = (bf16[16,320]{1,0:T(8,128)(2,1)S(1)}, bf16[16,320]{1,0:T(8,128)(2,1)S(1)}, u32[]{:S(2)}, u32[]{:S(2)}) collective-permute-start(bf16[16,320]{1,0:T(8,128)(2,1)S(1)} %fusion.16), channel_id=1, source_target_pairs={{0,1},{1,2},{2,3},{3,4},{4,5},{5,6},{6,7},{7,8},{8,9},{9,10},{10,1... | collective-permute-start | bytes 30728 | tf_op jit(solution)/shard_map/ppermute | solution.py:18
  317.8 11.5 %collective-permute-start.12 = (bf16[8,320]{1,0:T(8,128)(2,1)S(1)}, bf16[8,320]{1,0:T(8,128)(2,1)S(1)}, u32[]{:S(2)}, u32[]{:S(2)}) collective-permute-start(bf16[8,320]{1,0:T(8,128)(2,1)S(1)} %get-tuple-element.40), channel_id=1, source_target_pairs={{0,1},{1,2},{2,3},{3,4},{4,5},{5,6},{6,7},{7,8},{8,9},{9,10},{10,1... | collective-permute-start | bytes 15368 | tf_op jit(solution)/shard_map/ppermute | solution.py:18
  323.8 7.7 %collective-permute-start.13 = (bf16[8,320]{1,0:T(8,128)(2,1)S(1)}, bf16[8,320]{1,0:T(8,128)(2,1)S(1)}, u32[]{:S(2)}, u32[]{:S(2)}) collective-permute-start(bf16[8,320]{1,0:T(8,128)(2,1)S(1)} %get-tuple-element.41), channel_id=1, source_target_pairs={{1,0},{2,1},{3,2},{4,3},{5,4},{6,5},{7,6},{8,7},{9,8},{10,9},{11,1... | collective-permute-start | bytes 15368 | tf_op jit(solution)/shard_map/ppermute | solution.py:19
  338.2 7.1 %copy-start.17 = (bf16[4,320,320]{2,1,0:T(8,128)(2,1)S(1)}, bf16[4,320,320]{2,1,0:T(8,128)(2,1)}, u32[]{:S(2)}) copy-start(bf16[4,320,320]{2,1,0:T(8,128)(2,1)} %gather_fusion.35) | copy-start | bytes 2457604
  338.2 7.5 %copy-start.15 = (bf16[4,320,320]{2,1,0:T(8,128)(2,1)S(1)}, bf16[4,320,320]{2,1,0:T(8,128)(2,1)}, u32[]{:S(2)}) copy-start(bf16[4,320,320]{2,1,0:T(8,128)(2,1)} %gather_fusion.40) | copy-start | bytes 2457604
  338.2 8.0 %copy-start.13 = (bf16[4,320,320]{2,1,0:T(8,128)(2,1)S(1)}, bf16[4,320,320]{2,1,0:T(8,128)(2,1)}, u32[]{:S(2)}) copy-start(bf16[4,320,320]{2,1,0:T(8,128)(2,1)} %gather_fusion.45) | copy-start | bytes 2457604
  338.3 8.4 %copy-start.11 = (bf16[4,320,320]{2,1,0:T(8,128)(2,1)S(1)}, bf16[4,320,320]{2,1,0:T(8,128)(2,1)}, u32[]{:S(2)}) copy-start(bf16[4,320,320]{2,1,0:T(8,128)(2,1)} %gather_fusion.41) | copy-start | bytes 2457604
  338.3 8.8 %copy-start.9 = (bf16[4,320,320]{2,1,0:T(8,128)(2,1)S(1)}, bf16[4,320,320]{2,1,0:T(8,128)(2,1)}, u32[]{:S(2)}) copy-start(bf16[4,320,320]{2,1,0:T(8,128)(2,1)} %gather_fusion.36) | copy-start | bytes 2457604
  340.1 7.5 %copy-start.7 = (bf16[4,320,320]{2,1,0:T(8,128)(2,1)S(1)}, bf16[4,320,320]{2,1,0:T(8,128)(2,1)}, u32[]{:S(2)}) copy-start(bf16[4,320,320]{2,1,0:T(8,128)(2,1)} %gather_fusion.31) | copy-start | bytes 2457604
  341.9 6.2 %copy-start.5 = (bf16[4,320,320]{2,1,0:T(8,128)(2,1)S(1)}, bf16[4,320,320]{2,1,0:T(8,128)(2,1)}, u32[]{:S(2)}) copy-start(bf16[4,320,320]{2,1,0:T(8,128)(2,1)} %gather_fusion.26) | copy-start | bytes 2457604
  350.6 7.4 %collective-permute-start.15 = (f32[8,320]{1,0:T(8,128)S(1)}, f32[8,320]{1,0:T(8,128)S(1)}, u32[]{:S(2)}, u32[]{:S(2)}) collective-permute-start(f32[8,320]{1,0:T(8,128)S(1)} %get-tuple-element.36), channel_id=1, source_target_pairs={{1,0},{2,1},{3,2},{4,3},{5,4},{6,5},{7,6},{8,7},{9,8},{10,9},{11,1... | collective-permute-start | bytes 30728 | tf_op jit(solution)/shard_map/ppermute | solution.py:19
  352.6 6.3 %collective-permute-start.14 = (f32[8,320]{1,0:T(8,128)S(1)}, f32[8,320]{1,0:T(8,128)S(1)}, u32[]{:S(2)}, u32[]{:S(2)}) collective-permute-start(f32[8,320]{1,0:T(8,128)S(1)} %get-tuple-element.37), channel_id=1, source_target_pairs={{0,1},{1,2},{2,3},{3,4},{4,5},{5,6},{6,7},{7,8},{8,9},{9,10},{10,1... | collective-permute-start | bytes 30728 | tf_op jit(solution)/shard_map/ppermute | solution.py:18
where the time goes:
time: 364 us; the launch traced here: 360 us
  local copies, waits for them, and re-layouts  123 us (34%)
  starting transfers between devices  97.5 us (27%)
  matrix products  79.9 us (22%)
  waiting for transfers between devices  36 us (10%)
  other arithmetic  22.4 us (6%)
    ppermute x8, starting transfers between devices, with_halo(): after = lax.ppermute(initial, axis, down)  64 us
    gather x8, local copies, waits for them, and re-layouts, body(): item_lower[items_here]  39.1 us
    gather x8, local copies, waits for them, and re-layouts, body(): item_upper[items_here]  36.4 us
    ppermute x8, starting transfers between devices, with_halo(): before = lax.ppermute(last, axis, up)  33.5 us
    dot_general x6, matrix products, premultiply(): jnp.einsum('eij,ejk->eik', first_block, second_block, preferred_element_t...  26.2 us
    ppermute x8, waiting for transfers between devices, with_halo(): before = lax.ppermute(last, axis, up)  19.4 us
    ppermute x8, waiting for transfers between devices, with_halo(): after = lax.ppermute(initial, axis, down)  16.6 us
    dot_general x15, matrix products, body(): jnp.einsum('rij,rj->ri', item_lower[items_here], previous, preferred_elem...  16 us
  transfers between devices with their start and end apart: 16, of which 5 were waited for; matrix products, arithmetic and copies ran while one was open for 21% of the time, Pallas kernels for 0%

commit v1 on v0

v1 whole, which is shorter than its diff:
```python
import functools

import jax
import jax.numpy as jnp
from jax import lax
from jax.experimental import pallas as pl
from jax.experimental.pallas import tpu as pltpu
from jax.sharding import PartitionSpec as P

LMAX = 8
SWEEPS = 2
WIDE = 256
ANY = pl.BlockSpec(memory_space=pl.ANY)
SMEM = pl.BlockSpec(memory_space=pltpu.SMEM)
VMEM = pl.BlockSpec(memory_space=pltpu.VMEM)
NT = (((1,), (1,)), ((), ()))


def dot_nt(a, b):
    return lax.dot_general(a, b, NT, preferred_element_type=jnp.float32)


def dot_nn(a, b):
    return jnp.dot(a, b, preferred_element_type=jnp.float32)


def pair_product(pivot, lower, upper, out):
    out[:, :WIDE] = dot_nn(pivot, lower[:, :WIDE]).astype(jnp.bfloat16)
    out[:, WIDE : 2 * WIDE] = dot_nn(pivot, upper[:, :WIDE]).astype(jnp.bfloat16)
    tails = jnp.concatenate([lower[:, WIDE:], upper[:, WIDE:]], axis=1)
    out[:, 2 * WIDE :] = dot_nn(pivot, tails).astype(jnp.bfloat16)


def outgoing_kernel(chunk, slot_count, slots, target, piv, low, upp, first, second, pb, lb, ub, stage, insem, outsem):
    bucket = stage.shape[0]
    count = jnp.int32(0)
    for e in range(slots.shape[0]):
        hit = (slots[e] // slot_count) == target[0]

        @pl.when(hit)
        def _(e=e, count=count):
            pltpu.make_async_copy(piv.at[e], pb.at[count], insem.at[0, count]).start()
            pltpu.make_async_copy(low.at[e], lb.at[count], insem.at[1, count]).start()
            pltpu.make_async_copy(upp.at[e], ub.at[count], insem.at[2, count]).start()

        count = count + hit.astype(jnp.int32)

    def sent(k):
        dest = first.at[k] if k < chunk else second.at[k - chunk]
        return pltpu.make_async_copy(stage.at[k], dest, outsem.at[k])

    for k in range(bucket):

        @pl.when(k < count)
        def _(k=k):
            pltpu.make_async_copy(piv.at[0], pb.at[k], insem.at[0, k]).wait()
            pltpu.make_async_copy(low.at[0], lb.at[k], insem.at[1, k]).wait()
            pltpu.make_async_copy(upp.at[0], ub.at[k], insem.at[2, k]).wait()
            pair_product(pb[k], lb[k], ub[k], stage.at[k])
            sent(k).start()

    for k in range(bucket):

        @pl.when(k < count)
        def _(k=k):
            sent(k).wait()


def staying_kernel(slot_count, slots, me, target, piv, low, upp, beside, own, pb, lb, ub, stage, insem, outsem):
    elems = slots.shape[0]

    def loads(e):
        return [
            pltpu.make_async_copy(src.at[e], dst.at[e], insem.at[i, e])
            for i, (src, dst) in enumerate(((piv, pb), (low, lb), (upp, ub)))
        ]

    for e in range(elems):
        owner = slots[e] // slot_count

        @pl.when((owner == me[0]) | (owner == target[0]))
        def _(e=e):
            for copy in loads(e):
                copy.start()

    def step(e, count):
        owner = slots[e] // slot_count
        across = owner == target[0]

        @pl.when((owner == me[0]) | across)
        def _():
            for copy in loads(e):
                copy.wait()
            pair_product(pb[e], lb[e], ub[e], stage.at[e])

        @pl.when(across)
        def _():
            pltpu.make_async_copy(stage.at[e], beside.at[count], outsem.at[e]).start()

        @pl.when(owner == me[0])
        def _():
            pltpu.make_async_copy(stage.at[e], own.at[e], outsem.at[e]).start()

        return count + across.astype(jnp.int32)

    lax.fori_loop(0, elems, step, jnp.int32(0))
    for e in range(elems):
        owner = slots[e] // slot_count

        @pl.when((owner == me[0]) | (owner == target[0]))
        def _(e=e):
            pltpu.make_async_copy(stage.at[e], own.at[e], outsem.at[e]).wait()


def face_kernel(counts, send_ref, index_ref, rhs_ref, *refs):
    parts = refs[: len(counts)]
    faces_ref, piv_ref, side_ref, across_ref, own_ref, rows, gathered, scaled = refs[len(counts) :]
    e = pl.program_id(0)
    elems = rhs_ref.shape[0]
    faces = faces_ref.shape[1]
    width = rhs_ref.shape[1]

    @pl.when(e == 0)
    def _():
        at = 0
        for part, size in zip(parts, counts):
            rows[at : at + size] = part[...]
            at += size
        wanted = index_ref[...] == lax.broadcasted_iota(jnp.int32, (faces * elems, at), 1)
        picked = dot_nn(wanted.astype(jnp.bfloat16), rows[...])
        gathered[...] = picked.astype(jnp.bfloat16)

    total = dot_nt(gathered[:elems], faces_ref[0, 0])
    for f in range(1, faces):
        total += dot_nt(gathered[f * elems : (f + 1) * elems], faces_ref[0, f])
    residual = (rhs_ref[...] - total).astype(jnp.bfloat16)
    applied = dot_nt(residual, piv_ref[0])
    row = lax.broadcasted_iota(jnp.int32, (elems, width), 0)
    scaled[...] = jnp.where(row == e, applied, scaled[...])

    @pl.when(e == elems - 1)
    def _():
        own_ref[...] = scaled[...]
        bucket = side_ref.shape[0]
        for k in range(bucket):
            side_ref[k : k + 1] = scaled[pl.ds(send_ref[k], 1), :]
            across_ref[k : k + 1] = scaled[pl.ds(send_ref[bucket + k], 1), :]


def solve_kernel(last, chunk, table, back, side_m, own_m, first_m, second_m, side_s, own_s, across_s, *refs):
    outs = refs[:3] if last else refs[:1]
    mats, items, ahead, behind, sems = refs[len(outs) :]
    bucket = side_s.shape[0]
    elems = own_s.shape[0]
    width = own_s.shape[1]
    lines = table.shape[0] // LMAX
    tail = width - WIDE

    def load(p, r):
        slot = r * LMAX + p
        at = p * lines + r
        item = table[slot]
        sources = (
            (side_m, 0, bucket),
            (own_m, bucket, bucket + elems),
            (first_m, bucket + elems, bucket + elems + chunk),
            (second_m, bucket + elems + chunk, 2 * bucket + elems),
        )
        for source, low, high in sources:

            @pl.when((item >= low) & (item < high))
            def _(source=source, low=low):
                pltpu.make_async_copy(source.at[item - low], mats.at[at], sems.at[at]).start()

    for p in range(LMAX):
        for r in range(lines):
            load(p, r)

    items[:bucket] = side_s[...]
    items[bucket : bucket + elems] = own_s[...]
    items[bucket + elems :] = across_s[...]
    sublanes = ahead.shape[1]
    row = lax.broadcasted_iota(jnp.int32, (sublanes, width), 0)
    zeros = jnp.zeros((sublanes, tail), jnp.bfloat16)

    def sweep_step(p, x, half):
        lead = x[:, :WIDE]
        ends = [x[:, WIDE:], zeros] if half == 0 else [zeros, x[:, WIDE:]]
        ending = jnp.concatenate(ends, axis=1)
        carried = jnp.zeros((sublanes, width), jnp.float32)
        for r in range(lines):
            at = p * lines + r
            got = dot_nt(lead, mats[at, :, half * WIDE : (half + 1) * WIDE])
            got += dot_nt(ending, mats[at, :, 2 * WIDE :])
            live = table[r * LMAX + p] >= 0
            carried = jnp.where((row == r) & live, got, carried)
        return carried

    for p in range(LMAX):
        ahead[p] = jnp.zeros((sublanes, width), jnp.float32)
        for r in range(lines):
            item = table[r * LMAX + p]

            @pl.when(item >= 0)
            def _(p=p, r=r, item=item):
                ahead[p, r : r + 1, :] = items[pl.ds(item, 1), :]

    x = None
    for p in range(LMAX):
        for r in range(lines):

            @pl.when(table[r * LMAX + p] >= 0)
            def _(p=p, r=r):
                at = p * lines + r
                pltpu.make_async_copy(own_m.at[0], mats.at[at], sems.at[at]).wait()

        value = ahead[p]
        if p > 0:
            value = value - sweep_step(p, x, 0)
            ahead[p] = value
        x = value.astype(jnp.bfloat16)
    x = None
    for p in reversed(range(LMAX)):
        value = ahead[p]
        if p < LMAX - 1:
            value = value - sweep_step(p, x, 1)
        behind[p] = value
        x = value.astype(jnp.bfloat16)
    if last:
        at = 0
        for out in outs:
            for k in range(out.shape[0]):
                slot = back[at + k]
                out[k : k + 1] = behind[slot % LMAX, pl.ds(slot // LMAX, 1), :]
            at += out.shape[0]
    else:
        (out,) = outs
        for p in range(LMAX):
            items[p * lines : (p + 1) * lines] = behind[p, :lines, :]
        out[...] = items[...].astype(jnp.bfloat16)


def place_kernel(index, side, own, across, out, items):
    bucket = side.shape[0]
    elems = own.shape[0]
    items[:bucket] = side[...]
    items[bucket : bucket + elems] = own[...]
    items[bucket + elems :] = across[...]
    for e in range(elems):
        out[e : e + 1] = items[pl.ds(index[e], 1), :]


def pack_order(selected, bucket):
    members = jnp.arange(selected.shape[0], dtype=jnp.int32)
    before = (members[None, :] <= members[:, None]) & selected[None, :]
    ordering = jnp.sum(before.astype(jnp.int32), axis=1) - 1
    positions = jnp.arange(bucket, dtype=jnp.int32)[:, None]
    matches = selected[None, :] & (ordering[None, :] == positions)
    picked = jnp.sum(jnp.where(matches, members[None, :], 0), axis=1)
    return (picked, jnp.any(matches, axis=1), jnp.clip(ordering, 0, bucket - 1))


def body(
    chunk,
    right_side,
    start_state,
    pivot_inverse,
    lower_block,
    upper_block,
    face_blocks,
    neighbours,
    element_slot,
):
    elems, width = right_side.shape
    faces = face_blocks.shape[1]
    bucket = elems // 2
    slot_count = 2 * elems
    lines = slot_count // LMAX
    packed = 2 * width
    devices = lax.axis_size("dom")
    me = lax.axis_index("dom").astype(jnp.int32)
    odd = me % 2 == 1
    side = jnp.where(odd, me - 1, me + 1)
    across = jnp.where(odd, me + 1, me - 1)
    side_pairs = [(i, i ^ 1) for i in range(devices)]
    across_pairs = [(i, i + 1) for i in range(1, devices - 1, 2)]
    across_pairs = across_pairs + [(j, i) for i, j in across_pairs]

    def to_side(array):
        return lax.ppermute(array, "dom", side_pairs)

    def to_across(array):
        return lax.ppermute(array, "dom", across_pairs)

    f32, bf16 = jnp.float32, jnp.bfloat16
    block = (width, width)
    pair = (width, packed)
    dma = pltpu.SemaphoreType.DMA

    first, second = pl.pallas_call(
        functools.partial(outgoing_kernel, chunk, slot_count),
        out_shape=[
            jax.ShapeDtypeStruct((chunk,) + pair, bf16),
            jax.ShapeDtypeStruct((bucket - chunk,) + pair, bf16),
        ],
        in_specs=[SMEM, SMEM, ANY, ANY, ANY],
        out_specs=[ANY, ANY],
        scratch_shapes=[pltpu.VMEM((bucket,) + block, bf16)] * 3
        + [pltpu.VMEM((bucket,) + pair, bf16), dma((3, bucket)), dma((bucket,))],
        compiler_params=pltpu.CompilerParams(vmem_limit_bytes=40 << 20),
        name="outgoing",
    )(element_slot, across[None], pivot_inverse, lower_block, upper_block)
    first_in = to_across(first)
    rounded = start_state.astype(bf16)
    state_across = to_across(rounded)
    slot_across = to_across(element_slot)
    second_in = to_across(second)
    state_side = to_side(rounded)
    slot_side = to_side(element_slot)

    side_pack, own_pack = pl.pallas_call(
        functools.partial(staying_kernel, slot_count),
        out_shape=[
            jax.ShapeDtypeStruct((bucket,) + pair, bf16),
            jax.ShapeDtypeStruct((elems,) + pair, bf16),
        ],
        in_specs=[SMEM, SMEM, SMEM, ANY, ANY, ANY],
        out_specs=[ANY, ANY],
        scratch_shapes=[pltpu.VMEM((elems,) + block, bf16)] * 3
        + [pltpu.VMEM((elems,) + pair, bf16), dma((3, elems)), dma((elems,))],
        compiler_params=pltpu.CompilerParams(vmem_limit_bytes=40 << 20),
        name="staying",
    )(element_slot, me[None], side[None], pivot_inverse, lower_block, upper_block)
    side_in = to_side(side_pack)

    owner = element_slot // slot_count
    side_index, _, side_rank = pack_order(owner == side, bucket)
    across_index, _, across_rank = pack_order(owner == across, bucket)
    send_index = jnp.concatenate([side_index, across_index])
    spread = jnp.arange(elems, dtype=jnp.int32)
    item_of_own = jnp.where(
        owner == me,
        bucket + spread,
        jnp.where(owner == side, side_rank, bucket + elems + across_rank),
    )
    across_live = (across >= 0) & (across < devices)
    in_side, in_side_valid, _ = pack_order(slot_side // slot_count == me, bucket)
    in_across, in_across_valid, _ = pack_order((slot_across // slot_count == me) & across_live, bucket)
    item_slot = jnp.concatenate(
        [
            jnp.where(in_side_valid, slot_side[in_side] % slot_count, -1),
            jnp.where(owner == me, element_slot % slot_count, -1),
            jnp.where(in_across_valid, slot_across[in_across] % slot_count, -1),
        ]
    )
    everything = jnp.arange(slot_count, dtype=jnp.int32)
    slot_matches = item_slot[None, :] == everything[:, None]
    table = jnp.max(jnp.where(slot_matches, everything[None, :], -1), axis=1)
    back = jnp.maximum(item_slot, 0)

    home = neighbours // elems
    within = neighbours % elems
    near = jnp.where(home == me, elems, jnp.where(home == side, 0, 2 * elems)) + within
    near = jnp.where(neighbours >= 0, near, -1)
    all_slots = jnp.concatenate([slot_side, element_slot, slot_across])
    place = all_slots[jnp.maximum(near, 0)]
    place_owner = place // slot_count
    place_slot = place % slot_count
    place_row = (place_slot % LMAX) * lines + place_slot // LMAX
    across_chip = across // 2
    far = jnp.where(
        place_owner == me,
        0,
        jnp.where(
            place_owner == side,
            slot_count,
            jnp.where(place_owner // 2 == across_chip, 2 * slot_count, 4 * slot_count)
            + (place_owner % 2) * slot_count,
        ),
    )
    far = jnp.where(neighbours >= 0, far + place_row, -1)

    def face_part(index, parts):
        counts = tuple(part.shape[0] for part in parts)
        whole = lambda *shape: pl.BlockSpec(shape, lambda e: (0,) * len(shape))
        return pl.pallas_call(
            functools.partial(face_kernel, counts),
            grid=(elems,),
            out_shape=[
                jax.ShapeDtypeStruct((bucket, width), f32),
                jax.ShapeDtypeStruct((bucket, width), f32),
                jax.ShapeDtypeStruct((elems, width), f32),
            ],
            in_specs=[SMEM, whole(faces * elems, 1), whole(elems, width)]
            + [whole(count, width) for count in counts]
            + [
                pl.BlockSpec((1, faces, width, width), lambda e: (e, 0, 0, 0)),
                pl.BlockSpec((1, width, width), lambda e: (e, 0, 0)),
            ],
            out_specs=[whole(bucket, width), whole(bucket, width), whole(elems, width)],
            scratch_shapes=[
                pltpu.VMEM((sum(counts), width), bf16),
                pltpu.VMEM((faces * elems, width), bf16),
                pltpu.VMEM((elems, width), f32),
            ],
            compiler_params=pltpu.CompilerParams(vmem_limit_bytes=40 << 20),
            name="faces",
        )(send_index, index.reshape(-1, 1), right_side, *parts, face_blocks, pivot_inverse)

    def solve(last, side_s, own_s, across_s):
        if last:
            shapes = [(bucket, width), (elems, width), (bucket, width)]
            out_shape = [jax.ShapeDtypeStruct(shape, f32) for shape in shapes]
        else:
            out_shape = [jax.ShapeDtypeStruct((slot_count, width), bf16)]
        return pl.pallas_call(
            functools.partial(solve_kernel, last, chunk),
            out_shape=out_shape,
            in_specs=[SMEM, SMEM, ANY, ANY, ANY, ANY, VMEM, VMEM, VMEM],
            out_specs=[VMEM] * len(out_shape),
            scratch_shapes=[
                pltpu.VMEM((slot_count,) + pair, bf16),
                pltpu.VMEM((slot_count, width), f32),
                pltpu.VMEM((LMAX, 8, width), f32),
                pltpu.VMEM((LMAX, 8, width), f32),
                dma((slot_count,)),
            ],
            compiler_params=pltpu.CompilerParams(vmem_limit_bytes=40 << 20),
            name="solve",
        )(table, back, side_in, own_pack, first_in, second_in, side_s, own_s, across_s)

    index, parts = near, [state_side, rounded, state_across]
    for sweep in range(SWEEPS):
        scaled_side, scaled_across, scaled_own = face_part(index, parts)
        got_across = to_across(scaled_across)
        got_side = to_side(scaled_side)
        solved = solve(sweep == SWEEPS - 1, got_side, scaled_own, got_across)
        if sweep < SWEEPS - 1:
            (mine,) = solved
            beside = to_side(mine)
            chip = jnp.where(
                odd, jnp.concatenate([beside, mine]), jnp.concatenate([mine, beside])
            )
            over = to_across(chip)
            under = to_side(over)
            index, parts = far, [mine, beside, over, under]
    back_side, back_own, back_across = solved
    back_across = to_across(back_across)
    back_side = to_side(back_side)
    return pl.pallas_call(
        place_kernel,
        out_shape=jax.ShapeDtypeStruct((elems, width), f32),
        in_specs=[SMEM, VMEM, VMEM, VMEM],
        out_specs=VMEM,
        scratch_shapes=[pltpu.VMEM((slot_count, width), f32)],
        name="place",
    )(item_of_own, back_side, back_own, back_across)


def solution(mesh):
    placed = (
        P("dom", None),
        P("dom", None),
        P("dom", None, None),
        P("dom", None, None),
        P("dom", None, None),
        P("dom", None, None, None),
        P(None, "dom"),
        P("dom"),
    )
    return jax.shard_map(
        functools.partial(body, 2), mesh=mesh, in_specs=placed, out_specs=P("dom", None), check_vma=False
    )
```

time: 364 us -> 190 us (0.52)
  local copies, waits for them, and re-layouts: 123 us -> 22.2 us
  matrix products: 79.9 us -> 0 us
  Pallas kernels: 0 us -> 77.6 us
  starting transfers between devices: 97.5 us -> 57.4 us
  other arithmetic: 22.4 us -> 2.9 us
  waiting for transfers between devices: 36 us -> 27.9 us
    gather x65 -> x4, local copies, waits for them, and re-layouts: 118 us -> 2.15 us  [the longest x2 0.86 us: body(): place = all_slots[jnp.maximum(near, 0)]]
    dot_general x44 -> x0, matrix products: 79.9 us -> none  [the longest x6 26.2 us: premultiply(): jnp.einsum('eij,ejk->eik', first_block, second_block, preferred_element_t...]
    pallas_call x0 -> x7, Pallas kernels: none -> 77.6 us  [the longest x2 32.8 us: face_part(): pl.pallas_call(functools.partial(face_kernel, counts), grid=(elems,), out...]
    ppermute x16, starting transfers between devices: 97.5 us -> 57.4 us  [the longest x8 35.1 us: to_side(): return lax.ppermute(array, 'dom', side_pairs)]
    unnamed x68 -> x34, local copies, waits for them, and re-layouts: 0.26 us -> 19.8 us
    concatenate x8 -> x2, other arithmetic: 8.47 us -> 0.15 us  [the longest x1 0.08 us: body(): send_index = jnp.concatenate([side_index, across_index])]
    ppermute x16, waiting for transfers between devices: 36 us -> 27.9 us  [the longest x8 25.9 us: to_across(): return lax.ppermute(array, 'dom', across_pairs)]
    another operation x9 -> x0, other arithmetic: 7.54 us -> none  [the longest x1 7.35 us: body(): jnp.stack([pivot_inverse[send_index], lower_block[send_index], upper_bloc...]
  transfers between devices with their start and end apart: 16 -> 16, of which waited for: 5 -> 6; matrix products, arithmetic and copies ran while one was open for 21% -> 2% of each run, Pallas kernels for 0% -> 20%
where the time goes in v1:
time: 190 us; the launch traced here: 188 us
  Pallas kernels  77.6 us (41%)
  starting transfers between devices  57.4 us (30%)
  waiting for transfers between devices  27.9 us (15%)
  local copies, waits for them, and re-layouts  22.2 us (12%)
  other arithmetic  2.9 us (2%)
    ppermute x8, starting transfers between devices, to_side(): return lax.ppermute(array, 'dom', side_pairs)  35.1 us
    pallas_call x2, Pallas kernels, face_part(): pl.pallas_call(functools.partial(face_kernel, counts), grid=(elems,), out...  32.8 us
    ppermute x8, waiting for transfers between devices, to_across(): return lax.ppermute(array, 'dom', across_pairs)  25.9 us
    ppermute x8, starting transfers between devices, to_across(): return lax.ppermute(array, 'dom', across_pairs)  22.4 us
    pallas_call x2, Pallas kernels, solve(): pl.pallas_call(functools.partial(solve_kernel, last, chunk), out_shape=ou...  22.1 us
    unnamed x34, local copies, waits for them, and re-layouts  19.8 us
    pallas_call x1, Pallas kernels, body(): pl.pallas_call(functools.partial(staying_kernel, slot_count), out_shape=[...  11.5 us
    pallas_call x1, Pallas kernels, body(): pl.pallas_call(functools.partial(outgoing_kernel, chunk, slot_count), out...  9.65 us
  transfers between devices with their start and end apart: 16, of which 6 were waited for; matrix products, arithmetic and copies ran while one was open for 2% of the time, Pallas kernels for 20%

profile of v1, /device:TPU:23, one launch (start us, length us, event | category | flops | bytes accessed | tf_op | source)
XLA Modules:
  0.0 188.3 jit_solution(15525200935508645891)
XLA Ops:
  0.0 0.7 convert_element_type.19.refs_1_
  0.7 0.7 collective-permute-start.5
  1.4 3.0 %collective-permute-start.6 = (bf16[16,320]{1,0:T(8,128)(2,1)S(1)}, bf16[16,320]{1,0:T(8,128)(2,1)S(1)}, u32[]{:S(2)}, u32[]{:S(2)}) collective-permute-start(bf16[16,320]{1,0:T(8,128)(2,1)S(1)} %convert_element_type.19.refs_1_), channel_id=1, source_target_pairs={{1,2},{3,4},{5,6},{7,8},{9,10},{11,12},{13,14},{15,16},{17,18},{19... | collective-permute-start | bytes 30728 | tf_op jit(solution)/shard_map/ppermute | solution.py:293
  4.4 4.4 %collective-permute-start.1 = (s32[16]{0:T(128)}, s32[16]{0:T(128)S(1)}, u32[]{:S(2)}, u32[]{:S(2)}) collective-permute-start(s32[16]{0:T(128)} %slots.3), channel_id=1, source_target_pairs={{1,2},{3,4},{5,6},{7,8},{9,10},{11,12},{13,14},{15,16},{17,18},{19... | collective-permute-start | bytes 200 | tf_op jit(solution)/shard_map/ppermute | solution.py:293
  8.9 2.1 %copy-done = bf16[16,320,320]{2,1,0:T(8,128)(2,1)S(1)} copy-done((bf16[16,320,320]{2,1,0:T(8,128)(2,1)S(1)}, bf16[16,320,320]{2,1,0:T(8,128)(2,1)}, u32[]{:S(2)}) %copy-start) | copy-done | bytes 3276824
  11.0 2.1 %copy-done.6 = bf16[16,320,320]{2,1,0:T(8,128)(2,1)S(1)} copy-done((bf16[16,320,320]{2,1,0:T(8,128)(2,1)S(1)}, bf16[16,320,320]{2,1,0:T(8,128)(2,1)}, u32[]{:S(2)}) %copy-start.6) | copy-done | bytes 3276824
  13.1 0.7 copy-done.10
  13.8 11.5 %staying.1 = (bf16[8,320,640]{2,1,0:T(8,128)(2,1)}, bf16[16,320,640]{2,1,0:T(8,128)(2,1)}) custom-call(s32[16]{0:T(128)S(1)} %copy-done.10, s32[1]{0:T(128)} %bitcast.4.me, s32[1]{0:T(128)} %bitcast.5.target, bf16[16,320,320]{2,1,0:T(8,128)(2,1)S(1)} %copy-done, bf16[16,320,320]{2,1,0:T(8,128)(2,1)S(1)} %copy-done.6, bf16[16,320,320]{2,1,0:T(8,128)(2,1)} %upp.3), custom_call_target="tpu_custom_call" | custom-call | tf_op jit(solution)/shard_map/staying/pallas_call | solution.py:321
  25.3 4.6 %collective-permute-start.2 = (bf16[8,320,640]{2,1,0:T(8,128)(2,1)}, bf16[8,320,640]{2,1,0:T(8,128)(2,1)S(1)}, u32[]{:S(2)}, u32[]{:S(2)}) collective-permute-start(bf16[8,320,640]{2,1,0:T(8,128)(2,1)} %get-tuple-element.18), channel_id=1, source_target_pairs={{0,1},{1,0},{2,3},{3,2},{4,5},{5,4},{6,7},{7,6},{8,9},{9,8},{10,11... | collective-permute-start | bytes 9830408 | tf_op jit(solution)/shard_map/ppermute | solution.py:290
  30.1 0.6 broadcast_add_fusion.3
  30.7 2.1 %copy-done.1 = bf16[16,320,320]{2,1,0:T(8,128)(2,1)S(1)} copy-done((bf16[16,320,320]{2,1,0:T(8,128)(2,1)S(1)}, bf16[16,320,320]{2,1,0:T(8,128)(2,1)}, u32[]{:S(2)}) %copy-start.1) | copy-done | bytes 3276824
  32.8 2.1 %copy-done.7 = bf16[16,320,320]{2,1,0:T(8,128)(2,1)S(1)} copy-done((bf16[16,320,320]{2,1,0:T(8,128)(2,1)S(1)}, bf16[16,320,320]{2,1,0:T(8,128)(2,1)}, u32[]{:S(2)}) %copy-start.7) | copy-done | bytes 3276824
  34.9 9.6 %outgoing.1 = (bf16[2,320,640]{2,1,0:T(8,128)(2,1)S(1)}, bf16[6,320,640]{2,1,0:T(8,128)(2,1)S(1)}) custom-call(s32[16]{0:T(128)S(1)} %copy-done.11, s32[1]{0:T(128)} %bitcast.6.target, bf16[16,320,320]{2,1,0:T(8,128)(2,1)S(1)} %copy-done.1, bf16[16,320,320]{2,1,0:T(8,128)(2,1)S(1)} %copy-done.7, bf16[16,320,320]{2,1,0:T(8,128)(2,1)} %upp.3), custom_call_target="tpu_custom_call" | custom-call | tf_op jit(solution)/shard_map/outgoing/pallas_call | solution.py:300
  44.6 1.5 copy-done.12
  46.0 0.9 copy-done.13
  47.1 0.1 select_reduce_fusion.1
  47.2 0.1 select_reduce_fusion.2
  47.4 1.9 %collective-permute-start.4 = (bf16[6,320,640]{2,1,0:T(8,128)(2,1)}, bf16[6,320,640]{2,1,0:T(8,128)(2,1)}, u32[]{:S(2)}, u32[]{:S(2)}) collective-permute-start(bf16[6,320,640]{2,1,0:T(8,128)(2,1)} %copy-done.12), channel_id=1, source_target_pairs={{1,2},{3,4},{5,6},{7,8},{9,10},{11,12},{13,14},{15,16},{17,18},{19... | collective-permute-start | bytes 7372808 | tf_op jit(solution)/shard_map/ppermute | solution.py:293
  49.5 0.1 fusion.7
  49.6 0.1 select_reduce_fusion.3
  49.8 5.4 %collective-permute-start.3 = (bf16[2,320,640]{2,1,0:T(8,128)(2,1)}, bf16[2,320,640]{2,1,0:T(8,128)(2,1)}, u32[]{:S(2)}, u32[]{:S(2)}) collective-permute-start(bf16[2,320,640]{2,1,0:T(8,128)(2,1)} %copy-done.13), channel_id=1, source_target_pairs={{1,2},{3,4},{5,6},{7,8},{9,10},{11,12},{13,14},{15,16},{17,18},{19... | collective-permute-start | bytes 2457608 | tf_op jit(solution)/shard_map/ppermute | solution.py:293
  55.4 0.1 select_reduce_fusion.4
  55.5 0.6 gather_fusion.1
  56.2 0.6 gather_fusion
  56.8 0.1 fusion.5
  57.1 2.1 %copy-done.2 = bf16[16,320,320]{2,1,0:T(8,128)(2,1)S(1)} copy-done((bf16[16,320,320]{2,1,0:T(8,128)(2,1)S(1)}, bf16[16,320,320]{2,1,0:T(8,128)(2,1)}, u32[]{:S(2)}) %copy-start.2) | copy-done | bytes 3276824
  59.2 16.6 %faces.2 = (f32[8,320]{1,0:T(8,128)S(1)}, f32[8,320]{1,0:T(8,128)S(1)}, f32[16,320]{1,0:T(8,128)S(1)}) custom-call(s32[16]{0:T(128)S(1)} %pad_add_fusion.1.send_ref, s32[64,1]{1,0:T(8,128)S(1)} %reshape.78.index_ref, f32[16,320]{1,0:T(8,128)S(1)} %copy-done.8, bf16[16,320]{1,0:T(8,128)(2,1)S(1)} %collective-permute-done.5.refs_0_, ...), custom_call_target="tpu_custom_call" | custom-call | tf_op jit(solution)/shard_map/faces/pallas_call | solution.py:386
  75.8 1.9 %collective-permute-start.8 = (f32[8,320]{1,0:T(8,128)S(1)}, f32[8,320]{1,0:T(8,128)S(1)}, u32[]{:S(2)}, u32[]{:S(2)}) collective-permute-start(f32[8,320]{1,0:T(8,128)S(1)} %get-tuple-element.24), channel_id=1, source_target_pairs={{1,2},{3,4},{5,6},{7,8},{9,10},{11,12},{13,14},{15,16},{17,18},{19... | collective-permute-start | bytes 30728 | tf_op jit(solution)/shard_map/ppermute | solution.py:293
  77.9 11.8 %collective-permute-done.8.across_s = f32[8,320]{1,0:T(8,128)S(1)} collective-permute-done((f32[8,320]{1,0:T(8,128)S(1)}, f32[8,320]{1,0:T(8,128)S(1)}, u32[]{:S(2)}, u32[]{:S(2)}) %collective-permute-start.8) | collective-permute-done | bytes 10272 | tf_op jit(solution)/shard_map/ppermute | solution.py:293
  89.7 10.9 %solve.2.refs_0_ = bf16[32,320]{1,0:T(8,128)(2,1)S(1)} custom-call(s32[32]{0:T(128)S(1)} %select_reduce_fusion.table, s32[32]{0:T(128)S(1)} %get-tuple-element.33.back, bf16[8,320,640]{2,1,0:T(8,128)(2,1)S(1)} %collective-permute-done.2.side_m, bf16[16,320,640]{2,1,0:T(8,128)(2,1)S(1)} %copy-done.4, bf16[2,320,640]{2,1,0:T(8,128)(2,1)} %collective-permute-done.3.first_m, ...), custom_call_target="tpu_custom_call" | custom-call | tf_op jit(solution)/shard_map/solve/pallas_call | solution.py:416
  100.6 29.4 %collective-permute-start.9 = (bf16[32,320]{1,0:T(8,128)(2,1)S(1)}, bf16[32,320]{1,0:T(8,128)(2,1)S(1)}, u32[]{:S(2)}, u32[]{:S(2)}) collective-permute-start(bf16[32,320]{1,0:T(8,128)(2,1)S(1)} %solve.2.refs_0_), channel_id=1, source_target_pairs={{0,1},{1,0},{2,3},{3,2},{4,5},{5,4},{6,7},{7,6},{8,9},{9,8},{10,11... | collective-permute-start | bytes 61448 | tf_op jit(solution)/shard_map/ppermute | solution.py:290
  130.1 0.8 collective-permute-done.9.refs_1_
  130.9 1.9 %collective-permute-start.10 = (bf16[64,320]{1,0:T(8,128)(2,1)S(1)}, bf16[64,320]{1,0:T(8,128)(2,1)S(1)}, u32[]{:S(2)}, u32[]{:S(2)}) collective-permute-start(bf16[64,320]{1,0:T(8,128)(2,1)S(1)} %maximum_select_fusion), channel_id=1, source_target_pairs={{1,2},{3,4},{5,6},{7,8},{9,10},{11,12},{13,14},{15,16},{17,18},{19... | collective-permute-start | bytes 122888 | tf_op jit(solution)/shard_map/ppermute | solution.py:293
  132.9 0.8 gather_fusion.2
  133.8 4.3 %collective-permute-done.10.refs_2_ = bf16[64,320]{1,0:T(8,128)(2,1)S(1)} collective-permute-done((bf16[64,320]{1,0:T(8,128)(2,1)S(1)}, bf16[64,320]{1,0:T(8,128)(2,1)S(1)}, u32[]{:S(2)}, u32[]{:S(2)}) %collective-permute-start.10) | collective-permute-done | bytes 40992 | tf_op jit(solution)/shard_map/ppermute | solution.py:293
  138.2 1.1 collective-permute-done.11.refs_3_
  139.4 2.1 %copy-done.3 = bf16[16,320,320]{2,1,0:T(8,128)(2,1)S(1)} copy-done((bf16[16,320,320]{2,1,0:T(8,128)(2,1)S(1)}, bf16[16,320,320]{2,1,0:T(8,128)(2,1)}, u32[]{:S(2)}) %copy-start.3) | copy-done | bytes 3276824
  141.5 16.2 %faces.3 = (f32[8,320]{1,0:T(8,128)S(1)}, f32[8,320]{1,0:T(8,128)S(1)}, f32[16,320]{1,0:T(8,128)S(1)}) custom-call(s32[16]{0:T(128)S(1)} %pad_add_fusion.1.send_ref, s32[64,1]{1,0:T(8,128)S(1)} %reshape.77.index_ref, f32[16,320]{1,0:T(8,128)S(1)} %copy-done.8, bf16[32,320]{1,0:T(8,128)(2,1)S(1)} %solve.2.refs_0_, ...), custom_call_target="tpu_custom_call" | custom-call | tf_op jit(solution)/shard_map/faces/pallas_call | solution.py:386
  157.7 0.2 collective-permute-start.12
  157.9 1.9 %collective-permute-start.13 = (f32[8,320]{1,0:T(8,128)S(1)}, f32[8,320]{1,0:T(8,128)S(1)}, u32[]{:S(2)}, u32[]{:S(2)}) collective-permute-start(f32[8,320]{1,0:T(8,128)S(1)} %get-tuple-element.27), channel_id=1, source_target_pairs={{1,2},{3,4},{5,6},{7,8},{9,10},{11,12},{13,14},{15,16},{17,18},{19... | collective-permute-start | bytes 30728 | tf_op jit(solution)/shard_map/ppermute | solution.py:293
  159.9 4.9 %collective-permute-done.13.across_s = f32[8,320]{1,0:T(8,128)S(1)} collective-permute-done((f32[8,320]{1,0:T(8,128)S(1)}, f32[8,320]{1,0:T(8,128)S(1)}, u32[]{:S(2)}, u32[]{:S(2)}) %collective-permute-start.13) | collective-permute-done | bytes 10272 | tf_op jit(solution)/shard_map/ppermute | solution.py:293
  164.7 2.9 %copy-done.5 = bf16[16,320,640]{2,1,0:T(8,128)(2,1)S(1)} copy-done((bf16[16,320,640]{2,1,0:T(8,128)(2,1)S(1)}, bf16[16,320,640]{2,1,0:T(8,128)(2,1)}, u32[]{:S(2)}) %copy-start.5) | copy-done | bytes 6553624
  167.6 11.2 %solve.3 = (f32[8,320]{1,0:T(8,128)S(1)}, f32[16,320]{1,0:T(8,128)S(1)}, f32[8,320]{1,0:T(8,128)S(1)}) custom-call(s32[32]{0:T(128)S(1)} %select_reduce_fusion.table, s32[32]{0:T(128)S(1)} %get-tuple-element.33.back, bf16[8,320,640]{2,1,0:T(8,128)(2,1)S(1)} %collective-permute-done.2.side_m, bf16[16,320,640]{2,1,0:T(8,128)(2,1)S(1)} %copy-done.5, ...), custom_call_target="tpu_custom_call" | custom-call | tf_op jit(solution)/shard_map/solve/pallas_call | solution.py:416
  178.8 0.6 copy-done.9
  179.4 1.9 %collective-permute-start.15 = (f32[8,320]{1,0:T(8,128)S(1)}, f32[8,320]{1,0:T(8,128)S(1)}, u32[]{:S(2)}, u32[]{:S(2)}) collective-permute-start(f32[8,320]{1,0:T(8,128)S(1)} %get-tuple-element.30), channel_id=1, source_target_pairs={{1,2},{3,4},{5,6},{7,8},{9,10},{11,12},{13,14},{15,16},{17,18},{19... | collective-permute-start | bytes 30728 | tf_op jit(solution)/shard_map/ppermute | solution.py:293
  181.4 4.9 %collective-permute-done.15.across = f32[8,320]{1,0:T(8,128)S(1)} collective-permute-done((f32[8,320]{1,0:T(8,128)S(1)}, f32[8,320]{1,0:T(8,128)S(1)}, u32[]{:S(2)}, u32[]{:S(2)}) %collective-permute-start.15) | collective-permute-done | bytes 10272 | tf_op jit(solution)/shard_map/ppermute | solution.py:293
  186.2 0.6 copy-done.15
  186.8 1.4 place.1
  (63 shorter events, 1.4 us)
Async XLA Ops:
  0.7 56.3 %collective-permute-start.5 = (bf16[16,320]{1,0:T(8,128)(2,1)S(1)}, bf16[16,320]{1,0:T(8,128)(2,1)S(1)}, u32[]{:S(2)}, u32[]{:S(2)}) collective-permute-start(bf16[16,320]{1,0:T(8,128)(2,1)S(1)} %convert_element_type.19.refs_1_), channel_id=1, source_target_pairs={{0,1},{1,0},{2,3},{3,2},{4,5},{5,4},{6,7},{7,6},{8,9},{9,8},{10,11... | collective-permute-start | bytes 30728 | tf_op jit(solution)/shard_map/ppermute | solution.py:290
  1.4 55.6 %collective-permute-start.6 = (bf16[16,320]{1,0:T(8,128)(2,1)S(1)}, bf16[16,320]{1,0:T(8,128)(2,1)S(1)}, u32[]{:S(2)}, u32[]{:S(2)}) collective-permute-start(bf16[16,320]{1,0:T(8,128)(2,1)S(1)} %convert_element_type.19.refs_1_), channel_id=1, source_target_pairs={{1,2},{3,4},{5,6},{7,8},{9,10},{11,12},{13,14},{15,16},{17,18},{19... | collective-permute-start | bytes 30728 | tf_op jit(solution)/shard_map/ppermute | solution.py:293
  4.4 43.0 %collective-permute-start.1 = (s32[16]{0:T(128)}, s32[16]{0:T(128)S(1)}, u32[]{:S(2)}, u32[]{:S(2)}) collective-permute-start(s32[16]{0:T(128)} %slots.3), channel_id=1, source_target_pairs={{1,2},{3,4},{5,6},{7,8},{9,10},{11,12},{13,14},{15,16},{17,18},{19... | collective-permute-start | bytes 200 | tf_op jit(solution)/shard_map/ppermute | solution.py:293
  8.8 41.0 %collective-permute-start = (s32[16]{0:T(128)}, s32[16]{0:T(128)S(1)}, u32[]{:S(2)}, u32[]{:S(2)}) collective-permute-start(s32[16]{0:T(128)} %slots.3), channel_id=1, source_target_pairs={{0,1},{1,0},{2,3},{3,2},{4,5},{5,4},{6,7},{7,6},{8,9},{9,8},{10,11... | collective-permute-start | bytes 200 | tf_op jit(solution)/shard_map/ppermute | solution.py:290
  8.9 2.1 %copy-start = (bf16[16,320,320]{2,1,0:T(8,128)(2,1)S(1)}, bf16[16,320,320]{2,1,0:T(8,128)(2,1)}, u32[]{:S(2)}) copy-start(bf16[16,320,320]{2,1,0:T(8,128)(2,1)} %refs_5_.1) | copy-start | bytes 9830404
  11.0 2.1 %copy-start.6 = (bf16[16,320,320]{2,1,0:T(8,128)(2,1)S(1)}, bf16[16,320,320]{2,1,0:T(8,128)(2,1)}, u32[]{:S(2)}) copy-start(bf16[16,320,320]{2,1,0:T(8,128)(2,1)} %low.3) | copy-start | bytes 9830404
  13.1 0.7 copy-start.10
  13.8 16.2 %copy-start.11 = (s32[16]{0:T(128)S(1)}, s32[16]{0:T(128)}, u32[]{:S(2)}) copy-start(s32[16]{0:T(128)} %slots.3) | copy-start | bytes 196
  13.8 16.2 %copy-start.16 = (s32[4,16]{1,0:T(4,128)S(1)}, s32[4,16]{1,0:T(4,128)}, u32[]{:S(2)}) copy-start(s32[4,16]{1,0:T(4,128)} %param.14) | copy-start | bytes 772
  25.3 64.4 %collective-permute-start.2 = (bf16[8,320,640]{2,1,0:T(8,128)(2,1)}, bf16[8,320,640]{2,1,0:T(8,128)(2,1)S(1)}, u32[]{:S(2)}, u32[]{:S(2)}) collective-permute-start(bf16[8,320,640]{2,1,0:T(8,128)(2,1)} %get-tuple-element.18), channel_id=1, source_target_pairs={{0,1},{1,0},{2,3},{3,2},{4,5},{5,4},{6,7},{7,6},{8,9},{9,8},{10,11... | collective-permute-start | bytes 9830408 | tf_op jit(solution)/shard_map/ppermute | solution.py:290
  30.7 2.1 %copy-start.1 = (bf16[16,320,320]{2,1,0:T(8,128)(2,1)S(1)}, bf16[16,320,320]{2,1,0:T(8,128)(2,1)}, u32[]{:S(2)}) copy-start(bf16[16,320,320]{2,1,0:T(8,128)(2,1)} %refs_5_.1) | copy-start | bytes 9830404
  32.8 2.1 %copy-start.7 = (bf16[16,320,320]{2,1,0:T(8,128)(2,1)S(1)}, bf16[16,320,320]{2,1,0:T(8,128)(2,1)}, u32[]{:S(2)}) copy-start(bf16[16,320,320]{2,1,0:T(8,128)(2,1)} %low.3) | copy-start | bytes 9830404
  34.9 22.1 %copy-start.8 = (f32[16,320]{1,0:T(8,128)S(1)}, f32[16,320]{1,0:T(8,128)}, u32[]{:S(2)}) copy-start(f32[16,320]{1,0:T(8,128)} %rhs_ref.3) | copy-start | bytes 61444
  44.6 1.5 copy-start.12
  46.0 0.9 copy-start.13
  47.4 42.2 %collective-permute-start.4 = (bf16[6,320,640]{2,1,0:T(8,128)(2,1)}, bf16[6,320,640]{2,1,0:T(8,128)(2,1)}, u32[]{:S(2)}, u32[]{:S(2)}) collective-permute-start(bf16[6,320,640]{2,1,0:T(8,128)(2,1)} %copy-done.12), channel_id=1, source_target_pairs={{1,2},{3,4},{5,6},{7,8},{9,10},{11,12},{13,14},{15,16},{17,18},{19... | collective-permute-start | bytes 7372808 | tf_op jit(solution)/shard_map/ppermute | solution.py:293
  49.8 39.9 %collective-permute-start.3 = (bf16[2,320,640]{2,1,0:T(8,128)(2,1)}, bf16[2,320,640]{2,1,0:T(8,128)(2,1)}, u32[]{:S(2)}, u32[]{:S(2)}) collective-permute-start(bf16[2,320,640]{2,1,0:T(8,128)(2,1)} %copy-done.13), channel_id=1, source_target_pairs={{1,2},{3,4},{5,6},{7,8},{9,10},{11,12},{13,14},{15,16},{17,18},{19... | collective-permute-start | bytes 2457608 | tf_op jit(solution)/shard_map/ppermute | solution.py:293
  57.1 2.1 %copy-start.2 = (bf16[16,320,320]{2,1,0:T(8,128)(2,1)S(1)}, bf16[16,320,320]{2,1,0:T(8,128)(2,1)}, u32[]{:S(2)}) copy-start(bf16[16,320,320]{2,1,0:T(8,128)(2,1)} %refs_5_.1) | copy-start | bytes 9830404
  59.2 30.5 %copy-start.4 = (bf16[16,320,640]{2,1,0:T(8,128)(2,1)S(1)}, bf16[16,320,640]{2,1,0:T(8,128)(2,1)}, u32[]{:S(2)}) copy-start(bf16[16,320,640]{2,1,0:T(8,128)(2,1)} %get-tuple-element.19.own_m) | copy-start | bytes 19660804
  75.7 2.1 %collective-permute-start.7 = (f32[8,320]{1,0:T(8,128)S(1)}, f32[8,320]{1,0:T(8,128)S(1)}, u32[]{:S(2)}, u32[]{:S(2)}) collective-permute-start(f32[8,320]{1,0:T(8,128)S(1)} %get-tuple-element.22), channel_id=1, source_target_pairs={{0,1},{1,0},{2,3},{3,2},{4,5},{5,4},{6,7},{7,6},{8,9},{9,8},{10,11... | collective-permute-start | bytes 30728 | tf_op jit(solution)/shard_map/ppermute | solution.py:290
  75.8 13.9 %collective-permute-start.8 = (f32[8,320]{1,0:T(8,128)S(1)}, f32[8,320]{1,0:T(8,128)S(1)}, u32[]{:S(2)}, u32[]{:S(2)}) collective-permute-start(f32[8,320]{1,0:T(8,128)S(1)} %get-tuple-element.24), channel_id=1, source_target_pairs={{1,2},{3,4},{5,6},{7,8},{9,10},{11,12},{13,14},{15,16},{17,18},{19... | collective-permute-start | bytes 30728 | tf_op jit(solution)/shard_map/ppermute | solution.py:293
  100.6 30.3 %collective-permute-start.9 = (bf16[32,320]{1,0:T(8,128)(2,1)S(1)}, bf16[32,320]{1,0:T(8,128)(2,1)S(1)}, u32[]{:S(2)}, u32[]{:S(2)}) collective-permute-start(bf16[32,320]{1,0:T(8,128)(2,1)S(1)} %solve.2.refs_0_), channel_id=1, source_target_pairs={{0,1},{1,0},{2,3},{3,2},{4,5},{5,4},{6,7},{7,6},{8,9},{9,8},{10,11... | collective-permute-start | bytes 61448 | tf_op jit(solution)/shard_map/ppermute | solution.py:290
  130.9 7.2 %collective-permute-start.10 = (bf16[64,320]{1,0:T(8,128)(2,1)S(1)}, bf16[64,320]{1,0:T(8,128)(2,1)S(1)}, u32[]{:S(2)}, u32[]{:S(2)}) collective-permute-start(bf16[64,320]{1,0:T(8,128)(2,1)S(1)} %maximum_select_fusion), channel_id=1, source_target_pairs={{1,2},{3,4},{5,6},{7,8},{9,10},{11,12},{13,14},{15,16},{17,18},{19... | collective-permute-start | bytes 122888 | tf_op jit(solution)/shard_map/ppermute | solution.py:293
  138.1 1.2 collective-permute-start.11
  139.4 2.1 %copy-start.3 = (bf16[16,320,320]{2,1,0:T(8,128)(2,1)S(1)}, bf16[16,320,320]{2,1,0:T(8,128)(2,1)}, u32[]{:S(2)}) copy-start(bf16[16,320,320]{2,1,0:T(8,128)(2,1)} %refs_5_.1) | copy-start | bytes 9830404
  157.7 2.2 %collective-permute-start.12 = (f32[8,320]{1,0:T(8,128)S(1)}, f32[8,320]{1,0:T(8,128)S(1)}, u32[]{:S(2)}, u32[]{:S(2)}) collective-permute-start(f32[8,320]{1,0:T(8,128)S(1)} %get-tuple-element.25), channel_id=1, source_target_pairs={{0,1},{1,0},{2,3},{3,2},{4,5},{5,4},{6,7},{7,6},{8,9},{9,8},{10,11... | collective-permute-start | bytes 30728 | tf_op jit(solution)/shard_map/ppermute | solution.py:290
  157.9 6.8 %collective-permute-start.13 = (f32[8,320]{1,0:T(8,128)S(1)}, f32[8,320]{1,0:T(8,128)S(1)}, u32[]{:S(2)}, u32[]{:S(2)}) collective-permute-start(f32[8,320]{1,0:T(8,128)S(1)} %get-tuple-element.27), channel_id=1, source_target_pairs={{1,2},{3,4},{5,6},{7,8},{9,10},{11,12},{13,14},{15,16},{17,18},{19... | collective-permute-start | bytes 30728 | tf_op jit(solution)/shard_map/ppermute | solution.py:293
  164.7 2.9 %copy-start.5 = (bf16[16,320,640]{2,1,0:T(8,128)(2,1)S(1)}, bf16[16,320,640]{2,1,0:T(8,128)(2,1)}, u32[]{:S(2)}) copy-start(bf16[16,320,640]{2,1,0:T(8,128)(2,1)} %get-tuple-element.19.own_m) | copy-start | bytes 19660804
  178.8 0.6 copy-start.9
  179.4 1.9 %collective-permute-start.14 = (f32[8,320]{1,0:T(8,128)S(1)}, f32[8,320]{1,0:T(8,128)S(1)}, u32[]{:S(2)}, u32[]{:S(2)}) collective-permute-start(f32[8,320]{1,0:T(8,128)S(1)} %get-tuple-element.28), channel_id=1, source_target_pairs={{0,1},{1,0},{2,3},{3,2},{4,5},{5,4},{6,7},{7,6},{8,9},{9,8},{10,11... | collective-permute-start | bytes 30728 | tf_op jit(solution)/shard_map/ppermute | solution.py:290
  179.4 6.8 %collective-permute-start.15 = (f32[8,320]{1,0:T(8,128)S(1)}, f32[8,320]{1,0:T(8,128)S(1)}, u32[]{:S(2)}, u32[]{:S(2)}) collective-permute-start(f32[8,320]{1,0:T(8,128)S(1)} %get-tuple-element.30), channel_id=1, source_target_pairs={{1,2},{3,4},{5,6},{7,8},{9,10},{11,12},{13,14},{15,16},{17,18},{19... | collective-permute-start | bytes 30728 | tf_op jit(solution)/shard_map/ppermute | solution.py:293
  181.4 4.9 %copy-start.14 = (f32[8,320]{1,0:T(8,128)}, f32[8,320]{1,0:T(8,128)S(1)}, u32[]{:S(2)}) copy-start(f32[8,320]{1,0:T(8,128)S(1)} %collective-permute-done.14.side) | copy-start | bytes 30724
  186.2 0.6 copy-start.15

commit v2 on v1

--- a/solution.py
+++ b/solution.py
@@ -10,9 +10,13 @@
 LMAX = 8
 SWEEPS = 2
 WIDE = 256
-ANY = pl.BlockSpec(memory_space=pl.ANY)
+HBM = pl.BlockSpec(memory_space=pltpu.HBM)
 SMEM = pl.BlockSpec(memory_space=pltpu.SMEM)
 VMEM = pl.BlockSpec(memory_space=pltpu.VMEM)
+ROOMY = pltpu.CompilerParams(vmem_limit_bytes=57 << 20)
+FACING = pltpu.CompilerParams(vmem_limit_bytes=50 << 20)
+SNUG = pltpu.CompilerParams(vmem_limit_bytes=52 << 20)
+SMALL = pl.CostEstimate(flops=1 << 20, bytes_accessed=1 << 20, transcendentals=0)
 NT = (((1,), (1,)), ((), ()))
 
 
@@ -25,48 +29,53 @@
 
 
 def pair_product(pivot, lower, upper, out):
-    out[:, :WIDE] = dot_nn(pivot, lower[:, :WIDE]).astype(jnp.bfloat16)
-    out[:, WIDE : 2 * WIDE] = dot_nn(pivot, upper[:, :WIDE]).astype(jnp.bfloat16)
-    tails = jnp.concatenate([lower[:, WIDE:], upper[:, WIDE:]], axis=1)
-    out[:, 2 * WIDE :] = dot_nn(pivot, tails).astype(jnp.bfloat16)
-
-
-def outgoing_kernel(chunk, slot_count, slots, target, piv, low, upp, first, second, pb, lb, ub, stage, insem, outsem):
-    bucket = stage.shape[0]
-    count = jnp.int32(0)
-    for e in range(slots.shape[0]):
-        hit = (slots[e] // slot_count) == target[0]
-
-        @pl.when(hit)
-        def _(e=e, count=count):
-            pltpu.make_async_copy(piv.at[e], pb.at[count], insem.at[0, count]).start()
-            pltpu.make_async_copy(low.at[e], lb.at[count], insem.at[1, count]).start()
-            pltpu.make_async_copy(upp.at[e], ub.at[count], insem.at[2, count]).start()
-
-        count = count + hit.astype(jnp.int32)
-
-    def sent(k):
-        dest = first.at[k] if k < chunk else second.at[k - chunk]
-        return pltpu.make_async_copy(stage.at[k], dest, outsem.at[k])
-
-    for k in range(bucket):
-
-        @pl.when(k < count)
-        def _(k=k):
+    both = jnp.concatenate([lower.T, upper.T], axis=0)
+    got = dot_nt(both, pivot).astype(jnp.bfloat16)
+    width = pivot.shape[0]
+    out[:, :WIDE] = got[:width, :WIDE]
+    out[:, WIDE : 2 * WIDE] = got[width:, :WIDE]
+    out[:, 2 * WIDE :] = jnp.concatenate([got[:width, WIDE:], got[width:, WIDE:]], axis=1)
+
+
+def outgoing_kernel(slot_count, slots, targets, piv, low, upp, over_out, side_out, pb, lb, ub, stage, insem, outsem):
+    bucket = over_out.shape[0]
+    counts = []
+    for which in range(2):
+        count = jnp.int32(which * bucket)
+        for e in range(slots.shape[0]):
+            hit = (slots[e] // slot_count) == targets[which]
+
+            @pl.when(hit)
+            def _(e=e, count=count):
+                pltpu.make_async_copy(piv.at[e], pb.at[count], insem.at[0, count]).start()
+                pltpu.make_async_copy(low.at[e], lb.at[count], insem.at[1, count]).start()
+                pltpu.make_async_copy(upp.at[e], ub.at[count], insem.at[2, count]).start()
+
+            count = count + hit.astype(jnp.int32)
+        counts.append(count)
+    for which, out in enumerate((over_out, side_out)):
+        first = which * bucket
+
+        def step(k, carry, out=out, first=first):
             pltpu.make_async_copy(piv.at[0], pb.at[k], insem.at[0, k]).wait()
             pltpu.make_async_copy(low.at[0], lb.at[k], insem.at[1, k]).wait()
             pltpu.make_async_copy(upp.at[0], ub.at[k], insem.at[2, k]).wait()
             pair_product(pb[k], lb[k], ub[k], stage.at[k])
-            sent(k).start()
-
-    for k in range(bucket):
-
-        @pl.when(k < count)
-        def _(k=k):
-            sent(k).wait()
-
-
-def staying_kernel(slot_count, slots, me, target, piv, low, upp, beside, own, pb, lb, ub, stage, insem, outsem):
+            pltpu.make_async_copy(stage.at[k], out.at[k - first], outsem.at[k]).start()
+            return carry
+
+        lax.fori_loop(first, counts[which], step, 0)
+    for which, out in enumerate((over_out, side_out)):
+        first = which * bucket
+
+        def drain(k, carry, out=out, first=first):
+            pltpu.make_async_copy(stage.at[k], out.at[k - first], outsem.at[k]).wait()
+            return carry
+
+        lax.fori_loop(first, counts[which], drain, 0)
+
+
+def staying_kernel(slot_count, slots, me, piv, low, upp, own, pb, lb, ub, stage, insem, outsem):
     elems = slots.shape[0]
 
     def loads(e):
@@ -75,79 +84,84 @@
             for i, (src, dst) in enumerate(((piv, pb), (low, lb), (upp, ub)))
         ]
 
+    def send(e):
+        return pltpu.make_async_copy(stage.at[e], own.at[e], outsem.at[e])
+
     for e in range(elems):
-        owner = slots[e] // slot_count
-
-        @pl.when((owner == me[0]) | (owner == target[0]))
+
+        @pl.when(slots[e] // slot_count == me[0])
         def _(e=e):
             for copy in loads(e):
                 copy.start()
 
-    def step(e, count):
-        owner = slots[e] // slot_count
-        across = owner == target[0]
-
-        @pl.when((owner == me[0]) | across)
+    def step(e, carry):
+        @pl.when(slots[e] // slot_count == me[0])
         def _():
             for copy in loads(e):
                 copy.wait()
             pair_product(pb[e], lb[e], ub[e], stage.at[e])
-
-        @pl.when(across)
-        def _():
-            pltpu.make_async_copy(stage.at[e], beside.at[count], outsem.at[e]).start()
-
-        @pl.when(owner == me[0])
-        def _():
-            pltpu.make_async_copy(stage.at[e], own.at[e], outsem.at[e]).start()
-
-        return count + across.astype(jnp.int32)
-
-    lax.fori_loop(0, elems, step, jnp.int32(0))
+            send(e).start()
+
+        return carry
+
+    lax.fori_loop(0, elems, step, 0)
     for e in range(elems):
-        owner = slots[e] // slot_count
-
-        @pl.when((owner == me[0]) | (owner == target[0]))
+
+        @pl.when(slots[e] // slot_count == me[0])
         def _(e=e):
-            pltpu.make_async_copy(stage.at[e], own.at[e], outsem.at[e]).wait()
-
-
-def face_kernel(counts, send_ref, index_ref, rhs_ref, *refs):
+            send(e).wait()
+
+
+def face_kernel(counts, send, index, rhs, *refs):
     parts = refs[: len(counts)]
-    faces_ref, piv_ref, side_ref, across_ref, own_ref, rows, gathered, scaled = refs[len(counts) :]
-    e = pl.program_id(0)
-    elems = rhs_ref.shape[0]
-    faces = faces_ref.shape[1]
-    width = rhs_ref.shape[1]
-
-    @pl.when(e == 0)
-    def _():
-        at = 0
-        for part, size in zip(parts, counts):
-            rows[at : at + size] = part[...]
-            at += size
-        wanted = index_ref[...] == lax.broadcasted_iota(jnp.int32, (faces * elems, at), 1)
-        picked = dot_nn(wanted.astype(jnp.bfloat16), rows[...])
-        gathered[...] = picked.astype(jnp.bfloat16)
-
-    total = dot_nt(gathered[:elems], faces_ref[0, 0])
-    for f in range(1, faces):
-        total += dot_nt(gathered[f * elems : (f + 1) * elems], faces_ref[0, f])
-    residual = (rhs_ref[...] - total).astype(jnp.bfloat16)
-    applied = dot_nt(residual, piv_ref[0])
+    faces, piv, side_out, across_out, own_out, rows, gathered, held, scaled, fb, pb, fsem, psem = refs[len(counts) :]
+    elems, width = rhs.shape
+    count = faces.shape[1]
+    face_copies = [pltpu.make_async_copy(faces.at[e], fb.at[e], fsem.at[e]) for e in range(elems)]
+    piv_copies = [pltpu.make_async_copy(piv.at[e], pb.at[e], psem.at[e]) for e in range(elems)]
+    for face_copy, piv_copy in zip(face_copies, piv_copies):
+        face_copy.start()
+        piv_copy.start()
+    at = 0
+    for part, size in zip(parts, counts):
+        rows[at : at + size] = part[...]
+        at += size
+    wanted = index[...] == lax.broadcasted_iota(jnp.int32, (count * elems, at), 1)
+    picked = dot_nn(wanted.astype(jnp.bfloat16), rows[...]).astype(jnp.bfloat16)
+    gathered[...] = picked
+    ends = jnp.concatenate([picked[f * elems : (f + 1) * elems, WIDE:] for f in range(count)], axis=1)
     row = lax.broadcasted_iota(jnp.int32, (elems, width), 0)
-    scaled[...] = jnp.where(row == e, applied, scaled[...])
-
-    @pl.when(e == elems - 1)
-    def _():
-        own_ref[...] = scaled[...]
-        bucket = side_ref.shape[0]
-        for k in range(bucket):
-            side_ref[k : k + 1] = scaled[pl.ds(send_ref[k], 1), :]
-            across_ref[k : k + 1] = scaled[pl.ds(send_ref[bucket + k], 1), :]
-
-
-def solve_kernel(last, chunk, table, back, side_m, own_m, first_m, second_m, side_s, own_s, across_s, *refs):
+
+    def residual(e):
+        pltpu.make_async_copy(faces.at[e], fb.at[e], fsem.at[e]).wait()
+        total = dot_nt(gathered[:elems, :WIDE], fb[e, 0, :, :WIDE])
+        for f in range(1, count):
+            total += dot_nt(gathered[f * elems : (f + 1) * elems, :WIDE], fb[e, f, :, :WIDE])
+        tails = jnp.concatenate([fb[e, f, :, WIDE:] for f in range(count)], axis=1)
+        total += dot_nt(ends, tails)
+        return (rhs[...] - total).astype(jnp.bfloat16)
+
+    def apply(e):
+        pltpu.make_async_copy(piv.at[e], pb.at[e], psem.at[e]).wait()
+        scaled[...] = jnp.where(row == e, dot_nt(held[...], pb[e]), scaled[...])
+
+    held[...] = residual(0)
+
+    def step(e, carry):
+        apply(e - 1)
+        held[...] = residual(e)
+        return carry
+
+    lax.fori_loop(1, elems, step, 0)
+    apply(elems - 1)
+    own_out[...] = scaled[...]
+    bucket = side_out.shape[0]
+    for k in range(bucket):
+        side_out[k : k + 1] = scaled[pl.ds(send[k], 1), :]
+        across_out[k : k + 1] = scaled[pl.ds(send[bucket + k], 1), :]
+
+
+def solve_kernel(last, table, back, side_m, own_m, across_m, side_s, own_s, across_s, *refs):
     outs = refs[:3] if last else refs[:1]
     mats, items, ahead, behind, sems = refs[len(outs) :]
     bucket = side_s.shape[0]
@@ -163,8 +177,7 @@
         sources = (
             (side_m, 0, bucket),
             (own_m, bucket, bucket + elems),
-            (first_m, bucket + elems, bucket + elems + chunk),
-            (second_m, bucket + elems + chunk, 2 * bucket + elems),
+            (across_m, bucket + elems, 2 * bucket + elems),
         )
         for source, low, high in sources:
 
@@ -181,19 +194,15 @@
     items[bucket + elems :] = across_s[...]
     sublanes = ahead.shape[1]
     row = lax.broadcasted_iota(jnp.int32, (sublanes, width), 0)
-    zeros = jnp.zeros((sublanes, tail), jnp.bfloat16)
 
     def sweep_step(p, x, half):
-        lead = x[:, :WIDE]
-        ends = [x[:, WIDE:], zeros] if half == 0 else [zeros, x[:, WIDE:]]
-        ending = jnp.concatenate(ends, axis=1)
         carried = jnp.zeros((sublanes, width), jnp.float32)
         for r in range(lines):
             at = p * lines + r
-            got = dot_nt(lead, mats[at, :, half * WIDE : (half + 1) * WIDE])
-            got += dot_nt(ending, mats[at, :, 2 * WIDE :])
+            lead = dot_nn(x, mats[at, :, half * WIDE : (half + 1) * WIDE])
+            ending = dot_nn(x, mats[at, :, 2 * WIDE :])[:, half * tail : (half + 1) * tail]
             live = table[r * LMAX + p] >= 0
-            carried = jnp.where((row == r) & live, got, carried)
+            carried = jnp.where((row == r) & live, jnp.concatenate([lead, ending], axis=1), carried)
         return carried
 
     for p in range(LMAX):
@@ -261,7 +270,6 @@
 
 
 def body(
-    chunk,
     right_side,
     start_state,
     pivot_inverse,
@@ -297,43 +305,45 @@
     pair = (width, packed)
     dma = pltpu.SemaphoreType.DMA
 
-    first, second = pl.pallas_call(
-        functools.partial(outgoing_kernel, chunk, slot_count),
-        out_shape=[
-            jax.ShapeDtypeStruct((chunk,) + pair, bf16),
-            jax.ShapeDtypeStruct((bucket - chunk,) + pair, bf16),
-        ],
-        in_specs=[SMEM, SMEM, ANY, ANY, ANY],
-        out_specs=[ANY, ANY],
-        scratch_shapes=[pltpu.VMEM((bucket,) + block, bf16)] * 3
-        + [pltpu.VMEM((bucket,) + pair, bf16), dma((3, bucket)), dma((bucket,))],
-        compiler_params=pltpu.CompilerParams(vmem_limit_bytes=40 << 20),
+    rounded = start_state.astype(bf16)
+    owner = element_slot // slot_count
+    code = (element_slot - (me - 1) * slot_count).astype(bf16)
+    column = lax.broadcasted_iota(jnp.int32, (elems, 128), 1)
+    halo = jnp.concatenate([rounded, jnp.where(column == 0, code[:, None], jnp.zeros((), bf16))[:, : 384 - width]], axis=1)
+    halo_across = to_across(halo)
+    halo_side = to_side(halo)
+    outgoing, side_pack = pl.pallas_call(
+        functools.partial(outgoing_kernel, slot_count),
+        out_shape=[jax.ShapeDtypeStruct((bucket,) + pair, bf16)] * 2,
+        in_specs=[SMEM, SMEM, HBM, HBM, HBM],
+        out_specs=[HBM, HBM],
+        scratch_shapes=[pltpu.VMEM((2 * bucket,) + block, bf16)] * 3
+        + [pltpu.VMEM((2 * bucket,) + pair, bf16), dma((3, 2 * bucket)), dma((2 * bucket,))],
+        compiler_params=ROOMY,
+        cost_estimate=SMALL,
         name="outgoing",
-    )(element_slot, across[None], pivot_inverse, lower_block, upper_block)
-    first_in = to_across(first)
-    rounded = start_state.astype(bf16)
-    state_across = to_across(rounded)
-    slot_across = to_across(element_slot)
-    second_in = to_across(second)
-    state_side = to_side(rounded)
-    slot_side = to_side(element_slot)
-
-    side_pack, own_pack = pl.pallas_call(
+    )(element_slot, jnp.stack([across, side]), pivot_inverse, lower_block, upper_block)
+    outgoing, side_pack, halo_across, halo_side, pivot_inverse, face_blocks = lax.optimization_barrier(
+        (outgoing, side_pack, halo_across, halo_side, pivot_inverse, face_blocks)
+    )
+    across_in = to_across(outgoing)
+    side_in = to_side(side_pack)
+    state_side, state_across = halo_side[:, :width], halo_across[:, :width]
+    slot_side = halo_side[:, width].astype(jnp.int32) + (side - 1) * slot_count
+    slot_across = halo_across[:, width].astype(jnp.int32) + (across - 1) * slot_count
+
+    own_pack = pl.pallas_call(
         functools.partial(staying_kernel, slot_count),
-        out_shape=[
-            jax.ShapeDtypeStruct((bucket,) + pair, bf16),
-            jax.ShapeDtypeStruct((elems,) + pair, bf16),
-        ],
-        in_specs=[SMEM, SMEM, SMEM, ANY, ANY, ANY],
-        out_specs=[ANY, ANY],
+        out_shape=jax.ShapeDtypeStruct((elems,) + pair, bf16),
+        in_specs=[SMEM, SMEM, HBM, HBM, HBM],
+        out_specs=HBM,
         scratch_shapes=[pltpu.VMEM((elems,) + block, bf16)] * 3
         + [pltpu.VMEM((elems,) + pair, bf16), dma((3, elems)), dma((elems,))],
-        compiler_params=pltpu.CompilerParams(vmem_limit_bytes=40 << 20),
+        compiler_params=ROOMY,
+        cost_estimate=SMALL,
         name="staying",
-    )(element_slot, me[None], side[None], pivot_inverse, lower_block, upper_block)
-    side_in = to_side(side_pack)
-
-    owner = element_slot // slot_count
+    )(element_slot, me[None], pivot_inverse, lower_block, upper_block)
+
     side_index, _, side_rank = pack_order(owner == side, bucket)
     across_index, _, across_rank = pack_order(owner == across, bucket)
     send_index = jnp.concatenate([side_index, across_index])
@@ -382,28 +392,27 @@
 
     def face_part(index, parts):
         counts = tuple(part.shape[0] for part in parts)
-        whole = lambda *shape: pl.BlockSpec(shape, lambda e: (0,) * len(shape))
         return pl.pallas_call(
             functools.partial(face_kernel, counts),
-            grid=(elems,),
             out_shape=[
                 jax.ShapeDtypeStruct((bucket, width), f32),
                 jax.ShapeDtypeStruct((bucket, width), f32),
                 jax.ShapeDtypeStruct((elems, width), f32),
             ],
-            in_specs=[SMEM, whole(faces * elems, 1), whole(elems, width)]
-            + [whole(count, width) for count in counts]
-            + [
-                pl.BlockSpec((1, faces, width, width), lambda e: (e, 0, 0, 0)),
-                pl.BlockSpec((1, width, width), lambda e: (e, 0, 0)),
-            ],
-            out_specs=[whole(bucket, width), whole(bucket, width), whole(elems, width)],
+            in_specs=[SMEM, VMEM, VMEM] + [VMEM] * len(parts) + [HBM, HBM],
+            out_specs=[VMEM] * 3,
             scratch_shapes=[
                 pltpu.VMEM((sum(counts), width), bf16),
                 pltpu.VMEM((faces * elems, width), bf16),
+                pltpu.VMEM((elems, width), bf16),
                 pltpu.VMEM((elems, width), f32),
+                pltpu.VMEM((elems, faces) + block, bf16),
+                pltpu.VMEM((elems,) + block, bf16),
+                dma((elems,)),
+                dma((elems,)),
             ],
-            compiler_params=pltpu.CompilerParams(vmem_limit_bytes=40 << 20),
+            compiler_params=FACING,
+            cost_estimate=SMALL,
             name="faces",
         )(send_index, index.reshape(-1, 1), right_side, *parts, face_blocks, pivot_inverse)
 
@@ -414,9 +423,9 @@
         else:
             out_shape = [jax.ShapeDtypeStruct((slot_count, width), bf16)]
         return pl.pallas_call(
-            functools.partial(solve_kernel, last, chunk),
+            functools.partial(solve_kernel, last),
             out_shape=out_shape,
-            in_specs=[SMEM, SMEM, ANY, ANY, ANY, ANY, VMEM, VMEM, VMEM],
+            in_specs=[SMEM, SMEM, HBM, HBM, HBM, VMEM, VMEM, VMEM],
             out_specs=[VMEM] * len(out_shape),
             scratch_shapes=[
                 pltpu.VMEM((slot_count,) + pair, bf16),
@@ -425,9 +434,10 @@
                 pltpu.VMEM((LMAX, 8, width), f32),
                 dma((slot_count,)),
             ],
-            compiler_params=pltpu.CompilerParams(vmem_limit_bytes=40 << 20),
+            compiler_params=SNUG,
+            cost_estimate=SMALL,
             name="solve",
-        )(table, back, side_in, own_pack, first_in, second_in, side_s, own_s, across_s)
+        )(table, back, side_in, own_pack, across_in, side_s, own_s, across_s)
 
     index, parts = near, [state_side, rounded, state_across]
     for sweep in range(SWEEPS):
@@ -469,5 +479,5 @@
         P("dom"),
     )
     return jax.shard_map(
-        functools.partial(body, 2), mesh=mesh, in_specs=placed, out_specs=P("dom", None), check_vma=False
-    )
+        body, mesh=mesh, in_specs=placed, out_specs=P("dom", None), check_vma=False
+    )

time: 190 us -> 148 us (0.78)
  the two profiles are of different devices: /device:TPU:23 before, /device:TPU:7 now
where the time goes in v2:
time: 148 us; the launch traced here: 149 us
  Pallas kernels  55.5 us (38%)
  starting transfers between devices  53.3 us (36%)
  waiting for transfers between devices  26.6 us (18%)
  local copies, waits for them, and re-layouts  7.36 us (5%)
  other arithmetic  5.4 us (4%)
    ppermute x7, starting transfers between devices, to_side(): return lax.ppermute(array, 'dom', side_pairs)  37.7 us
    pallas_call x2, Pallas kernels, face_part(): pl.pallas_call(functools.partial(face_kernel, counts), out_shape=[jax.Sha...  28.3 us
    ppermute x6, waiting for transfers between devices, to_across(): return lax.ppermute(array, 'dom', across_pairs)  24.7 us
    ppermute x6, starting transfers between devices, to_across(): return lax.ppermute(array, 'dom', across_pairs)  15.7 us
    pallas_call x1, Pallas kernels, body(): pl.pallas_call(functools.partial(outgoing_kernel, slot_count), out_shape=...  12.7 us
    pallas_call x2, Pallas kernels, solve(): pl.pallas_call(functools.partial(solve_kernel, last), out_shape=out_shape...  11.2 us
    unnamed x16, local copies, waits for them, and re-layouts  4.97 us
  transfers between devices with their start and end apart: 13, of which 6 were waited for; matrix products, arithmetic and copies ran while one was open for 4% of the time, Pallas kernels for 21%

profile of v2, /device:TPU:7, one launch (start us, length us, event | category | flops | bytes accessed | tf_op | source)
XLA Modules:
  0.0 148.6 jit_solution(16507559651608379265)
XLA Ops:
  0.0 0.7 convert_element_type.36.refs_1_
  0.7 0.7 compare_select_fusion.15
  1.6 0.7 collective-permute-start.1
  2.2 3.0 %collective-permute-start = (bf16[16,384]{1,0:T(8,128)(2,1)S(1)}, bf16[16,384]{1,0:T(8,128)(2,1)S(1)}, u32[]{:S(2)}, u32[]{:S(2)}) collective-permute-start(bf16[16,384]{1,0:T(8,128)(2,1)S(1)} %pad_maximum_fusion), channel_id=1, source_target_pairs={{1,2},{3,4},{5,6},{7,8},{9,10},{11,12},{13,14},{15,16},{17,18},{19... | collective-permute-start | bytes 36872 | tf_op jit(solution)/shard_map/ppermute | solution.py:301
  5.3 0.7 broadcast_maximum_fusion
  6.0 0.1 convert_reduce_fusion.2
  6.1 0.7 pad_add_fusion.targets
  6.8 12.7 %outgoing.1 = (bf16[8,320,640]{2,1,0:T(8,128)(2,1)}, bf16[8,320,640]{2,1,0:T(8,128)(2,1)}) custom-call(s32[16]{0:T(128)} %slots.3, s32[2]{0:T(128)} %pad_add_fusion.targets, bf16[16,320,320]{2,1,0:T(8,128)(2,1)} %refs_5_, bf16[16,320,320]{2,1,0:T(8,128)(2,1)} %low.3, bf16[16,320,320]{2,1,0:T(8,128)(2,1)} %upp.3), custom_call_target="tpu_custom_call" | custom-call | flops 1048576 | bytes 1048576 | tf_op jit(solution)/shard_map/outgoing/pallas_call | solution.py:315
  19.6 1.9 %collective-permute-start.3 = (bf16[8,320,640]{2,1,0:T(8,128)(2,1)}, bf16[8,320,640]{2,1,0:T(8,128)(2,1)}, u32[]{:S(2)}, u32[]{:S(2)}) collective-permute-start(bf16[8,320,640]{2,1,0:T(8,128)(2,1)} %get-tuple-element.28), channel_id=1, source_target_pairs={{1,2},{3,4},{5,6},{7,8},{9,10},{11,12},{13,14},{15,16},{17,18},{19... | collective-permute-start | bytes 9830408 | tf_op jit(solution)/shard_map/ppermute | solution.py:301
  21.5 0.6 broadcast_add_fusion.3
  22.3 0.1 select_reduce_fusion.1
  22.4 0.1 select_reduce_fusion.2
  22.6 0.2 add_reduce_fusion
  22.8 0.2 add_reduce_fusion.1
  23.0 0.1 convert_reduce_fusion.1
  23.1 0.1 select_reduce_fusion.4
  23.3 0.6 gather_fusion
  23.9 0.1 convert_reduce_fusion
  24.0 0.1 select_reduce_fusion.3
  24.2 0.6 gather_fusion.1
  24.8 2.1 %copy-done = bf16[16,320,320]{2,1,0:T(8,128)(2,1)S(1)} copy-done((bf16[16,320,320]{2,1,0:T(8,128)(2,1)S(1)}, bf16[16,320,320]{2,1,0:T(8,128)(2,1)}, u32[]{:S(2)}) %copy-start) | copy-done | bytes 3276824
  26.9 16.2 %faces.2 = (f32[8,320]{1,0:T(8,128)S(1)}, f32[8,320]{1,0:T(8,128)S(1)}, f32[16,320]{1,0:T(8,128)S(1)}) custom-call(s32[16]{0:T(128)S(1)} %pad_add_fusion.2.send, s32[64,1]{1,0:T(8,128)S(1)} %reshape.128.index, f32[16,320]{1,0:T(8,128)S(1)} %copy-done.1, bf16[16,320]{1,0:T(8,128)(2,1)S(1)} %bitcast.14, bf16[16,320]{1,0:T(8,128)(2,1)S(1)} %convert_element_type.36.refs_1_, ...), custom_call_target="tpu_custom_call" | custom-call | flops 1048576 | bytes 1048576 | tf_op jit(solution)/shard_map/faces/pallas_call | solution.py:395
  43.2 0.7 collective-permute-start.4
  43.9 4.8 %collective-permute-start.5 = (f32[8,320]{1,0:T(8,128)S(1)}, f32[8,320]{1,0:T(8,128)S(1)}, u32[]{:S(2)}, u32[]{:S(2)}) collective-permute-start(f32[8,320]{1,0:T(8,128)S(1)} %get-tuple-element.32), channel_id=1, source_target_pairs={{1,2},{3,4},{5,6},{7,8},{9,10},{11,12},{13,14},{15,16},{17,18},{19... | collective-permute-start | bytes 30728 | tf_op jit(solution)/shard_map/ppermute | solution.py:301
  48.7 0.1 fusion.7
  48.8 0.1 fusion.5
  49.0 0.1 select_reduce_fusion.table
  49.2 1.9 %staying.1.own_m = bf16[16,320,640]{2,1,0:T(8,128)(2,1)} custom-call(s32[16]{0:T(128)} %slots.3, s32[1]{0:T(128)} %bitcast.6.me, bf16[16,320,320]{2,1,0:T(8,128)(2,1)} %refs_5_, bf16[16,320,320]{2,1,0:T(8,128)(2,1)} %low.3, bf16[16,320,320]{2,1,0:T(8,128)(2,1)} %upp.3), custom_call_target="tpu_custom_call" | custom-call | flops 1048576 | bytes 1048576 | tf_op jit(solution)/shard_map/staying/pallas_call | solution.py:335
  51.0 10.8 %collective-permute-done.5.across_s = f32[8,320]{1,0:T(8,128)S(1)} collective-permute-done((f32[8,320]{1,0:T(8,128)S(1)}, f32[8,320]{1,0:T(8,128)S(1)}, u32[]{:S(2)}, u32[]{:S(2)}) %collective-permute-start.5) | collective-permute-done | bytes 10272 | tf_op jit(solution)/shard_map/ppermute | solution.py:301
  61.8 1.7 %copy-done.3 = bf16[8,320,640]{2,1,0:T(8,128)(2,1)} copy-done((bf16[8,320,640]{2,1,0:T(8,128)(2,1)}, bf16[8,320,640]{2,1,0:T(8,128)(2,1)S(1)}, u32[]{:S(2)}) %copy-start.3) | copy-done | bytes 3276824
  63.5 5.6 %solve.2.refs_0_ = bf16[32,320]{1,0:T(8,128)(2,1)S(1)} custom-call(s32[32]{0:T(128)S(1)} %select_reduce_fusion.table, s32[32]{0:T(128)S(1)} %get-tuple-element.41.back, bf16[8,320,640]{2,1,0:T(8,128)(2,1)} %copy-done.3, bf16[16,320,640]{2,1,0:T(8,128)(2,1)} %staying.1.own_m, bf16[8,320,640]{2,1,0:T(8,128)(2,1)} %collective-permute-done.3.across_m, ...), custom_call_target="tpu_custom_call" | custom-call | flops 1048576 | bytes 1048576 | tf_op jit(solution)/shard_map/solve/pallas_call | solution.py:425
  69.1 35.2 %collective-permute-start.6 = (bf16[32,320]{1,0:T(8,128)(2,1)S(1)}, bf16[32,320]{1,0:T(8,128)(2,1)S(1)}, u32[]{:S(2)}, u32[]{:S(2)}) collective-permute-start(bf16[32,320]{1,0:T(8,128)(2,1)S(1)} %solve.2.refs_0_), channel_id=1, source_target_pairs={{0,1},{1,0},{2,3},{3,2},{4,5},{5,4},{6,7},{7,6},{8,9},{9,8},{10,11... | collective-permute-start | bytes 61448 | tf_op jit(solution)/shard_map/ppermute | solution.py:298
  104.3 0.8 collective-permute-done.6.refs_1_
  105.2 1.9 %collective-permute-start.7 = (bf16[64,320]{1,0:T(8,128)(2,1)S(1)}, bf16[64,320]{1,0:T(8,128)(2,1)S(1)}, u32[]{:S(2)}, u32[]{:S(2)}) collective-permute-start(bf16[64,320]{1,0:T(8,128)(2,1)S(1)} %maximum_select_fusion), channel_id=1, source_target_pairs={{1,2},{3,4},{5,6},{7,8},{9,10},{11,12},{13,14},{15,16},{17,18},{19... | collective-permute-start | bytes 122888 | tf_op jit(solution)/shard_map/ppermute | solution.py:301
  107.2 0.8 gather_fusion.2
  108.1 4.3 %collective-permute-done.7.refs_2_ = bf16[64,320]{1,0:T(8,128)(2,1)S(1)} collective-permute-done((bf16[64,320]{1,0:T(8,128)(2,1)S(1)}, bf16[64,320]{1,0:T(8,128)(2,1)S(1)}, u32[]{:S(2)}, u32[]{:S(2)}) %collective-permute-start.7) | collective-permute-done | bytes 40992 | tf_op jit(solution)/shard_map/ppermute | solution.py:301
  112.5 1.1 collective-permute-done.8.refs_3_
  113.6 12.1 %faces.3 = (f32[8,320]{1,0:T(8,128)S(1)}, f32[8,320]{1,0:T(8,128)S(1)}, f32[16,320]{1,0:T(8,128)S(1)}) custom-call(s32[16]{0:T(128)S(1)} %pad_add_fusion.2.send, s32[64,1]{1,0:T(8,128)S(1)} %reshape.127.index, f32[16,320]{1,0:T(8,128)S(1)} %copy-done.1, bf16[32,320]{1,0:T(8,128)(2,1)S(1)} %solve.2.refs_0_, ...), custom_call_target="tpu_custom_call" | custom-call | flops 1048576 | bytes 1048576 | tf_op jit(solution)/shard_map/faces/pallas_call | solution.py:395
  125.7 0.2 collective-permute-start.9
  126.0 1.9 %collective-permute-start.10 = (f32[8,320]{1,0:T(8,128)S(1)}, f32[8,320]{1,0:T(8,128)S(1)}, u32[]{:S(2)}, u32[]{:S(2)}) collective-permute-start(f32[8,320]{1,0:T(8,128)S(1)} %get-tuple-element.35), channel_id=1, source_target_pairs={{1,2},{3,4},{5,6},{7,8},{9,10},{11,12},{13,14},{15,16},{17,18},{19... | collective-permute-start | bytes 30728 | tf_op jit(solution)/shard_map/ppermute | solution.py:301
  127.9 4.9 %collective-permute-done.10.across_s = f32[8,320]{1,0:T(8,128)S(1)} collective-permute-done((f32[8,320]{1,0:T(8,128)S(1)}, f32[8,320]{1,0:T(8,128)S(1)}, u32[]{:S(2)}, u32[]{:S(2)}) %collective-permute-start.10) | collective-permute-done | bytes 10272 | tf_op jit(solution)/shard_map/ppermute | solution.py:301
  132.8 5.6 %solve.3 = (f32[8,320]{1,0:T(8,128)S(1)}, f32[16,320]{1,0:T(8,128)S(1)}, f32[8,320]{1,0:T(8,128)S(1)}) custom-call(s32[32]{0:T(128)S(1)} %select_reduce_fusion.table, s32[32]{0:T(128)S(1)} %get-tuple-element.41.back, bf16[8,320,640]{2,1,0:T(8,128)(2,1)} %copy-done.3, bf16[16,320,640]{2,1,0:T(8,128)(2,1)} %staying.1.own_m, ...), custom_call_target="tpu_custom_call" | custom-call | flops 1048576 | bytes 1048576 | tf_op jit(solution)/shard_map/solve/pallas_call | solution.py:425
  138.4 0.6 copy-done.2
  139.0 0.8 collective-permute-start.11
  139.7 2.1 %collective-permute-start.12 = (f32[8,320]{1,0:T(8,128)S(1)}, f32[8,320]{1,0:T(8,128)S(1)}, u32[]{:S(2)}, u32[]{:S(2)}) collective-permute-start(f32[8,320]{1,0:T(8,128)S(1)} %get-tuple-element.38), channel_id=1, source_target_pairs={{1,2},{3,4},{5,6},{7,8},{9,10},{11,12},{13,14},{15,16},{17,18},{19... | collective-permute-start | bytes 30728 | tf_op jit(solution)/shard_map/ppermute | solution.py:301
  141.9 4.7 %collective-permute-done.12.across = f32[8,320]{1,0:T(8,128)S(1)} collective-permute-done((f32[8,320]{1,0:T(8,128)S(1)}, f32[8,320]{1,0:T(8,128)S(1)}, u32[]{:S(2)}, u32[]{:S(2)}) %collective-permute-start.12) | collective-permute-done | bytes 10272 | tf_op jit(solution)/shard_map/ppermute | solution.py:301
  146.6 0.6 copy-done.5
  147.1 1.4 place.1
  (44 shorter events, 1.0 us)
Async XLA Ops:
  1.6 17.9 %collective-permute-start.1 = (bf16[16,384]{1,0:T(8,128)(2,1)S(1)}, bf16[16,384]{1,0:T(8,128)(2,1)S(1)}, u32[]{:S(2)}, u32[]{:S(2)}) collective-permute-start(bf16[16,384]{1,0:T(8,128)(2,1)S(1)} %pad_maximum_fusion), channel_id=1, source_target_pairs={{0,1},{1,0},{2,3},{3,2},{4,5},{5,4},{6,7},{7,6},{8,9},{9,8},{10,11... | collective-permute-start | bytes 36872 | tf_op jit(solution)/shard_map/ppermute | solution.py:298
  2.2 17.3 %collective-permute-start = (bf16[16,384]{1,0:T(8,128)(2,1)S(1)}, bf16[16,384]{1,0:T(8,128)(2,1)S(1)}, u32[]{:S(2)}, u32[]{:S(2)}) collective-permute-start(bf16[16,384]{1,0:T(8,128)(2,1)S(1)} %pad_maximum_fusion), channel_id=1, source_target_pairs={{1,2},{3,4},{5,6},{7,8},{9,10},{11,12},{13,14},{15,16},{17,18},{19... | collective-permute-start | bytes 36872 | tf_op jit(solution)/shard_map/ppermute | solution.py:301
  6.8 18.1 %copy-start.1 = (f32[16,320]{1,0:T(8,128)S(1)}, f32[16,320]{1,0:T(8,128)}, u32[]{:S(2)}) copy-start(f32[16,320]{1,0:T(8,128)} %rhs.5) | copy-start | bytes 61444
  19.5 42.3 %collective-permute-start.2 = (bf16[8,320,640]{2,1,0:T(8,128)(2,1)}, bf16[8,320,640]{2,1,0:T(8,128)(2,1)S(1)}, u32[]{:S(2)}, u32[]{:S(2)}) collective-permute-start(bf16[8,320,640]{2,1,0:T(8,128)(2,1)} %get-tuple-element.26), channel_id=1, source_target_pairs={{0,1},{1,0},{2,3},{3,2},{4,5},{5,4},{6,7},{7,6},{8,9},{9,8},{10,11... | collective-permute-start | bytes 9830408 | tf_op jit(solution)/shard_map/ppermute | solution.py:298
  19.6 42.3 %collective-permute-start.3 = (bf16[8,320,640]{2,1,0:T(8,128)(2,1)}, bf16[8,320,640]{2,1,0:T(8,128)(2,1)}, u32[]{:S(2)}, u32[]{:S(2)}) collective-permute-start(bf16[8,320,640]{2,1,0:T(8,128)(2,1)} %get-tuple-element.28), channel_id=1, source_target_pairs={{1,2},{3,4},{5,6},{7,8},{9,10},{11,12},{13,14},{15,16},{17,18},{19... | collective-permute-start | bytes 9830408 | tf_op jit(solution)/shard_map/ppermute | solution.py:301
  24.8 2.1 %copy-start = (bf16[16,320,320]{2,1,0:T(8,128)(2,1)S(1)}, bf16[16,320,320]{2,1,0:T(8,128)(2,1)}, u32[]{:S(2)}) copy-start(bf16[16,320,320]{2,1,0:T(8,128)(2,1)} %refs_5_) | copy-start | bytes 9830404
  43.2 7.9 %collective-permute-start.4 = (f32[8,320]{1,0:T(8,128)S(1)}, f32[8,320]{1,0:T(8,128)S(1)}, u32[]{:S(2)}, u32[]{:S(2)}) collective-permute-start(f32[8,320]{1,0:T(8,128)S(1)} %get-tuple-element.30), channel_id=1, source_target_pairs={{0,1},{1,0},{2,3},{3,2},{4,5},{5,4},{6,7},{7,6},{8,9},{9,8},{10,11... | collective-permute-start | bytes 30728 | tf_op jit(solution)/shard_map/ppermute | solution.py:298
  43.9 18.0 %collective-permute-start.5 = (f32[8,320]{1,0:T(8,128)S(1)}, f32[8,320]{1,0:T(8,128)S(1)}, u32[]{:S(2)}, u32[]{:S(2)}) collective-permute-start(f32[8,320]{1,0:T(8,128)S(1)} %get-tuple-element.32), channel_id=1, source_target_pairs={{1,2},{3,4},{5,6},{7,8},{9,10},{11,12},{13,14},{15,16},{17,18},{19... | collective-permute-start | bytes 30728 | tf_op jit(solution)/shard_map/ppermute | solution.py:301
  61.8 1.7 %copy-start.3 = (bf16[8,320,640]{2,1,0:T(8,128)(2,1)}, bf16[8,320,640]{2,1,0:T(8,128)(2,1)S(1)}, u32[]{:S(2)}) copy-start(bf16[8,320,640]{2,1,0:T(8,128)(2,1)S(1)} %collective-permute-done.2.side_m) | copy-start | bytes 9830404
  63.5 43.6 %copy-start.6 = (s32[16]{0:T(128)S(1)}, s32[16]{0:T(128)}, u32[]{:S(2)}) copy-start(s32[16]{0:T(128)} %slots.3) | copy-start | bytes 196
  63.5 48.9 %copy-start.7 = (s32[4,16]{1,0:T(4,128)S(1)}, s32[4,16]{1,0:T(4,128)}, u32[]{:S(2)}) copy-start(s32[4,16]{1,0:T(4,128)} %param.14) | copy-start | bytes 772
  69.1 36.1 %collective-permute-start.6 = (bf16[32,320]{1,0:T(8,128)(2,1)S(1)}, bf16[32,320]{1,0:T(8,128)(2,1)S(1)}, u32[]{:S(2)}, u32[]{:S(2)}) collective-permute-start(bf16[32,320]{1,0:T(8,128)(2,1)S(1)} %solve.2.refs_0_), channel_id=1, source_target_pairs={{0,1},{1,0},{2,3},{3,2},{4,5},{5,4},{6,7},{7,6},{8,9},{9,8},{10,11... | collective-permute-start | bytes 61448 | tf_op jit(solution)/shard_map/ppermute | solution.py:298
  105.2 7.2 %collective-permute-start.7 = (bf16[64,320]{1,0:T(8,128)(2,1)S(1)}, bf16[64,320]{1,0:T(8,128)(2,1)S(1)}, u32[]{:S(2)}, u32[]{:S(2)}) collective-permute-start(bf16[64,320]{1,0:T(8,128)(2,1)S(1)} %maximum_select_fusion), channel_id=1, source_target_pairs={{1,2},{3,4},{5,6},{7,8},{9,10},{11,12},{13,14},{15,16},{17,18},{19... | collective-permute-start | bytes 122888 | tf_op jit(solution)/shard_map/ppermute | solution.py:301
  112.4 1.2 collective-permute-start.8
  125.7 2.1 %collective-permute-start.9 = (f32[8,320]{1,0:T(8,128)S(1)}, f32[8,320]{1,0:T(8,128)S(1)}, u32[]{:S(2)}, u32[]{:S(2)}) collective-permute-start(f32[8,320]{1,0:T(8,128)S(1)} %get-tuple-element.33), channel_id=1, source_target_pairs={{0,1},{1,0},{2,3},{3,2},{4,5},{5,4},{6,7},{7,6},{8,9},{9,8},{10,11... | collective-permute-start | bytes 30728 | tf_op jit(solution)/shard_map/ppermute | solution.py:298
  126.0 6.8 %collective-permute-start.10 = (f32[8,320]{1,0:T(8,128)S(1)}, f32[8,320]{1,0:T(8,128)S(1)}, u32[]{:S(2)}, u32[]{:S(2)}) collective-permute-start(f32[8,320]{1,0:T(8,128)S(1)} %get-tuple-element.35), channel_id=1, source_target_pairs={{1,2},{3,4},{5,6},{7,8},{9,10},{11,12},{13,14},{15,16},{17,18},{19... | collective-permute-start | bytes 30728 | tf_op jit(solution)/shard_map/ppermute | solution.py:301
  138.4 0.6 copy-start.2
  139.0 2.9 %collective-permute-start.11 = (f32[8,320]{1,0:T(8,128)S(1)}, f32[8,320]{1,0:T(8,128)S(1)}, u32[]{:S(2)}, u32[]{:S(2)}) collective-permute-start(f32[8,320]{1,0:T(8,128)S(1)} %get-tuple-element.36), channel_id=1, source_target_pairs={{0,1},{1,0},{2,3},{3,2},{4,5},{5,4},{6,7},{7,6},{8,9},{9,8},{10,11... | collective-permute-start | bytes 30728 | tf_op jit(solution)/shard_map/ppermute | solution.py:298
  139.7 6.8 %collective-permute-start.12 = (f32[8,320]{1,0:T(8,128)S(1)}, f32[8,320]{1,0:T(8,128)S(1)}, u32[]{:S(2)}, u32[]{:S(2)}) collective-permute-start(f32[8,320]{1,0:T(8,128)S(1)} %get-tuple-element.38), channel_id=1, source_target_pairs={{1,2},{3,4},{5,6},{7,8},{9,10},{11,12},{13,14},{15,16},{17,18},{19... | collective-permute-start | bytes 30728 | tf_op jit(solution)/shard_map/ppermute | solution.py:301
  141.9 4.7 %copy-start.4 = (f32[8,320]{1,0:T(8,128)}, f32[8,320]{1,0:T(8,128)S(1)}, u32[]{:S(2)}) copy-start(f32[8,320]{1,0:T(8,128)S(1)} %collective-permute-done.11.side) | copy-start | bytes 30724
  146.5 0.6 copy-start.5

commit v3 on v2

--- a/solution.py
+++ b/solution.py
@@ -8,6 +8,8 @@
 from jax.sharding import PartitionSpec as P
 
 LMAX = 8
+FIRST = 4
+SIDES = 4
 SWEEPS = 2
 WIDE = 256
 HBM = pl.BlockSpec(memory_space=pltpu.HBM)
@@ -28,6 +30,24 @@
     return jnp.dot(a, b, preferred_element_type=jnp.float32)
 
 
+def product(block, pivot):
+    return dot_nt(block.T, pivot).astype(jnp.bfloat16)
+
+
+def put(got, out, half):
+    width = got.shape[1]
+    tail = width - WIDE
+    out[:, pl.ds(pl.multiple_of(half * WIDE, WIDE), WIDE)] = got[:, :WIDE]
+
+    @pl.when(half == 0)
+    def _():
+        out[:, 2 * WIDE : 2 * WIDE + tail] = got[:, WIDE:]
+
+    @pl.when(half == 1)
+    def _():
+        out[:, 2 * WIDE + tail :] = got[:, WIDE:]
+
+
 def pair_product(pivot, lower, upper, out):
     both = jnp.concatenate([lower.T, upper.T], axis=0)
     got = dot_nt(both, pivot).astype(jnp.bfloat16)
@@ -37,42 +57,194 @@
     out[:, 2 * WIDE :] = jnp.concatenate([got[:width, WIDE:], got[width:, WIDE:]], axis=1)
 
 
-def outgoing_kernel(slot_count, slots, targets, piv, low, upp, over_out, side_out, pb, lb, ub, stage, insem, outsem):
-    bucket = over_out.shape[0]
-    counts = []
-    for which in range(2):
-        count = jnp.int32(which * bucket)
-        for e in range(slots.shape[0]):
-            hit = (slots[e] // slot_count) == targets[which]
-
-            @pl.when(hit)
-            def _(e=e, count=count):
-                pltpu.make_async_copy(piv.at[e], pb.at[count], insem.at[0, count]).start()
-                pltpu.make_async_copy(low.at[e], lb.at[count], insem.at[1, count]).start()
-                pltpu.make_async_copy(upp.at[e], ub.at[count], insem.at[2, count]).start()
-
-            count = count + hit.astype(jnp.int32)
-        counts.append(count)
-    for which, out in enumerate((over_out, side_out)):
-        first = which * bucket
-
-        def step(k, carry, out=out, first=first):
-            pltpu.make_async_copy(piv.at[0], pb.at[k], insem.at[0, k]).wait()
-            pltpu.make_async_copy(low.at[0], lb.at[k], insem.at[1, k]).wait()
-            pltpu.make_async_copy(upp.at[0], ub.at[k], insem.at[2, k]).wait()
-            pair_product(pb[k], lb[k], ub[k], stage.at[k])
-            pltpu.make_async_copy(stage.at[k], out.at[k - first], outsem.at[k]).start()
-            return carry
-
-        lax.fori_loop(first, counts[which], step, 0)
-    for which, out in enumerate((over_out, side_out)):
-        first = which * bucket
-
-        def drain(k, carry, out=out, first=first):
-            pltpu.make_async_copy(stage.at[k], out.at[k - first], outsem.at[k]).wait()
-            return carry
-
-        lax.fori_loop(first, counts[which], drain, 0)
+def places_taken(slots, owner, slot_count, taken):
+    for e in range(slots.shape[0]):
+        mine = slots[e] // slot_count == owner
+        taken = jnp.where(mine, taken | (jnp.int32(1) << (slots[e] % slot_count)), taken)
+    return taken
+
+
+def is_taken(taken, slot):
+    return ((taken >> slot) & 1) == 1
+
+
+def block_jobs(slot, taken, hit, blind, seen, extra):
+    jobs = []
+    position = slot % LMAX
+    for possible, beside in ((position > 0, slot - 1), (position < LMAX - 1, slot + 1)):
+        possible = hit & possible
+        early = possible & (seen < blind)
+        late = possible & (seen >= blind) & is_taken(taken, jnp.clip(beside, 0, 31))
+        jobs.append((early, late, seen, extra))
+        seen = seen + possible.astype(jnp.int32)
+        extra = extra + late.astype(jnp.int32)
+    return jobs, seen, extra
+
+
+def run_jobs(count, piv, pb, mb, stage, outs, insem, outsem):
+    def pair_copies(at):
+        return [pltpu.make_async_copy(stage.at[at], out, outsem.at[at]) for out in outs]
+
+    def step(m, carry):
+        pltpu.make_async_copy(piv.at[0], pb.at[m], insem.at[0, m]).wait()
+        pltpu.make_async_copy(piv.at[0], mb.at[m], insem.at[1, m]).wait()
+        put(product(mb[m], pb[m]), stage.at[m // 2], m % 2)
+        for j, copy in enumerate(pair_copies(m // 2)):
+
+            @pl.when((m // 2 == j) & ((m % 2 == 1) | (m == count - 1)))
+            def _(copy=copy):
+                copy.start()
+
+        return carry
+
+    lax.fori_loop(0, count, step, 0)
+    for j in range(len(outs)):
+
+        @pl.when(2 * j < count)
+        def _(j=j):
+            pltpu.make_async_copy(stage.at[j], outs[j], outsem.at[j]).wait()
+
+
+def first_kernel(slot_count, slots, across, piv, low, upp, out, pb, mb, stage, insem, outsem):
+    blind = 2 * out.shape[0]
+    seen, extra = jnp.int32(0), jnp.int32(0)
+    for e in range(slots.shape[0]):
+        hit = slots[e] // slot_count == across[0]
+        jobs, seen, extra = block_jobs(slots[e] % slot_count, jnp.int32(0), hit, blind, seen, extra)
+        for (early, _, at, _), source in zip(jobs, (low, upp)):
+
+            @pl.when(early)
+            def _(e=e, at=at, source=source):
+                pltpu.make_async_copy(piv.at[e], pb.at[at], insem.at[0, at]).start()
+                pltpu.make_async_copy(source.at[e], mb.at[at], insem.at[1, at]).start()
+
+    outs = [out.at[j] for j in range(out.shape[0])]
+    run_jobs(jnp.minimum(seen, blind), piv, pb, mb, stage, outs, insem, outsem)
+
+
+def rest_kernel(blind, sides, slot_count, slots, across_slots, far_slots, ids, piv, low, upp, *refs):
+    side_outs, refs = refs[:sides], refs[sides:]
+    outs = refs[: len(refs) - 11]
+    share = side_outs[0].shape[0]
+    pb, mb, stage, insem, outsem, sp, sl, su, side_stage, side_in, side_sem = refs[len(outs) :]
+    across, side = ids[0], ids[1]
+    taken = jnp.int32(0)
+    for array in (slots, across_slots, far_slots):
+        taken = places_taken(array, across, slot_count, taken)
+    seen, extra, beside = jnp.int32(0), jnp.int32(0), jnp.int32(0)
+    for e in range(slots.shape[0]):
+        owner = slots[e] // slot_count
+        jobs, seen, extra = block_jobs(slots[e] % slot_count, taken, owner == across, blind, seen, extra)
+        for (_, late, _, at), source in zip(jobs, (low, upp)):
+
+            @pl.when(late)
+            def _(e=e, at=at, source=source):
+                pltpu.make_async_copy(piv.at[e], pb.at[at], insem.at[0, at]).start()
+                pltpu.make_async_copy(source.at[e], mb.at[at], insem.at[1, at]).start()
+
+    for e in range(slots.shape[0]):
+        hit = slots[e] // slot_count == side
+
+        @pl.when(hit)
+        def _(e=e, beside=beside):
+            pltpu.make_async_copy(piv.at[e], sp.at[beside], side_in.at[0, beside]).start()
+            pltpu.make_async_copy(low.at[e], sl.at[beside], side_in.at[1, beside]).start()
+            pltpu.make_async_copy(upp.at[e], su.at[beside], side_in.at[2, beside]).start()
+
+        beside = beside + hit.astype(jnp.int32)
+    run_jobs(extra, piv, pb, mb, stage, outs, insem, outsem)
+
+    def step(k, carry):
+        pltpu.make_async_copy(piv.at[0], sp.at[k], side_in.at[0, k]).wait()
+        pltpu.make_async_copy(piv.at[0], sl.at[k], side_in.at[1, k]).wait()
+        pltpu.make_async_copy(piv.at[0], su.at[k], side_in.at[2, k]).wait()
+        pair_product(sp[k], sl[k], su[k], side_stage.at[k])
+        for j, side_out in enumerate(side_outs):
+
+            @pl.when(k // share == j)
+            def _(side_out=side_out):
+                pltpu.make_async_copy(side_stage.at[k], side_out.at[k % share], side_sem.at[k]).start()
+
+        return carry
+
+    def drain(k, carry):
+        pltpu.make_async_copy(side_stage.at[k], side_outs[0].at[0], side_sem.at[k]).wait()
+        return carry
+
+    lax.fori_loop(0, beside, step, 0)
+    lax.fori_loop(0, beside, drain, 0)
+
+
+def plan_kernel(blind, slot_count, slots, side_slots, across_slots, far_slots, ids, table, lower_at, upper_at, back, item_of_own, send, counts):
+    across, side, me = ids[0], ids[1], ids[2]
+    elems = slots.shape[0]
+    bucket = elems // 2
+    for k in range(slot_count):
+        table[k] = jnp.int32(-1)
+        lower_at[k] = jnp.int32(-1)
+        upper_at[k] = jnp.int32(-1)
+        back[k] = jnp.int32(0)
+    for k in range(2 * bucket):
+        send[k] = jnp.int32(0)
+    taken, beyond = jnp.int32(0), jnp.int32(0)
+    for array in (slots, side_slots, across_slots):
+        taken = places_taken(array, me, slot_count, taken)
+    for array in (slots, across_slots, far_slots):
+        beyond = places_taken(array, across, slot_count, beyond)
+    beside, over = jnp.int32(0), jnp.int32(0)
+    seen, out_extra = jnp.int32(0), jnp.int32(0)
+    for e in range(elems):
+        owner, slot = slots[e] // slot_count, slots[e] % slot_count
+        own, to_side, to_across = owner == me, owner == side, owner == across
+        item_of_own[e] = jnp.where(own, bucket + e, jnp.where(to_side, beside, bucket + elems + over))
+
+        @pl.when(own)
+        def _(e=e, slot=slot):
+            table[slot] = jnp.int32(bucket + e)
+            lower_at[slot] = jnp.int32(2 * (bucket + e))
+            upper_at[slot] = jnp.int32(2 * (bucket + e) + 1)
+            back[bucket + e] = slot
+
+        @pl.when(to_side)
+        def _(e=e, beside=beside):
+            send[beside] = jnp.int32(e)
+
+        @pl.when(to_across)
+        def _(e=e, over=over):
+            send[bucket + over] = jnp.int32(e)
+
+        _, seen, out_extra = block_jobs(slot, beyond, to_across, blind, seen, out_extra)
+        beside = beside + to_side.astype(jnp.int32)
+        over = over + to_across.astype(jnp.int32)
+    k = jnp.int32(0)
+    for e in range(elems):
+        mine, slot = side_slots[e] // slot_count == me, side_slots[e] % slot_count
+
+        @pl.when(mine)
+        def _(k=k, slot=slot):
+            table[slot] = k
+            lower_at[slot] = 2 * k
+            upper_at[slot] = 2 * k + 1
+            back[k] = slot
+
+        k = k + mine.astype(jnp.int32)
+    k = jnp.int32(bucket + elems)
+    seen, in_extra = jnp.int32(0), jnp.int32(0)
+    for e in range(elems):
+        mine, slot = across_slots[e] // slot_count == me, across_slots[e] % slot_count
+        jobs, seen, in_extra = block_jobs(slot, taken, mine, blind, seen, in_extra)
+
+        @pl.when(mine)
+        def _(k=k, slot=slot, jobs=jobs):
+            table[slot] = k
+            back[k] = slot
+            for (early, late, first, extra), at in zip(jobs, (lower_at, upper_at)):
+                place = jnp.where(early, first, jnp.where(late, blind + extra, jnp.int32(-1)))
+                at[slot] = jnp.where(place >= 0, place + 2 * (bucket + elems), place)
+
+        k = k + mine.astype(jnp.int32)
+    counts[0] = (out_extra + 1) // 2
+    counts[1] = (in_extra + 1) // 2
 
 
 def staying_kernel(slot_count, slots, me, piv, low, upp, own, pb, lb, ub, stage, insem, outsem):
@@ -161,33 +333,42 @@
         across_out[k : k + 1] = scaled[pl.ds(send[bucket + k], 1), :]
 
 
-def solve_kernel(last, table, back, side_m, own_m, across_m, side_s, own_s, across_s, *refs):
+def solve_kernel(last, rests, table, lower_at, upper_at, back, counts, *refs):
+    sides_m, (own_m, first_m), refs = refs[:SIDES], refs[SIDES : SIDES + 2], refs[SIDES + 2 :]
+    rest_m = refs[:rests]
+    side_s, own_s, across_s = refs[rests : rests + 3]
+    refs = refs[rests + 3 :]
     outs = refs[:3] if last else refs[:1]
-    mats, items, ahead, behind, sems = refs[len(outs) :]
+    mats, items, ahead, behind, sems, first_sem, rest_sem = refs[len(outs) :]
     bucket = side_s.shape[0]
     elems = own_s.shape[0]
     width = own_s.shape[1]
     lines = table.shape[0] // LMAX
     tail = width - WIDE
-
-    def load(p, r):
-        slot = r * LMAX + p
-        at = p * lines + r
-        item = table[slot]
-        sources = (
-            (side_m, 0, bucket),
-            (own_m, bucket, bucket + elems),
-            (across_m, bucket + elems, 2 * bucket + elems),
-        )
-        for source, low, high in sources:
-
-            @pl.when((item >= low) & (item < high))
-            def _(source=source, low=low):
-                pltpu.make_async_copy(source.at[item - low], mats.at[at], sems.at[at]).start()
-
+    firsts = first_m.shape[0]
+    base = bucket + elems
+    first_copy = pltpu.make_async_copy(first_m, mats.at[base : base + firsts], first_sem.at[0])
+    first_copy.start()
+    rest_copies = [
+        pltpu.make_async_copy(rest, mats.at[base + firsts + j], rest_sem.at[j]) for j, rest in enumerate(rest_m)
+    ]
+    for j, copy in enumerate(rest_copies):
+
+        @pl.when(j < counts[1])
+        def _(copy=copy):
+            copy.start()
+
+    share = bucket // SIDES
+    sources = [(side_m, j * share, (j + 1) * share) for j, side_m in enumerate(sides_m)] + [(own_m, bucket, base)]
     for p in range(LMAX):
         for r in range(lines):
-            load(p, r)
+            item = table[r * LMAX + p]
+            for source, low, high in sources:
+
+                @pl.when((item >= low) & (item < high))
+                def _(source=source, low=low, item=item, p=p, r=r):
+                    sem = sems.at[p * lines + r]
+                    pltpu.make_async_copy(source.at[item - low], mats.at[item], sem).start()
 
     items[:bucket] = side_s[...]
     items[bucket : bucket + elems] = own_s[...]
@@ -195,14 +376,16 @@
     sublanes = ahead.shape[1]
     row = lax.broadcasted_iota(jnp.int32, (sublanes, width), 0)
 
-    def sweep_step(p, x, half):
+    def sweep_step(p, x, places):
         carried = jnp.zeros((sublanes, width), jnp.float32)
         for r in range(lines):
-            at = p * lines + r
-            lead = dot_nn(x, mats[at, :, half * WIDE : (half + 1) * WIDE])
-            ending = dot_nn(x, mats[at, :, 2 * WIDE :])[:, half * tail : (half + 1) * tail]
-            live = table[r * LMAX + p] >= 0
-            carried = jnp.where((row == r) & live, jnp.concatenate([lead, ending], axis=1), carried)
+            place = places[r * LMAX + p]
+            at = jnp.maximum(place, 0)
+            unit, half = at // 2, at % 2
+            lead = dot_nn(x, mats[unit, :, pl.ds(pl.multiple_of(half * WIDE, WIDE), WIDE)])
+            ending = dot_nn(x, mats[unit, :, 2 * WIDE :])
+            ending = jnp.where(half == 0, ending[:, :tail], ending[:, tail:])
+            carried = jnp.where((row == r) & (place >= 0), jnp.concatenate([lead, ending], axis=1), carried)
         return carried
 
     for p in range(LMAX):
@@ -218,21 +401,30 @@
     for p in range(LMAX):
         for r in range(lines):
 
-            @pl.when(table[r * LMAX + p] >= 0)
-            def _(p=p, r=r):
-                at = p * lines + r
-                pltpu.make_async_copy(own_m.at[0], mats.at[at], sems.at[at]).wait()
+            item = table[r * LMAX + p]
+
+            @pl.when((item >= 0) & (item < base))
+            def _(p=p, r=r, item=item):
+                pltpu.make_async_copy(own_m.at[0], mats.at[item], sems.at[p * lines + r]).wait()
+
+        if p == 1:
+            first_copy.wait()
+            for j, copy in enumerate(rest_copies):
+
+                @pl.when(j < counts[1])
+                def _(copy=copy):
+                    copy.wait()
 
         value = ahead[p]
         if p > 0:
-            value = value - sweep_step(p, x, 0)
+            value = value - sweep_step(p, x, lower_at)
             ahead[p] = value
         x = value.astype(jnp.bfloat16)
     x = None
     for p in reversed(range(LMAX)):
         value = ahead[p]
         if p < LMAX - 1:
-            value = value - sweep_step(p, x, 1)
+            value = value - sweep_step(p, x, upper_at)
         behind[p] = value
         x = value.astype(jnp.bfloat16)
     if last:
@@ -257,16 +449,6 @@
     items[bucket + elems :] = across[...]
     for e in range(elems):
         out[e : e + 1] = items[pl.ds(index[e], 1), :]
-
-
-def pack_order(selected, bucket):
-    members = jnp.arange(selected.shape[0], dtype=jnp.int32)
-    before = (members[None, :] <= members[:, None]) & selected[None, :]
-    ordering = jnp.sum(before.astype(jnp.int32), axis=1) - 1
-    positions = jnp.arange(bucket, dtype=jnp.int32)[:, None]
-    matches = selected[None, :] & (ordering[None, :] == positions)
-    picked = jnp.sum(jnp.where(matches, members[None, :], 0), axis=1)
-    return (picked, jnp.any(matches, axis=1), jnp.clip(ordering, 0, bucket - 1))
 
 
 def body(
@@ -291,8 +473,9 @@
     side = jnp.where(odd, me - 1, me + 1)
     across = jnp.where(odd, me + 1, me - 1)
     side_pairs = [(i, i ^ 1) for i in range(devices)]
-    across_pairs = [(i, i + 1) for i in range(1, devices - 1, 2)]
-    across_pairs = across_pairs + [(j, i) for i, j in across_pairs]
+    up_pairs = [(i, i + 1) for i in range(1, devices - 1, 2)]
+    down_pairs = [(j, i) for i, j in up_pairs]
+    across_pairs = up_pairs + down_pairs
 
     def to_side(array):
         return lax.ppermute(array, "dom", side_pairs)
@@ -305,32 +488,72 @@
     pair = (width, packed)
     dma = pltpu.SemaphoreType.DMA
 
+    firsts, rests = FIRST, bucket - FIRST
+    blind = 2 * firsts
+    ids = jnp.stack([across, side, me])
     rounded = start_state.astype(bf16)
-    owner = element_slot // slot_count
     code = (element_slot - (me - 1) * slot_count).astype(bf16)
-    column = lax.broadcasted_iota(jnp.int32, (elems, 128), 1)
-    halo = jnp.concatenate([rounded, jnp.where(column == 0, code[:, None], jnp.zeros((), bf16))[:, : 384 - width]], axis=1)
-    halo_across = to_across(halo)
-    halo_side = to_side(halo)
-    outgoing, side_pack = pl.pallas_call(
-        functools.partial(outgoing_kernel, slot_count),
-        out_shape=[jax.ShapeDtypeStruct((bucket,) + pair, bf16)] * 2,
+    room = -width % 128
+    column = lax.broadcasted_iota(jnp.int32, (elems, room), 1)
+
+    def framed(first_code, second_code):
+        extra = jnp.where(column == 0, first_code[:, None], second_code[:, None])
+        return jnp.concatenate([rounded, extra], axis=1)
+
+    halo_side = to_side(framed(code, code))
+    halo_across = to_across(framed(code, halo_side[:, width]))
+    across_live = (across >= 0) & (across < devices)
+    nowhere = devices * slot_count
+    across_mate = across ^ 1
+
+    def slots_of(codes, home, live):
+        return jnp.where(live, codes.astype(jnp.int32) + (home - 1) * slot_count, nowhere)
+
+    first = pl.pallas_call(
+        functools.partial(first_kernel, slot_count),
+        out_shape=jax.ShapeDtypeStruct((firsts,) + pair, bf16),
         in_specs=[SMEM, SMEM, HBM, HBM, HBM],
-        out_specs=[HBM, HBM],
-        scratch_shapes=[pltpu.VMEM((2 * bucket,) + block, bf16)] * 3
-        + [pltpu.VMEM((2 * bucket,) + pair, bf16), dma((3, 2 * bucket)), dma((2 * bucket,))],
+        out_specs=HBM,
+        scratch_shapes=[pltpu.VMEM((blind,) + block, bf16)] * 2
+        + [pltpu.VMEM((firsts,) + pair, bf16), dma((2, blind)), dma((firsts,))],
         compiler_params=ROOMY,
         cost_estimate=SMALL,
-        name="outgoing",
-    )(element_slot, jnp.stack([across, side]), pivot_inverse, lower_block, upper_block)
-    outgoing, side_pack, halo_across, halo_side, pivot_inverse, face_blocks = lax.optimization_barrier(
-        (outgoing, side_pack, halo_across, halo_side, pivot_inverse, face_blocks)
+        name="first",
+    )(element_slot, across[None], pivot_inverse, lower_block, upper_block)
+    first, halo_across, halo_side, pivot_inverse, face_blocks = lax.optimization_barrier(
+        (first, halo_across, halo_side, pivot_inverse, face_blocks)
     )
-    across_in = to_across(outgoing)
-    side_in = to_side(side_pack)
+    first_in = to_across(first)
     state_side, state_across = halo_side[:, :width], halo_across[:, :width]
-    slot_side = halo_side[:, width].astype(jnp.int32) + (side - 1) * slot_count
-    slot_across = halo_across[:, width].astype(jnp.int32) + (across - 1) * slot_count
+    slot_side = slots_of(halo_side[:, width], side, True)
+    slot_across = slots_of(halo_across[:, width], across, across_live)
+    slot_far = slots_of(halo_across[:, width + 1], across_mate, across_live)
+    made = pl.pallas_call(
+        functools.partial(rest_kernel, blind, SIDES, slot_count),
+        out_shape=[jax.ShapeDtypeStruct((bucket // SIDES,) + pair, bf16)] * SIDES
+        + [jax.ShapeDtypeStruct(pair, bf16)] * rests,
+        in_specs=[SMEM] * 4 + [HBM] * 3,
+        out_specs=[HBM] * (SIDES + rests),
+        scratch_shapes=[pltpu.VMEM((2 * rests,) + block, bf16)] * 2
+        + [pltpu.VMEM((rests,) + pair, bf16), dma((2, 2 * rests)), dma((rests,))]
+        + [pltpu.VMEM((bucket,) + block, bf16)] * 3
+        + [pltpu.VMEM((bucket,) + pair, bf16), dma((3, bucket)), dma((bucket,))],
+        compiler_params=ROOMY,
+        cost_estimate=SMALL,
+        name="rest",
+    )(element_slot, slot_across, slot_far, ids, pivot_inverse, lower_block, upper_block)
+    rest = made[SIDES:]
+    side_in = tuple(to_side(part) for part in made[:SIDES])
+    whole = jax.ShapeDtypeStruct((slot_count,), jnp.int32)
+    some = jax.ShapeDtypeStruct((elems,), jnp.int32)
+    table, lower_at, upper_at, back, item_of_own, send_index, counts = pl.pallas_call(
+        functools.partial(plan_kernel, blind, slot_count),
+        out_shape=[whole] * 4 + [some] * 2 + [jax.ShapeDtypeStruct((2,), jnp.int32)],
+        in_specs=[SMEM] * 5,
+        out_specs=[SMEM] * 7,
+        cost_estimate=SMALL,
+        name="plan",
+    )(element_slot, slot_side, slot_across, slot_far, ids)
 
     own_pack = pl.pallas_call(
         functools.partial(staying_kernel, slot_count),
@@ -343,30 +566,6 @@
         cost_estimate=SMALL,
         name="staying",
     )(element_slot, me[None], pivot_inverse, lower_block, upper_block)
-
-    side_index, _, side_rank = pack_order(owner == side, bucket)
-    across_index, _, across_rank = pack_order(owner == across, bucket)
-    send_index = jnp.concatenate([side_index, across_index])
-    spread = jnp.arange(elems, dtype=jnp.int32)
-    item_of_own = jnp.where(
-        owner == me,
-        bucket + spread,
-        jnp.where(owner == side, side_rank, bucket + elems + across_rank),
-    )
-    across_live = (across >= 0) & (across < devices)
-    in_side, in_side_valid, _ = pack_order(slot_side // slot_count == me, bucket)
-    in_across, in_across_valid, _ = pack_order((slot_across // slot_count == me) & across_live, bucket)
-    item_slot = jnp.concatenate(
-        [
-            jnp.where(in_side_valid, slot_side[in_side] % slot_count, -1),
-            jnp.where(owner == me, element_slot % slot_count, -1),
-            jnp.where(in_across_valid, slot_across[in_across] % slot_count, -1),
-        ]
-    )
-    everything = jnp.arange(slot_count, dtype=jnp.int32)
-    slot_matches = item_slot[None, :] == everything[:, None]
-    table = jnp.max(jnp.where(slot_matches, everything[None, :], -1), axis=1)
-    back = jnp.maximum(item_slot, 0)
 
     home = neighbours // elems
     within = neighbours % elems
@@ -416,16 +615,16 @@
             name="faces",
         )(send_index, index.reshape(-1, 1), right_side, *parts, face_blocks, pivot_inverse)
 
-    def solve(last, side_s, own_s, across_s):
+    def solve(last, blocks, side_s, own_s, across_s):
         if last:
             shapes = [(bucket, width), (elems, width), (bucket, width)]
             out_shape = [jax.ShapeDtypeStruct(shape, f32) for shape in shapes]
         else:
             out_shape = [jax.ShapeDtypeStruct((slot_count, width), bf16)]
         return pl.pallas_call(
-            functools.partial(solve_kernel, last),
+            functools.partial(solve_kernel, last, rests),
             out_shape=out_shape,
-            in_specs=[SMEM, SMEM, HBM, HBM, HBM, VMEM, VMEM, VMEM],
+            in_specs=[SMEM] * 5 + [HBM] * (SIDES + 2 + rests) + [VMEM] * 3,
             out_specs=[VMEM] * len(out_shape),
             scratch_shapes=[
                 pltpu.VMEM((slot_count,) + pair, bf16),
@@ -433,18 +632,41 @@
                 pltpu.VMEM((LMAX, 8, width), f32),
                 pltpu.VMEM((LMAX, 8, width), f32),
                 dma((slot_count,)),
+                dma((1,)),
+                dma((rests,)),
             ],
             compiler_params=SNUG,
             cost_estimate=SMALL,
             name="solve",
-        )(table, back, side_in, own_pack, across_in, side_s, own_s, across_s)
-
+        )(table, lower_at, upper_at, back, counts, *blocks, side_s, own_s, across_s)
+
+    def exchange(going, coming, *arrays):
+        *blocks, vectors = arrays
+        got = []
+        for j, block in enumerate(blocks):
+            pairs = (up_pairs if j < going else []) + (down_pairs if j < coming else [])
+            got.append(lax.ppermute(block, "dom", pairs) if pairs else jnp.zeros_like(block))
+        return (*got, to_across(vectors))
+
+    exchanges = [
+        functools.partial(exchange, going, coming) for going in range(rests + 1) for coming in range(rests + 1)
+    ]
     index, parts = near, [state_side, rounded, state_across]
     for sweep in range(SWEEPS):
         scaled_side, scaled_across, scaled_own = face_part(index, parts)
-        got_across = to_across(scaled_across)
         got_side = to_side(scaled_side)
-        solved = solve(sweep == SWEEPS - 1, got_side, scaled_own, got_across)
+        if sweep == 0:
+            rest, scaled_across, counts, own_pack, first_in, side_in, got_side = lax.optimization_barrier(
+                (tuple(rest), scaled_across, counts, own_pack, first_in, side_in, got_side)
+            )
+            going = jnp.where(odd, counts[0], counts[1])
+            coming = jnp.where(odd, counts[1], counts[0])
+            branch = going * (rests + 1) + coming
+            *rest_in, got_across = lax.switch(branch, exchanges, *rest, scaled_across)
+        else:
+            got_across = to_across(scaled_across)
+        blocks = (*side_in, own_pack, first_in, *rest_in)
+        solved = solve(sweep == SWEEPS - 1, blocks, got_side, scaled_own, got_across)
         if sweep < SWEEPS - 1:
             (mine,) = solved
             beside = to_side(mine)

time: 148 us -> 142 us (0.959)
  the two profiles are of different devices: /device:TPU:7 before, /device:TPU:28 now
where the time goes in v3:
time: 142 us; the launch traced here: 140 us
  Pallas kernels  64.4 us (45%)
  starting transfers between devices  37.7 us (27%)
  waiting for transfers between devices  25.2 us (18%)
  local copies, waits for them, and re-layouts  6.86 us (5%)
  other arithmetic  3.12 us (2%)
  between operations  2.94 us (2%)
    pallas_call x2, Pallas kernels, face_part(): pl.pallas_call(functools.partial(face_kernel, counts), out_shape=[jax.Sha...  28.3 us
    ppermute x6, starting transfers between devices, to_across(): return lax.ppermute(array, 'dom', across_pairs)  23.1 us
    ppermute x6, waiting for transfers between devices, to_across(): return lax.ppermute(array, 'dom', across_pairs)  21.8 us
    pallas_call x2, Pallas kernels, solve(): pl.pallas_call(functools.partial(solve_kernel, last, rests), out_shape=ou...  15.6 us
    pallas_call x1, Pallas kernels, body(): pl.pallas_call(functools.partial(staying_kernel, slot_count), out_shape=j...  12.9 us
    ppermute x10, starting transfers between devices, to_side(): return lax.ppermute(array, 'dom', side_pairs)  10.7 us
    unnamed x34, local copies, waits for them, and re-layouts  3.98 us
    ppermute x3, starting transfers between devices, exchange(): lax.ppermute(block, 'dom', pairs)  3.88 us
  transfers between devices with their start and end apart: 19, of which 8 were waited for; matrix products, arithmetic and copies ran while one was open for 2% of the time, Pallas kernels for 25%

profile of v3, /device:TPU:28, one launch (start us, length us, event | category | flops | bytes accessed | tf_op | source)
XLA Modules:
  0.0 140.3 jit_solution(14561729366575591233)
XLA Ops:
  0.0 0.7 convert_element_type.18.refs_1_
  0.7 0.7 subtract_convert_fusion
  1.5 0.1 pad_maximum_fusion
  1.6 1.2 collective-permute-done.95
  2.7 0.2 slice_reduce_fusion
  3.0 0.1 pad_maximum_fusion.1
  3.1 3.1 %collective-permute-start.96 = (bf16[16,384]{1,0:T(8,128)(2,1)S(1)}, bf16[16,384]{1,0:T(8,128)(2,1)S(1)}, u32[]{:S(2)}, u32[]{:S(2)}) collective-permute-start(bf16[16,384]{1,0:T(8,128)(2,1)S(1)} %pad_maximum_fusion.1), channel_id=1, source_target_pairs={{1,2},{3,4},{5,6},{7,8},{9,10},{11,12},{13,14},{15,16},{17,18},{19... | collective-permute-start | bytes 36872 | tf_op jit(solution)/shard_map/ppermute | solution.py:484
  6.2 1.3 first.1
  7.5 1.5 %collective-permute-done.96 = bf16[16,384]{1,0:T(8,128)(2,1)S(1)} collective-permute-done((bf16[16,384]{1,0:T(8,128)(2,1)S(1)}, bf16[16,384]{1,0:T(8,128)(2,1)S(1)}, u32[]{:S(2)}, u32[]{:S(2)}) %collective-permute-start.96) | collective-permute-done | bytes 12320 | tf_op jit(solution)/shard_map/ppermute | solution.py:484
  9.0 6.8 %collective-permute-start.97 = (bf16[4,320,640]{2,1,0:T(8,128)(2,1)}, bf16[4,320,640]{2,1,0:T(8,128)(2,1)S(1)}, u32[]{:S(2)}, u32[]{:S(2)}) collective-permute-start(bf16[4,320,640]{2,1,0:T(8,128)(2,1)} %first.1), channel_id=1, source_target_pairs={{1,2},{3,4},{5,6},{7,8},{9,10},{11,12},{13,14},{15,16},{17,18},{19... | collective-permute-start | bytes 4915208 | tf_op jit(solution)/shard_map/ppermute | solution.py:484
  15.9 0.1 reshape.34.index
  16.0 0.6 pad_add_fusion.ids
  16.5 0.8 select_reduce_fusion
  17.3 2.9 %plan.1 = (s32[32]{0:T(128)}, s32[32]{0:T(128)}, s32[32]{0:T(128)}, s32[32]{0:T(128)}, s32[16]{0:T(128)}, /*index=5*/s32[16]{0:T(128)}, s32[2]{0:T(128)}) custom-call(s32[16]{0:T(128)} %slots.7, s32[16]{0:T(128)} %get-tuple-element.388.side_slots, s32[16]{0:T(128)} %get-tuple-element.383.across_slots, s32[16]{0:T(128)} %get-tuple-element.382.far_slots, ...), custom_call_target="tpu_custom_call" | custom-call | flops 1048576 | bytes 1048576 | tf_op jit(solution)/shard_map/plan/pallas_call | solution.py:549
  20.2 2.1 %copy-done = bf16[16,320,320]{2,1,0:T(8,128)(2,1)S(1)} copy-done((bf16[16,320,320]{2,1,0:T(8,128)(2,1)S(1)}, bf16[16,320,320]{2,1,0:T(8,128)(2,1)}, u32[]{:S(2)}) %copy-start) | copy-done | bytes 3276824
  22.3 0.6 copy-done.4
  22.9 16.2 %faces.2 = (f32[8,320]{1,0:T(8,128)S(1)}, f32[8,320]{1,0:T(8,128)S(1)}, f32[16,320]{1,0:T(8,128)S(1)}) custom-call(s32[16]{0:T(128)S(1)} %copy-done.4, s32[64,1]{1,0:T(8,128)S(1)} %reshape.34.index, f32[16,320]{1,0:T(8,128)S(1)} %copy-done.1, bf16[16,320]{1,0:T(8,128)(2,1)S(1)} %bitcast.8, bf16[16,320]{1,0:T(8,128)(2,1)S(1)} %convert_element_type.18.refs_1_, ...), custom_call_target="tpu_custom_call" | custom-call | flops 1048576 | bytes 1048576 | tf_op jit(solution)/shard_map/faces/pallas_call | solution.py:594
  39.2 2.0 %rest.1 = (bf16[2,320,640]{2,1,0:T(8,128)(2,1)}, bf16[2,320,640]{2,1,0:T(8,128)(2,1)}, bf16[2,320,640]{2,1,0:T(8,128)(2,1)}, bf16[2,320,640]{2,1,0:T(8,128)(2,1)...) custom-call(s32[16]{0:T(128)} %slots.7, ...), custom_call_target="tpu_custom_call" | custom-call | flops 1048576 | bytes 1048576 | tf_op jit(solution)/shard_map/rest/pallas_call | solution.py:531
  41.2 9.8 %collective-permute-start.98 = (bf16[2,320,640]{2,1,0:T(8,128)(2,1)}, bf16[2,320,640]{2,1,0:T(8,128)(2,1)S(1)}, u32[]{:S(2)}, u32[]{:S(2)}) collective-permute-start(bf16[2,320,640]{2,1,0:T(8,128)(2,1)} %get-tuple-element.352), channel_id=1, source_target_pairs={{0,1},{1,0},{2,3},{3,2},{4,5},{5,4},{6,7},{7,6},{8,9},{9,8},{10,11... | collective-permute-start | bytes 2457608 | tf_op jit(solution)/shard_map/ppermute | solution.py:481
  51.0 0.4 collective-permute-start.100
  51.5 0.1 reshape.26
  51.6 12.9 %staying.1.refs_4_ = bf16[16,320,640]{2,1,0:T(8,128)(2,1)} custom-call(s32[16]{0:T(128)} %slots.7, s32[1]{0:T(128)} %bitcast.2.me, bf16[16,320,320]{2,1,0:T(8,128)(2,1)} %refs_5_, bf16[16,320,320]{2,1,0:T(8,128)(2,1)} %low.5, bf16[16,320,320]{2,1,0:T(8,128)(2,1)} %upp.5), custom_call_target="tpu_custom_call" | custom-call | flops 1048576 | bytes 1048576 | tf_op jit(solution)/shard_map/staying/pallas_call | solution.py:558
  64.6 0.7 fusion.18
  67.8 21.2 %conditional.1 = (bf16[320,640]{1,0:T(8,128)(2,1)}, bf16[320,640]{1,0:T(8,128)(2,1)}, bf16[320,640]{1,0:T(8,128)(2,1)}, bf16[320,640]{1,0:T(8,128)(2,1)}, f32[8,320]{1,0:T(8,128)}) conditional(s32[]{:T(128)} %clamp.3, f32[8,320]{1,0:T(8,128)S(1)} %get-tuple-element.364, (bf16[320,640]{1,0:T(8,128)(2,1)}, ...), branch_computations={%region_0.1_spmd, %region_1.2_spmd, %region_2.3_spmd, %region_3.4_... | conditional | bytes 6594800 | solution.py:665
  67.8 1.3 collective-permute-start.49
  69.1 1.3 collective-permute-start.50
  70.4 1.3 collective-permute-start.51
  71.7 7.4 %collective-permute-start.52 = (f32[8,320]{1,0:T(8,128)S(1)}, f32[8,320]{1,0:T(8,128)}, u32[]{:S(2)}, u32[]{:S(2)}) collective-permute-start(f32[8,320]{1,0:T(8,128)S(1)} %get-tuple-element.245), channel_id=1, source_target_pairs={{1,2},{3,4},{5,6},{7,8},{9,10},{11,12},{13,14},{15,16},{17,18},{19... | collective-permute-start | bytes 30728 | tf_op jit(solution)/shard_map/cond/branch_15_fun/ppermute | solution.py:484
  79.2 8.9 %collective-permute-done.52 = f32[8,320]{1,0:T(8,128)} collective-permute-done((f32[8,320]{1,0:T(8,128)S(1)}, f32[8,320]{1,0:T(8,128)}, u32[]{:S(2)}, u32[]{:S(2)}) %collective-permute-start.52) | collective-permute-done | bytes 10272 | tf_op jit(solution)/shard_map/cond/branch_15_fun/ppermute | solution.py:484
  88.1 0.8 broadcast.100
  89.0 7.9 %solve.2.refs_0_ = bf16[32,320]{1,0:T(8,128)(2,1)S(1)} custom-call(s32[32]{0:T(128)S(1)} %copy-done.6, s32[32]{0:T(128)S(1)} %copy-done.7, s32[32]{0:T(128)S(1)} %copy-done.8, s32[32]{0:T(128)S(1)} %copy-done.9, s32[2]{0:T(128)S(1)} %copy-done.3, bf16[2,320,640]{2,1,0:T(8,128)(2,1)S(1)} %collective-permute-done.98.refs_0_, ...), custom_call_target="tpu_custom_call" | custom-call | flops 1048576 | bytes 1048576 | tf_op jit(solution)/shard_map/solve/pallas_call | solution.py:624
  97.0 1.1 collective-permute-done.103.refs_1_
  98.2 1.9 %collective-permute-start.104 = (bf16[64,320]{1,0:T(8,128)(2,1)S(1)}, bf16[64,320]{1,0:T(8,128)(2,1)S(1)}, u32[]{:S(2)}, u32[]{:S(2)}) collective-permute-start(bf16[64,320]{1,0:T(8,128)(2,1)S(1)} %maximum_select_fusion), channel_id=1, source_target_pairs={{1,2},{3,4},{5,6},{7,8},{9,10},{11,12},{13,14},{15,16},{17,18},{19... | collective-permute-start | bytes 122888 | tf_op jit(solution)/shard_map/ppermute | solution.py:484
  100.2 0.8 gather_fusion
  101.0 0.1 reshape.25
  101.1 3.4 %collective-permute-done.104.refs_2_ = bf16[64,320]{1,0:T(8,128)(2,1)S(1)} collective-permute-done((bf16[64,320]{1,0:T(8,128)(2,1)S(1)}, bf16[64,320]{1,0:T(8,128)(2,1)S(1)}, u32[]{:S(2)}, u32[]{:S(2)}) %collective-permute-start.104) | collective-permute-done | bytes 40992 | tf_op jit(solution)/shard_map/ppermute | solution.py:484
  104.5 0.1 reshape.35.index
  104.6 1.1 collective-permute-done.105.refs_3_
  105.7 12.1 %faces.3 = (f32[8,320]{1,0:T(8,128)S(1)}, f32[8,320]{1,0:T(8,128)S(1)}, f32[16,320]{1,0:T(8,128)S(1)}) custom-call(s32[16]{0:T(128)S(1)} %copy-done.5, s32[64,1]{1,0:T(8,128)S(1)} %reshape.35.index, f32[16,320]{1,0:T(8,128)S(1)} %copy-done.1, bf16[32,320]{1,0:T(8,128)(2,1)S(1)} %solve.2.refs_0_, bf16[32,320]{1,0:T(8,128)(2,1)S(1)} %collective-permute-done.103.refs_1_, ...), custom_call_target="tpu_custom_call" | custom-call | flops 1048576 | bytes 1048576 | tf_op jit(solution)/shard_map/faces/pallas_call | solution.py:594
  117.8 0.2 collective-permute-start.106
  118.1 1.9 %collective-permute-start.107 = (f32[8,320]{1,0:T(8,128)S(1)}, f32[8,320]{1,0:T(8,128)S(1)}, u32[]{:S(2)}, u32[]{:S(2)}) collective-permute-start(f32[8,320]{1,0:T(8,128)S(1)} %get-tuple-element.378), channel_id=1, source_target_pairs={{1,2},{3,4},{5,6},{7,8},{9,10},{11,12},{13,14},{15,16},{17,18},{19... | collective-permute-start | bytes 30728 | tf_op jit(solution)/shard_map/ppermute | solution.py:484
  120.0 4.0 %collective-permute-done.107.refs_12_ = f32[8,320]{1,0:T(8,128)S(1)} collective-permute-done((f32[8,320]{1,0:T(8,128)S(1)}, f32[8,320]{1,0:T(8,128)S(1)}, u32[]{:S(2)}, u32[]{:S(2)}) %collective-permute-start.107) | collective-permute-done | bytes 10272 | tf_op jit(solution)/shard_map/ppermute | solution.py:484
  124.0 7.7 %solve.3 = (f32[8,320]{1,0:T(8,128)S(1)}, f32[16,320]{1,0:T(8,128)S(1)}, f32[8,320]{1,0:T(8,128)S(1)}) custom-call(s32[32]{0:T(128)S(1)} %copy-done.6, s32[32]{0:T(128)S(1)} %copy-done.7, s32[32]{0:T(128)S(1)} %copy-done.8, s32[32]{0:T(128)S(1)} %copy-done.9, s32[2]{0:T(128)S(1)} %copy-done.3, bf16[2,320,640]{2,1,0:T(8,128)(2,1)S(1)} %collective-permute-done.98.refs_0_, ...), custom_call_target="tpu_custom_call" | custom-call | flops 1048576 | bytes 1048576 | tf_op jit(solution)/shard_map/solve/pallas_call | solution.py:624
  131.7 0.6 copy-done.2
  132.3 1.9 %collective-permute-start.109 = (f32[8,320]{1,0:T(8,128)S(1)}, f32[8,320]{1,0:T(8,128)S(1)}, u32[]{:S(2)}, u32[]{:S(2)}) collective-permute-start(f32[8,320]{1,0:T(8,128)S(1)} %get-tuple-element.381), channel_id=1, source_target_pairs={{1,2},{3,4},{5,6},{7,8},{9,10},{11,12},{13,14},{15,16},{17,18},{19... | collective-permute-start | bytes 30728 | tf_op jit(solution)/shard_map/ppermute | solution.py:484
  134.3 4.0 %collective-permute-done.109.across = f32[8,320]{1,0:T(8,128)S(1)} collective-permute-done((f32[8,320]{1,0:T(8,128)S(1)}, f32[8,320]{1,0:T(8,128)S(1)}, u32[]{:S(2)}, u32[]{:S(2)}) %collective-permute-start.109) | collective-permute-done | bytes 10272 | tf_op jit(solution)/shard_map/ppermute | solution.py:484
  138.2 0.6 copy-done.12
  138.8 1.4 %place.1 = f32[16,320]{1,0:T(8,128)} custom-call(s32[16]{0:T(128)} %get-tuple-element.337.index, f32[8,320]{1,0:T(8,128)} %copy-done.11, f32[16,320]{1,0:T(8,128)} %copy-done.2, f32[8,320]{1,0:T(8,128)} %copy-done.12), custom_call_target="tpu_custom_call" | custom-call | tf_op jit(solution)/shard_map/place/pallas_call | solution.py:682
  (56 shorter events, 0.7 us)
Async XLA Ops:
  1.6 1.2 collective-permute-start.95
  3.1 5.9 %collective-permute-start.96 = (bf16[16,384]{1,0:T(8,128)(2,1)S(1)}, bf16[16,384]{1,0:T(8,128)(2,1)S(1)}, u32[]{:S(2)}, u32[]{:S(2)}) collective-permute-start(bf16[16,384]{1,0:T(8,128)(2,1)S(1)} %pad_maximum_fusion.1), channel_id=1, source_target_pairs={{1,2},{3,4},{5,6},{7,8},{9,10},{11,12},{13,14},{15,16},{17,18},{19... | collective-permute-start | bytes 36872 | tf_op jit(solution)/shard_map/ppermute | solution.py:484
  6.2 9.6 %copy-start.14 = (s32[4,16]{1,0:T(4,128)S(1)}, s32[4,16]{1,0:T(4,128)}, u32[]{:S(2)}) copy-start(s32[4,16]{1,0:T(4,128)} %param.39) | copy-start | bytes 772
  6.2 14.0 %copy-start.1 = (f32[16,320]{1,0:T(8,128)S(1)}, f32[16,320]{1,0:T(8,128)}, u32[]{:S(2)}) copy-start(f32[16,320]{1,0:T(8,128)} %rhs.7) | copy-start | bytes 61444
  9.0 55.6 %collective-permute-start.97 = (bf16[4,320,640]{2,1,0:T(8,128)(2,1)}, bf16[4,320,640]{2,1,0:T(8,128)(2,1)S(1)}, u32[]{:S(2)}, u32[]{:S(2)}) collective-permute-start(bf16[4,320,640]{2,1,0:T(8,128)(2,1)} %first.1), channel_id=1, source_target_pairs={{1,2},{3,4},{5,6},{7,8},{9,10},{11,12},{13,14},{15,16},{17,18},{19... | collective-permute-start | bytes 4915208 | tf_op jit(solution)/shard_map/ppermute | solution.py:484
  20.2 2.1 %copy-start = (bf16[16,320,320]{2,1,0:T(8,128)(2,1)S(1)}, bf16[16,320,320]{2,1,0:T(8,128)(2,1)}, u32[]{:S(2)}) copy-start(bf16[16,320,320]{2,1,0:T(8,128)(2,1)} %refs_5_) | copy-start | bytes 9830404
  22.3 0.6 copy-start.4
  39.1 12.3 %collective-permute-start.102 = (f32[8,320]{1,0:T(8,128)S(1)}, f32[8,320]{1,0:T(8,128)S(1)}, u32[]{:S(2)}, u32[]{:S(2)}) collective-permute-start(f32[8,320]{1,0:T(8,128)S(1)} %get-tuple-element.356), channel_id=1, source_target_pairs={{0,1},{1,0},{2,3},{3,2},{4,5},{5,4},{6,7},{7,6},{8,9},{9,8},{10,11... | collective-permute-start | bytes 30728 | tf_op jit(solution)/shard_map/ppermute | solution.py:481
  41.2 23.4 %collective-permute-start.98 = (bf16[2,320,640]{2,1,0:T(8,128)(2,1)}, bf16[2,320,640]{2,1,0:T(8,128)(2,1)S(1)}, u32[]{:S(2)}, u32[]{:S(2)}) collective-permute-start(bf16[2,320,640]{2,1,0:T(8,128)(2,1)} %get-tuple-element.352), channel_id=1, source_target_pairs={{0,1},{1,0},{2,3},{3,2},{4,5},{5,4},{6,7},{7,6},{8,9},{9,8},{10,11... | collective-permute-start | bytes 2457608 | tf_op jit(solution)/shard_map/ppermute | solution.py:481
  50.9 13.6 %collective-permute-start.99 = (bf16[2,320,640]{2,1,0:T(8,128)(2,1)}, bf16[2,320,640]{2,1,0:T(8,128)(2,1)S(1)}, u32[]{:S(2)}, u32[]{:S(2)}) collective-permute-start(bf16[2,320,640]{2,1,0:T(8,128)(2,1)} %get-tuple-element.353), channel_id=1, source_target_pairs={{0,1},{1,0},{2,3},{3,2},{4,5},{5,4},{6,7},{7,6},{8,9},{9,8},{10,11... | collective-permute-start | bytes 2457608 | tf_op jit(solution)/shard_map/ppermute | solution.py:481
  51.0 13.5 %collective-permute-start.100 = (bf16[2,320,640]{2,1,0:T(8,128)(2,1)}, bf16[2,320,640]{2,1,0:T(8,128)(2,1)}, u32[]{:S(2)}, u32[]{:S(2)}) collective-permute-start(bf16[2,320,640]{2,1,0:T(8,128)(2,1)} %get-tuple-element.354), channel_id=1, source_target_pairs={{0,1},{1,0},{2,3},{3,2},{4,5},{5,4},{6,7},{7,6},{8,9},{9,8},{10,11... | collective-permute-start | bytes 2457608 | tf_op jit(solution)/shard_map/ppermute | solution.py:481
  51.4 13.1 %collective-permute-start.101 = (bf16[2,320,640]{2,1,0:T(8,128)(2,1)}, bf16[2,320,640]{2,1,0:T(8,128)(2,1)}, u32[]{:S(2)}, u32[]{:S(2)}) collective-permute-start(bf16[2,320,640]{2,1,0:T(8,128)(2,1)} %get-tuple-element.355), channel_id=1, source_target_pairs={{0,1},{1,0},{2,3},{3,2},{4,5},{5,4},{6,7},{7,6},{8,9},{9,8},{10,11... | collective-permute-start | bytes 2457608 | tf_op jit(solution)/shard_map/ppermute | solution.py:481
  51.6 13.0 %copy-start.3 = (s32[2]{0:T(128)S(1)}, s32[2]{0:T(128)}, u32[]{:S(2)}) copy-start(s32[2]{0:T(128)} %get-tuple-element.357.counts) | copy-start | bytes 28
  64.6 3.2 %copy-start.10 = (bf16[4,320,640]{2,1,0:T(8,128)(2,1)}, bf16[4,320,640]{2,1,0:T(8,128)(2,1)S(1)}, u32[]{:S(2)}) copy-start(bf16[4,320,640]{2,1,0:T(8,128)(2,1)S(1)} %collective-permute-done.97.refs_5_) | copy-start | bytes 4915204
  67.7 21.2 %copy-start.6 = (s32[32]{0:T(128)S(1)}, s32[32]{0:T(128)}, u32[]{:S(2)}) copy-start(s32[32]{0:T(128)} %get-tuple-element.338.table) | copy-start | bytes 388
  67.7 21.2 %copy-start.7 = (s32[32]{0:T(128)S(1)}, s32[32]{0:T(128)}, u32[]{:S(2)}) copy-start(s32[32]{0:T(128)} %get-tuple-element.339.lower_at) | copy-start | bytes 388
  67.8 21.2 %copy-start.8 = (s32[32]{0:T(128)S(1)}, s32[32]{0:T(128)}, u32[]{:S(2)}) copy-start(s32[32]{0:T(128)} %get-tuple-element.340.upper_at) | copy-start | bytes 388
  67.8 21.2 %copy-start.9 = (s32[32]{0:T(128)S(1)}, s32[32]{0:T(128)}, u32[]{:S(2)}) copy-start(s32[32]{0:T(128)} %get-tuple-element.341.back) | copy-start | bytes 388
  67.8 20.3 %collective-permute-start.49 = (bf16[320,640]{1,0:T(8,128)(2,1)}, bf16[320,640]{1,0:T(8,128)(2,1)}, u32[]{:S(2)}, u32[]{:S(2)}) collective-permute-start(bf16[320,640]{1,0:T(8,128)(2,1)} %get-tuple-element.242), channel_id=1, source_target_pairs={{1,2},{3,4},{5,6},{7,8},{9,10},{11,12},{13,14},{15,16},{17,18},{19... | collective-permute-start | bytes 1228808 | tf_op jit(solution)/shard_map/cond/branch_15_fun/ppermute | solution.py:648
  69.1 19.0 %collective-permute-start.50 = (bf16[320,640]{1,0:T(8,128)(2,1)}, bf16[320,640]{1,0:T(8,128)(2,1)}, u32[]{:S(2)}, u32[]{:S(2)}) collective-permute-start(bf16[320,640]{1,0:T(8,128)(2,1)} %get-tuple-element.243), channel_id=1, source_target_pairs={{1,2},{3,4},{5,6},{7,8},{9,10},{11,12},{13,14},{15,16},{17,18},{19... | collective-permute-start | bytes 1228808 | tf_op jit(solution)/shard_map/cond/branch_15_fun/ppermute | solution.py:648
  70.4 17.7 %collective-permute-start.51 = (bf16[320,640]{1,0:T(8,128)(2,1)}, bf16[320,640]{1,0:T(8,128)(2,1)}, u32[]{:S(2)}, u32[]{:S(2)}) collective-permute-start(bf16[320,640]{1,0:T(8,128)(2,1)} %get-tuple-element.244), channel_id=1, source_target_pairs={{1,2},{3,4},{5,6},{7,8},{9,10},{11,12},{13,14},{15,16},{17,18},{19... | collective-permute-start | bytes 1228808 | tf_op jit(solution)/shard_map/cond/branch_15_fun/ppermute | solution.py:648
  71.7 16.4 %collective-permute-start.52 = (f32[8,320]{1,0:T(8,128)S(1)}, f32[8,320]{1,0:T(8,128)}, u32[]{:S(2)}, u32[]{:S(2)}) collective-permute-start(f32[8,320]{1,0:T(8,128)S(1)} %get-tuple-element.245), channel_id=1, source_target_pairs={{1,2},{3,4},{5,6},{7,8},{9,10},{11,12},{13,14},{15,16},{17,18},{19... | collective-permute-start | bytes 30728 | tf_op jit(solution)/shard_map/cond/branch_15_fun/ppermute | solution.py:484
  89.0 11.2 %copy-start.13 = (s32[16]{0:T(128)S(1)}, s32[16]{0:T(128)}, u32[]{:S(2)}) copy-start(s32[16]{0:T(128)} %slots.7) | copy-start | bytes 196
  89.0 11.2 %copy-start.15 = (s32[16]{0:T(128)S(1)}, s32[16]{0:T(128)}, u32[]{:S(2)}) copy-start(s32[16]{0:T(128)} %get-tuple-element.383.across_slots) | copy-start | bytes 196
  89.0 11.2 %copy-start.16 = (s32[16]{0:T(128)S(1)}, s32[16]{0:T(128)}, u32[]{:S(2)}) copy-start(s32[16]{0:T(128)} %get-tuple-element.388.side_slots) | copy-start | bytes 196
  89.0 16.7 %copy-start.5 = (s32[16]{0:T(128)S(1)}, s32[16]{0:T(128)}, u32[]{:S(2)}) copy-start(s32[16]{0:T(128)} %get-tuple-element.347.send) | copy-start | bytes 196
  96.9 1.3 collective-permute-start.103
  98.2 6.3 %collective-permute-start.104 = (bf16[64,320]{1,0:T(8,128)(2,1)S(1)}, bf16[64,320]{1,0:T(8,128)(2,1)S(1)}, u32[]{:S(2)}, u32[]{:S(2)}) collective-permute-start(bf16[64,320]{1,0:T(8,128)(2,1)S(1)} %maximum_select_fusion), channel_id=1, source_target_pairs={{1,2},{3,4},{5,6},{7,8},{9,10},{11,12},{13,14},{15,16},{17,18},{19... | collective-permute-start | bytes 122888 | tf_op jit(solution)/shard_map/ppermute | solution.py:484
  104.5 1.2 collective-permute-start.105
  117.8 2.1 %collective-permute-start.106 = (f32[8,320]{1,0:T(8,128)S(1)}, f32[8,320]{1,0:T(8,128)S(1)}, u32[]{:S(2)}, u32[]{:S(2)}) collective-permute-start(f32[8,320]{1,0:T(8,128)S(1)} %get-tuple-element.376), channel_id=1, source_target_pairs={{0,1},{1,0},{2,3},{3,2},{4,5},{5,4},{6,7},{7,6},{8,9},{9,8},{10,11... | collective-permute-start | bytes 30728 | tf_op jit(solution)/shard_map/ppermute | solution.py:481
  118.1 5.9 %collective-permute-start.107 = (f32[8,320]{1,0:T(8,128)S(1)}, f32[8,320]{1,0:T(8,128)S(1)}, u32[]{:S(2)}, u32[]{:S(2)}) collective-permute-start(f32[8,320]{1,0:T(8,128)S(1)} %get-tuple-element.378), channel_id=1, source_target_pairs={{1,2},{3,4},{5,6},{7,8},{9,10},{11,12},{13,14},{15,16},{17,18},{19... | collective-permute-start | bytes 30728 | tf_op jit(solution)/shard_map/ppermute | solution.py:484
  131.7 0.6 copy-start.2
  132.3 1.9 %collective-permute-start.108 = (f32[8,320]{1,0:T(8,128)S(1)}, f32[8,320]{1,0:T(8,128)S(1)}, u32[]{:S(2)}, u32[]{:S(2)}) collective-permute-start(f32[8,320]{1,0:T(8,128)S(1)} %get-tuple-element.379), channel_id=1, source_target_pairs={{0,1},{1,0},{2,3},{3,2},{4,5},{5,4},{6,7},{7,6},{8,9},{9,8},{10,11... | collective-permute-start | bytes 30728 | tf_op jit(solution)/shard_map/ppermute | solution.py:481
  132.3 5.9 %collective-permute-start.109 = (f32[8,320]{1,0:T(8,128)S(1)}, f32[8,320]{1,0:T(8,128)S(1)}, u32[]{:S(2)}, u32[]{:S(2)}) collective-permute-start(f32[8,320]{1,0:T(8,128)S(1)} %get-tuple-element.381), channel_id=1, source_target_pairs={{1,2},{3,4},{5,6},{7,8},{9,10},{11,12},{13,14},{15,16},{17,18},{19... | collective-permute-start | bytes 30728 | tf_op jit(solution)/shard_map/ppermute | solution.py:484
  134.3 4.0 %copy-start.11 = (f32[8,320]{1,0:T(8,128)}, f32[8,320]{1,0:T(8,128)S(1)}, u32[]{:S(2)}) copy-start(f32[8,320]{1,0:T(8,128)S(1)} %collective-permute-done.108.side) | copy-start | bytes 30724
  138.2 0.6 copy-start.12

commit v4 on v3

--- a/solution.py
+++ b/solution.py
@@ -286,37 +286,48 @@
 
 def face_kernel(counts, send, index, rhs, *refs):
     parts = refs[: len(counts)]
-    faces, piv, side_out, across_out, own_out, rows, gathered, held, scaled, fb, pb, fsem, psem = refs[len(counts) :]
+    faces, piv, side_out, across_out, own_out, rows, gathered, flat, rhs_t, held, scaled, fb, pb, fsem, psem = refs[
+        len(counts) :
+    ]
     elems, width = rhs.shape
     count = faces.shape[1]
-    face_copies = [pltpu.make_async_copy(faces.at[e], fb.at[e], fsem.at[e]) for e in range(elems)]
-    piv_copies = [pltpu.make_async_copy(piv.at[e], pb.at[e], psem.at[e]) for e in range(elems)]
-    for face_copy, piv_copy in zip(face_copies, piv_copies):
-        face_copy.start()
-        piv_copy.start()
+    for e in range(elems):
+        pltpu.make_async_copy(faces.at[e], fb.at[e], fsem.at[e]).start()
+        pltpu.make_async_copy(piv.at[e], pb.at[e], psem.at[e]).start()
     at = 0
     for part, size in zip(parts, counts):
         rows[at : at + size] = part[...]
         at += size
     wanted = index[...] == lax.broadcasted_iota(jnp.int32, (count * elems, at), 1)
-    picked = dot_nn(wanted.astype(jnp.bfloat16), rows[...]).astype(jnp.bfloat16)
-    gathered[...] = picked
-    ends = jnp.concatenate([picked[f * elems : (f + 1) * elems, WIDE:] for f in range(count)], axis=1)
-    row = lax.broadcasted_iota(jnp.int32, (elems, width), 0)
+    gathered[...] = dot_nn(wanted.astype(jnp.bfloat16), rows[...])
+    flat[...] = jnp.zeros(flat.shape, jnp.float32)
+    flat[:elems, :width] = rhs[...]
+    rhs_t[...] = flat[...].T
+    lanes = rhs_t.shape[1]
+    column = lax.broadcasted_iota(jnp.int32, (width, lanes), 1)
 
     def residual(e):
         pltpu.make_async_copy(faces.at[e], fb.at[e], fsem.at[e]).wait()
-        total = dot_nt(gathered[:elems, :WIDE], fb[e, 0, :, :WIDE])
-        for f in range(1, count):
-            total += dot_nt(gathered[f * elems : (f + 1) * elems, :WIDE], fb[e, f, :, :WIDE])
-        tails = jnp.concatenate([fb[e, f, :, WIDE:] for f in range(count)], axis=1)
-        total += dot_nt(ends, tails)
-        return (rhs[...] - total).astype(jnp.bfloat16)
+        states = [gathered[pl.ds(f * elems + e, 1), :] for f in range(count)]
+
+        def term(f, low, high):
+            return fb[e, f, :, low:high].astype(jnp.float32) * states[f][:, low:high]
+
+        lead, ending = None, None
+        for f in range(count):
+            for low in range(0, WIDE, lanes):
+                more = term(f, low, low + lanes)
+                lead = more if lead is None else lead + more
+            more = term(f, WIDE, width)
+            ending = more if ending is None else ending + more
+        total = jnp.sum(lead, axis=1, keepdims=True) + jnp.sum(ending, axis=1, keepdims=True)
+        return (rhs_t[:width] - total).astype(jnp.bfloat16)
 
     def apply(e):
         pltpu.make_async_copy(piv.at[e], pb.at[e], psem.at[e]).wait()
-        scaled[...] = jnp.where(row == e, dot_nt(held[...], pb[e]), scaled[...])
-
+        scaled[:width] = jnp.where(column == e, dot_nn(pb[e], held[...]), scaled[:width])
+
+    scaled[...] = jnp.zeros(scaled.shape, jnp.float32)
     held[...] = residual(0)
 
     def step(e, carry):
@@ -326,11 +337,12 @@
 
     lax.fori_loop(1, elems, step, 0)
     apply(elems - 1)
-    own_out[...] = scaled[...]
+    flat[...] = scaled[...].T
+    own_out[...] = flat[:elems, :width]
     bucket = side_out.shape[0]
     for k in range(bucket):
-        side_out[k : k + 1] = scaled[pl.ds(send[k], 1), :]
-        across_out[k : k + 1] = scaled[pl.ds(send[bucket + k], 1), :]
+        side_out[k : k + 1] = flat[pl.ds(send[k], 1), :][:, :width]
+        across_out[k : k + 1] = flat[pl.ds(send[bucket + k], 1), :][:, :width]
 
 
 def solve_kernel(last, rests, table, lower_at, upper_at, back, counts, *refs):
@@ -439,6 +451,10 @@
         for p in range(LMAX):
             items[p * lines : (p + 1) * lines] = behind[p, :lines, :]
         out[...] = items[...].astype(jnp.bfloat16)
+
+
+def nothing_kernel(*outs):
+    pass
 
 
 def place_kernel(index, side, own, across, out, items):
@@ -602,9 +618,11 @@
             out_specs=[VMEM] * 3,
             scratch_shapes=[
                 pltpu.VMEM((sum(counts), width), bf16),
-                pltpu.VMEM((faces * elems, width), bf16),
-                pltpu.VMEM((elems, width), bf16),
-                pltpu.VMEM((elems, width), f32),
+                pltpu.VMEM((faces * elems, width), f32),
+                pltpu.VMEM((128, width + room), f32),
+                pltpu.VMEM((width + room, 128), f32),
+                pltpu.VMEM((width, 128), bf16),
+                pltpu.VMEM((width + room, 128), f32),
                 pltpu.VMEM((elems, faces) + block, bf16),
                 pltpu.VMEM((elems,) + block, bf16),
                 dma((elems,)),
@@ -645,7 +663,13 @@
         got = []
         for j, block in enumerate(blocks):
             pairs = (up_pairs if j < going else []) + (down_pairs if j < coming else [])
-            got.append(lax.ppermute(block, "dom", pairs) if pairs else jnp.zeros_like(block))
+            if pairs:
+                got.append(lax.ppermute(block, "dom", pairs))
+        unused = len(blocks) - len(got)
+        if unused:
+            got += pl.pallas_call(
+                nothing_kernel, out_shape=[jax.ShapeDtypeStruct(pair, bf16)] * unused, out_specs=[HBM] * unused, name="unused"
+            )()
         return (*got, to_across(vectors))
 
     exchanges = [

time: 142 us -> 132 us (0.930)
  the two profiles are of different devices: /device:TPU:28 before, /device:TPU:23 now
where the time goes in v4:
time: 132 us; the launch traced here: 130 us
  Pallas kernels  61.5 us (47%)
  starting transfers between devices  35.5 us (27%)
  waiting for transfers between devices  20.7 us (16%)
  local copies, waits for them, and re-layouts  6.05 us (5%)
  other arithmetic  3.19 us (2%)
  between operations  3.04 us (2%)
    pallas_call x2, Pallas kernels, face_part(): pl.pallas_call(functools.partial(face_kernel, counts), out_shape=[jax.Sha...  24.5 us
    ppermute x10, starting transfers between devices, to_side(): return lax.ppermute(array, 'dom', side_pairs)  18.7 us
    ppermute x6, waiting for transfers between devices, to_across(): return lax.ppermute(array, 'dom', across_pairs)  17.9 us
    ppermute x6, starting transfers between devices, to_across(): return lax.ppermute(array, 'dom', across_pairs)  16.8 us
    pallas_call x2, Pallas kernels, solve(): pl.pallas_call(functools.partial(solve_kernel, last, rests), out_shape=ou...  13.5 us
    pallas_call x1, Pallas kernels, body(): pl.pallas_call(functools.partial(rest_kernel, blind, SIDES, slot_count),...  8.23 us
    pallas_call x1, Pallas kernels, body(): pl.pallas_call(functools.partial(staying_kernel, slot_count), out_shape=j...  6.98 us
    pallas_call x1, Pallas kernels, body(): pl.pallas_call(functools.partial(first_kernel, slot_count), out_shape=jax...  4.03 us
  transfers between devices with their start and end apart: 16, of which 7 were waited for; matrix products, arithmetic and copies ran while one was open for 2% of the time, Pallas kernels for 28%

profile of v4, /device:TPU:23, one launch (start us, length us, event | category | flops | bytes accessed | tf_op | source)
XLA Modules:
  0.0 130.0 jit_solution(1865913364533690132)
XLA Ops:
  0.0 0.7 convert_element_type.18.refs_1_
  0.7 0.7 subtract_convert_fusion
  1.5 0.1 pad_maximum_fusion
  1.6 0.7 collective-permute-start.95
  2.2 0.8 collective-permute-done.95
  3.1 0.2 slice_reduce_fusion
  3.3 0.1 broadcast_select_fusion
  3.3 0.1 pad_maximum_fusion.1
  3.4 3.3 %collective-permute-start.96 = (bf16[16,384]{1,0:T(8,128)(2,1)S(1)}, bf16[16,384]{1,0:T(8,128)(2,1)S(1)}, u32[]{:S(2)}, u32[]{:S(2)}) collective-permute-start(bf16[16,384]{1,0:T(8,128)(2,1)S(1)} %pad_maximum_fusion.1), channel_id=1, source_target_pairs={{1,2},{3,4},{5,6},{7,8},{9,10},{11,12},{13,14},{15,16},{17,18},{19... | collective-permute-start | bytes 36872 | tf_op jit(solution)/shard_map/ppermute | solution.py:500
  6.8 4.0 %first.1 = bf16[4,320,640]{2,1,0:T(8,128)(2,1)} custom-call(s32[16]{0:T(128)} %slots.7, s32[1]{0:T(128)} %bitcast.across, bf16[16,320,320]{2,1,0:T(8,128)(2,1)} %refs_5_, bf16[16,320,320]{2,1,0:T(8,128)(2,1)} %low.5, bf16[16,320,320]{2,1,0:T(8,128)(2,1)} %upp.5), custom_call_target="tpu_custom_call" | custom-call | flops 1048576 | bytes 1048576 | tf_op jit(solution)/shard_map/first/pallas_call | solution.py:528
  10.8 4.6 %collective-permute-start.97 = (bf16[4,320,640]{2,1,0:T(8,128)(2,1)}, bf16[4,320,640]{2,1,0:T(8,128)(2,1)S(1)}, u32[]{:S(2)}, u32[]{:S(2)}) collective-permute-start(bf16[4,320,640]{2,1,0:T(8,128)(2,1)} %first.1), channel_id=1, source_target_pairs={{1,2},{3,4},{5,6},{7,8},{9,10},{11,12},{13,14},{15,16},{17,18},{19... | collective-permute-start | bytes 4915208 | tf_op jit(solution)/shard_map/ppermute | solution.py:500
  15.5 0.1 reshape.34.index
  15.6 0.6 pad_add_fusion.ids
  16.2 0.8 select_reduce_fusion
  17.0 2.9 %plan.1 = (s32[32]{0:T(128)}, s32[32]{0:T(128)}, s32[32]{0:T(128)}, s32[32]{0:T(128)}, s32[16]{0:T(128)}, /*index=5*/s32[16]{0:T(128)}, s32[2]{0:T(128)}) custom-call(s32[16]{0:T(128)} %slots.7, s32[16]{0:T(128)} %get-tuple-element.411.side_slots, s32[16]{0:T(128)} %get-tuple-element.406.across_slots, s32[16]{0:T(128)} %get-tuple-element.405.far_slots, ...), custom_call_target="tpu_custom_call" | custom-call | flops 1048576 | bytes 1048576 | tf_op jit(solution)/shard_map/plan/pallas_call | solution.py:565
  19.9 2.1 %copy-done = bf16[16,320,320]{2,1,0:T(8,128)(2,1)S(1)} copy-done((bf16[16,320,320]{2,1,0:T(8,128)(2,1)S(1)}, bf16[16,320,320]{2,1,0:T(8,128)(2,1)}, u32[]{:S(2)}) %copy-start) | copy-done | bytes 3276824
  22.0 0.6 copy-done.4
  22.6 14.2 %faces.2 = (f32[8,320]{1,0:T(8,128)S(1)}, f32[8,320]{1,0:T(8,128)S(1)}, f32[16,320]{1,0:T(8,128)S(1)}) custom-call(s32[16]{0:T(128)S(1)} %copy-done.4, s32[64,1]{1,0:T(8,128)S(1)} %reshape.34.index, f32[16,320]{1,0:T(8,128)S(1)} %copy-done.1, bf16[16,320]{1,0:T(8,128)(2,1)S(1)} %bitcast.8, bf16[16,320]{1,0:T(8,128)(2,1)S(1)} %convert_element_type.18.refs_1_, ...), custom_call_target="tpu_custom_call" | custom-call | flops 1048576 | bytes 1048576 | tf_op jit(solution)/shard_map/faces/pallas_call | solution.py:610
  36.8 0.2 collective-permute-start.102
  37.0 8.2 %rest.1 = (bf16[2,320,640]{2,1,0:T(8,128)(2,1)}, bf16[2,320,640]{2,1,0:T(8,128)(2,1)}, bf16[2,320,640]{2,1,0:T(8,128)(2,1)}, bf16[2,320,640]{2,1,0:T(8,128)(2,1)...) custom-call(s32[16]{0:T(128)} %slots.7, ...), custom_call_target="tpu_custom_call" | custom-call | flops 1048576 | bytes 1048576 | tf_op jit(solution)/shard_map/rest/pallas_call | solution.py:547
  45.3 0.5 collective-permute-start.99
  45.8 0.1 collective-permute-start.100
  45.9 0.4 collective-permute-start.101
  46.3 0.1 reshape.26
  46.4 7.0 %staying.1.refs_4_ = bf16[16,320,640]{2,1,0:T(8,128)(2,1)} custom-call(s32[16]{0:T(128)} %slots.7, s32[1]{0:T(128)} %bitcast.2.me, bf16[16,320,320]{2,1,0:T(8,128)(2,1)} %refs_5_, bf16[16,320,320]{2,1,0:T(8,128)(2,1)} %low.5, bf16[16,320,320]{2,1,0:T(8,128)(2,1)} %upp.5), custom_call_target="tpu_custom_call" | custom-call | flops 1048576 | bytes 1048576 | tf_op jit(solution)/shard_map/staying/pallas_call | solution.py:574
  53.5 0.7 fusion.18
  56.8 7.0 %conditional.1 = (bf16[320,640]{1,0:T(8,128)(2,1)}, bf16[320,640]{1,0:T(8,128)(2,1)}, bf16[320,640]{1,0:T(8,128)(2,1)}, bf16[320,640]{1,0:T(8,128)(2,1)}, f32[8,320]{1,0:T(8,128)}) conditional(s32[]{:T(128)} %clamp.3, f32[8,320]{1,0:T(8,128)S(1)} %get-tuple-element.387, (bf16[320,640]{1,0:T(8,128)(2,1)}, ...), branch_computations={%region_0.1_spmd, %region_1.2_spmd, %region_2.3_spmd, %region_3.4_... | conditional | bytes 8233228 | solution.py:689
  56.8 2.8 %collective-permute-start = (f32[8,320]{1,0:T(8,128)S(1)}, f32[8,320]{1,0:T(8,128)}, u32[]{:S(2)}, u32[]{:S(2)}) collective-permute-start(f32[8,320]{1,0:T(8,128)S(1)} %param), channel_id=1, source_target_pairs={{1,2},{3,4},{5,6},{7,8},{9,10},{11,12},{13,14},{15,16},{17,18},{19... | collective-permute-start | bytes 30728 | tf_op jit(solution)/shard_map/cond/branch_0_fun/ppermute | solution.py:500
  59.6 4.3 %collective-permute-done = f32[8,320]{1,0:T(8,128)} collective-permute-done((f32[8,320]{1,0:T(8,128)S(1)}, f32[8,320]{1,0:T(8,128)}, u32[]{:S(2)}, u32[]{:S(2)}) %collective-permute-start) | collective-permute-done | bytes 10272 | tf_op jit(solution)/shard_map/cond/branch_0_fun/ppermute | solution.py:500
  63.9 6.8 %solve.2.refs_0_ = bf16[32,320]{1,0:T(8,128)(2,1)S(1)} custom-call(s32[32]{0:T(128)S(1)} %copy-done.6, s32[32]{0:T(128)S(1)} %copy-done.7, s32[32]{0:T(128)S(1)} %copy-done.8, s32[32]{0:T(128)S(1)} %copy-done.9, s32[2]{0:T(128)S(1)} %copy-done.3, bf16[2,320,640]{2,1,0:T(8,128)(2,1)S(1)} %collective-permute-done.98.refs_0_, ...), custom_call_target="tpu_custom_call" | custom-call | flops 1048576 | bytes 1048576 | tf_op jit(solution)/shard_map/solve/pallas_call | solution.py:642
  70.8 16.5 %collective-permute-start.103 = (bf16[32,320]{1,0:T(8,128)(2,1)S(1)}, bf16[32,320]{1,0:T(8,128)(2,1)S(1)}, u32[]{:S(2)}, u32[]{:S(2)}) collective-permute-start(bf16[32,320]{1,0:T(8,128)(2,1)S(1)} %solve.2.refs_0_), channel_id=1, source_target_pairs={{0,1},{1,0},{2,3},{3,2},{4,5},{5,4},{6,7},{7,6},{8,9},{9,8},{10,11... | collective-permute-start | bytes 61448 | tf_op jit(solution)/shard_map/ppermute | solution.py:497
  87.3 0.8 collective-permute-done.103.refs_1_
  88.1 1.9 %collective-permute-start.104 = (bf16[64,320]{1,0:T(8,128)(2,1)S(1)}, bf16[64,320]{1,0:T(8,128)(2,1)S(1)}, u32[]{:S(2)}, u32[]{:S(2)}) collective-permute-start(bf16[64,320]{1,0:T(8,128)(2,1)S(1)} %maximum_select_fusion), channel_id=1, source_target_pairs={{1,2},{3,4},{5,6},{7,8},{9,10},{11,12},{13,14},{15,16},{17,18},{19... | collective-permute-start | bytes 122888 | tf_op jit(solution)/shard_map/ppermute | solution.py:500
  90.2 0.8 gather_fusion
  90.9 0.1 reshape.25
  91.0 4.3 %collective-permute-done.104.refs_2_ = bf16[64,320]{1,0:T(8,128)(2,1)S(1)} collective-permute-done((bf16[64,320]{1,0:T(8,128)(2,1)S(1)}, bf16[64,320]{1,0:T(8,128)(2,1)S(1)}, u32[]{:S(2)}, u32[]{:S(2)}) %collective-permute-start.104) | collective-permute-done | bytes 40992 | tf_op jit(solution)/shard_map/ppermute | solution.py:500
  95.4 0.1 reshape.35.index
  95.5 1.1 collective-permute-done.105.refs_3_
  96.6 10.3 %faces.3 = (f32[8,320]{1,0:T(8,128)S(1)}, f32[8,320]{1,0:T(8,128)S(1)}, f32[16,320]{1,0:T(8,128)S(1)}) custom-call(s32[16]{0:T(128)S(1)} %copy-done.5, s32[64,1]{1,0:T(8,128)S(1)} %reshape.35.index, f32[16,320]{1,0:T(8,128)S(1)} %copy-done.1, bf16[32,320]{1,0:T(8,128)(2,1)S(1)} %solve.2.refs_0_, bf16[32,320]{1,0:T(8,128)(2,1)S(1)} %collective-permute-done.103.refs_1_, ...), custom_call_target="tpu_custom_call" | custom-call | flops 1048576 | bytes 1048576 | tf_op jit(solution)/shard_map/faces/pallas_call | solution.py:610
  106.9 0.2 collective-permute-start.106
  107.1 1.9 %collective-permute-start.107 = (f32[8,320]{1,0:T(8,128)S(1)}, f32[8,320]{1,0:T(8,128)S(1)}, u32[]{:S(2)}, u32[]{:S(2)}) collective-permute-start(f32[8,320]{1,0:T(8,128)S(1)} %get-tuple-element.401), channel_id=1, source_target_pairs={{1,2},{3,4},{5,6},{7,8},{9,10},{11,12},{13,14},{15,16},{17,18},{19... | collective-permute-start | bytes 30728 | tf_op jit(solution)/shard_map/ppermute | solution.py:500
  109.1 4.9 %collective-permute-done.107.refs_12_ = f32[8,320]{1,0:T(8,128)S(1)} collective-permute-done((f32[8,320]{1,0:T(8,128)S(1)}, f32[8,320]{1,0:T(8,128)S(1)}, u32[]{:S(2)}, u32[]{:S(2)}) %collective-permute-start.107) | collective-permute-done | bytes 10272 | tf_op jit(solution)/shard_map/ppermute | solution.py:500
  113.9 6.7 %solve.3 = (f32[8,320]{1,0:T(8,128)S(1)}, f32[16,320]{1,0:T(8,128)S(1)}, f32[8,320]{1,0:T(8,128)S(1)}) custom-call(s32[32]{0:T(128)S(1)} %copy-done.6, s32[32]{0:T(128)S(1)} %copy-done.7, s32[32]{0:T(128)S(1)} %copy-done.8, s32[32]{0:T(128)S(1)} %copy-done.9, s32[2]{0:T(128)S(1)} %copy-done.3, bf16[2,320,640]{2,1,0:T(8,128)(2,1)S(1)} %collective-permute-done.98.refs_0_, ...), custom_call_target="tpu_custom_call" | custom-call | flops 1048576 | bytes 1048576 | tf_op jit(solution)/shard_map/solve/pallas_call | solution.py:642
  120.6 0.6 copy-done.2
  121.2 2.3 %collective-permute-start.109 = (f32[8,320]{1,0:T(8,128)S(1)}, f32[8,320]{1,0:T(8,128)S(1)}, u32[]{:S(2)}, u32[]{:S(2)}) collective-permute-start(f32[8,320]{1,0:T(8,128)S(1)} %get-tuple-element.404), channel_id=1, source_target_pairs={{1,2},{3,4},{5,6},{7,8},{9,10},{11,12},{13,14},{15,16},{17,18},{19... | collective-permute-start | bytes 30728 | tf_op jit(solution)/shard_map/ppermute | solution.py:500
  123.5 4.5 %collective-permute-done.109.across = f32[8,320]{1,0:T(8,128)S(1)} collective-permute-done((f32[8,320]{1,0:T(8,128)S(1)}, f32[8,320]{1,0:T(8,128)S(1)}, u32[]{:S(2)}, u32[]{:S(2)}) %collective-permute-start.109) | collective-permute-done | bytes 10272 | tf_op jit(solution)/shard_map/ppermute | solution.py:500
  128.0 0.6 copy-done.22
  128.6 1.4 %place.1 = f32[16,320]{1,0:T(8,128)} custom-call(s32[16]{0:T(128)} %get-tuple-element.360.index, f32[8,320]{1,0:T(8,128)} %copy-done.21, f32[16,320]{1,0:T(8,128)} %copy-done.2, f32[8,320]{1,0:T(8,128)} %copy-done.22), custom_call_target="tpu_custom_call" | custom-call | tf_op jit(solution)/shard_map/place/pallas_call | solution.py:706
  (52 shorter events, 0.4 us)
Async XLA Ops:
  1.6 1.5 %collective-permute-start.95 = (bf16[16,384]{1,0:T(8,128)(2,1)S(1)}, bf16[16,384]{1,0:T(8,128)(2,1)S(1)}, u32[]{:S(2)}, u32[]{:S(2)}) collective-permute-start(bf16[16,384]{1,0:T(8,128)(2,1)S(1)} %pad_maximum_fusion), channel_id=1, source_target_pairs={{0,1},{1,0},{2,3},{3,2},{4,5},{5,4},{6,7},{7,6},{8,9},{9,8},{10,11... | collective-permute-start | bytes 36872 | tf_op jit(solution)/shard_map/ppermute | solution.py:497
  3.4 7.4 %collective-permute-start.96 = (bf16[16,384]{1,0:T(8,128)(2,1)S(1)}, bf16[16,384]{1,0:T(8,128)(2,1)S(1)}, u32[]{:S(2)}, u32[]{:S(2)}) collective-permute-start(bf16[16,384]{1,0:T(8,128)(2,1)S(1)} %pad_maximum_fusion.1), channel_id=1, source_target_pairs={{1,2},{3,4},{5,6},{7,8},{9,10},{11,12},{13,14},{15,16},{17,18},{19... | collective-permute-start | bytes 36872 | tf_op jit(solution)/shard_map/ppermute | solution.py:500
  6.8 8.7 %copy-start.24 = (s32[4,16]{1,0:T(4,128)S(1)}, s32[4,16]{1,0:T(4,128)}, u32[]{:S(2)}) copy-start(s32[4,16]{1,0:T(4,128)} %param.39) | copy-start | bytes 772
  6.8 13.1 %copy-start.1 = (f32[16,320]{1,0:T(8,128)S(1)}, f32[16,320]{1,0:T(8,128)}, u32[]{:S(2)}) copy-start(f32[16,320]{1,0:T(8,128)} %rhs.7) | copy-start | bytes 61444
  10.8 42.6 %collective-permute-start.97 = (bf16[4,320,640]{2,1,0:T(8,128)(2,1)}, bf16[4,320,640]{2,1,0:T(8,128)(2,1)S(1)}, u32[]{:S(2)}, u32[]{:S(2)}) collective-permute-start(bf16[4,320,640]{2,1,0:T(8,128)(2,1)} %first.1), channel_id=1, source_target_pairs={{1,2},{3,4},{5,6},{7,8},{9,10},{11,12},{13,14},{15,16},{17,18},{19... | collective-permute-start | bytes 4915208 | tf_op jit(solution)/shard_map/ppermute | solution.py:500
  19.9 2.1 %copy-start = (bf16[16,320,320]{2,1,0:T(8,128)(2,1)S(1)}, bf16[16,320,320]{2,1,0:T(8,128)(2,1)}, u32[]{:S(2)}) copy-start(bf16[16,320,320]{2,1,0:T(8,128)(2,1)} %refs_5_) | copy-start | bytes 9830404
  22.0 0.6 copy-start.4
  36.8 9.1 %collective-permute-start.102 = (f32[8,320]{1,0:T(8,128)S(1)}, f32[8,320]{1,0:T(8,128)S(1)}, u32[]{:S(2)}, u32[]{:S(2)}) collective-permute-start(f32[8,320]{1,0:T(8,128)S(1)} %get-tuple-element.379), channel_id=1, source_target_pairs={{0,1},{1,0},{2,3},{3,2},{4,5},{5,4},{6,7},{7,6},{8,9},{9,8},{10,11... | collective-permute-start | bytes 30728 | tf_op jit(solution)/shard_map/ppermute | solution.py:497
  45.2 8.2 %collective-permute-start.98 = (bf16[2,320,640]{2,1,0:T(8,128)(2,1)}, bf16[2,320,640]{2,1,0:T(8,128)(2,1)S(1)}, u32[]{:S(2)}, u32[]{:S(2)}) collective-permute-start(bf16[2,320,640]{2,1,0:T(8,128)(2,1)} %get-tuple-element.375), channel_id=1, source_target_pairs={{0,1},{1,0},{2,3},{3,2},{4,5},{5,4},{6,7},{7,6},{8,9},{9,8},{10,11... | collective-permute-start | bytes 2457608 | tf_op jit(solution)/shard_map/ppermute | solution.py:497
  45.3 8.1 %collective-permute-start.99 = (bf16[2,320,640]{2,1,0:T(8,128)(2,1)}, bf16[2,320,640]{2,1,0:T(8,128)(2,1)S(1)}, u32[]{:S(2)}, u32[]{:S(2)}) collective-permute-start(bf16[2,320,640]{2,1,0:T(8,128)(2,1)} %get-tuple-element.376), channel_id=1, source_target_pairs={{0,1},{1,0},{2,3},{3,2},{4,5},{5,4},{6,7},{7,6},{8,9},{9,8},{10,11... | collective-permute-start | bytes 2457608 | tf_op jit(solution)/shard_map/ppermute | solution.py:497
  45.8 7.6 %collective-permute-start.100 = (bf16[2,320,640]{2,1,0:T(8,128)(2,1)}, bf16[2,320,640]{2,1,0:T(8,128)(2,1)}, u32[]{:S(2)}, u32[]{:S(2)}) collective-permute-start(bf16[2,320,640]{2,1,0:T(8,128)(2,1)} %get-tuple-element.377), channel_id=1, source_target_pairs={{0,1},{1,0},{2,3},{3,2},{4,5},{5,4},{6,7},{7,6},{8,9},{9,8},{10,11... | collective-permute-start | bytes 2457608 | tf_op jit(solution)/shard_map/ppermute | solution.py:497
  45.9 7.6 %collective-permute-start.101 = (bf16[2,320,640]{2,1,0:T(8,128)(2,1)}, bf16[2,320,640]{2,1,0:T(8,128)(2,1)}, u32[]{:S(2)}, u32[]{:S(2)}) collective-permute-start(bf16[2,320,640]{2,1,0:T(8,128)(2,1)} %get-tuple-element.378), channel_id=1, source_target_pairs={{0,1},{1,0},{2,3},{3,2},{4,5},{5,4},{6,7},{7,6},{8,9},{9,8},{10,11... | collective-permute-start | bytes 2457608 | tf_op jit(solution)/shard_map/ppermute | solution.py:497
  46.4 7.1 %copy-start.3 = (s32[2]{0:T(128)S(1)}, s32[2]{0:T(128)}, u32[]{:S(2)}) copy-start(s32[2]{0:T(128)} %get-tuple-element.380.counts) | copy-start | bytes 28
  46.4 17.5 %copy-start.6 = (s32[32]{0:T(128)S(1)}, s32[32]{0:T(128)}, u32[]{:S(2)}) copy-start(s32[32]{0:T(128)} %get-tuple-element.361.table) | copy-start | bytes 388
  46.4 17.5 %copy-start.7 = (s32[32]{0:T(128)S(1)}, s32[32]{0:T(128)}, u32[]{:S(2)}) copy-start(s32[32]{0:T(128)} %get-tuple-element.362.lower_at) | copy-start | bytes 388
  46.4 17.5 %copy-start.8 = (s32[32]{0:T(128)S(1)}, s32[32]{0:T(128)}, u32[]{:S(2)}) copy-start(s32[32]{0:T(128)} %get-tuple-element.363.upper_at) | copy-start | bytes 388
  46.4 17.5 %copy-start.9 = (s32[32]{0:T(128)S(1)}, s32[32]{0:T(128)}, u32[]{:S(2)}) copy-start(s32[32]{0:T(128)} %get-tuple-element.364.back) | copy-start | bytes 388
  53.5 10.4 %copy-start.10 = (bf16[4,320,640]{2,1,0:T(8,128)(2,1)}, bf16[4,320,640]{2,1,0:T(8,128)(2,1)S(1)}, u32[]{:S(2)}) copy-start(bf16[4,320,640]{2,1,0:T(8,128)(2,1)S(1)} %collective-permute-done.97.refs_5_) | copy-start | bytes 4915204
  56.8 7.0 %collective-permute-start = (f32[8,320]{1,0:T(8,128)S(1)}, f32[8,320]{1,0:T(8,128)}, u32[]{:S(2)}, u32[]{:S(2)}) collective-permute-start(f32[8,320]{1,0:T(8,128)S(1)} %param), channel_id=1, source_target_pairs={{1,2},{3,4},{5,6},{7,8},{9,10},{11,12},{13,14},{15,16},{17,18},{19... | collective-permute-start | bytes 30728 | tf_op jit(solution)/shard_map/cond/branch_0_fun/ppermute | solution.py:500
  63.9 26.2 %copy-start.23 = (s32[16]{0:T(128)S(1)}, s32[16]{0:T(128)}, u32[]{:S(2)}) copy-start(s32[16]{0:T(128)} %slots.7) | copy-start | bytes 196
  63.9 26.2 %copy-start.25 = (s32[16]{0:T(128)S(1)}, s32[16]{0:T(128)}, u32[]{:S(2)}) copy-start(s32[16]{0:T(128)} %get-tuple-element.406.across_slots) | copy-start | bytes 196
  63.9 26.2 %copy-start.26 = (s32[16]{0:T(128)S(1)}, s32[16]{0:T(128)}, u32[]{:S(2)}) copy-start(s32[16]{0:T(128)} %get-tuple-element.411.side_slots) | copy-start | bytes 196
  63.9 32.6 %copy-start.5 = (s32[16]{0:T(128)S(1)}, s32[16]{0:T(128)}, u32[]{:S(2)}) copy-start(s32[16]{0:T(128)} %get-tuple-element.370.send) | copy-start | bytes 196
  70.8 17.4 %collective-permute-start.103 = (bf16[32,320]{1,0:T(8,128)(2,1)S(1)}, bf16[32,320]{1,0:T(8,128)(2,1)S(1)}, u32[]{:S(2)}, u32[]{:S(2)}) collective-permute-start(bf16[32,320]{1,0:T(8,128)(2,1)S(1)} %solve.2.refs_0_), channel_id=1, source_target_pairs={{0,1},{1,0},{2,3},{3,2},{4,5},{5,4},{6,7},{7,6},{8,9},{9,8},{10,11... | collective-permute-start | bytes 61448 | tf_op jit(solution)/shard_map/ppermute | solution.py:497
  88.1 7.2 %collective-permute-start.104 = (bf16[64,320]{1,0:T(8,128)(2,1)S(1)}, bf16[64,320]{1,0:T(8,128)(2,1)S(1)}, u32[]{:S(2)}, u32[]{:S(2)}) collective-permute-start(bf16[64,320]{1,0:T(8,128)(2,1)S(1)} %maximum_select_fusion), channel_id=1, source_target_pairs={{1,2},{3,4},{5,6},{7,8},{9,10},{11,12},{13,14},{15,16},{17,18},{19... | collective-permute-start | bytes 122888 | tf_op jit(solution)/shard_map/ppermute | solution.py:500
  95.3 1.2 collective-permute-start.105
  95.5 18.5 %copy-start.20 = (bf16[320,640]{1,0:T(8,128)(2,1)S(1)}, bf16[320,640]{1,0:T(8,128)(2,1)}, u32[]{:S(2)}) copy-start(bf16[320,640]{1,0:T(8,128)(2,1)} %get-tuple-element.395.refs_9_) | copy-start | bytes 1228804
  106.9 2.1 %collective-permute-start.106 = (f32[8,320]{1,0:T(8,128)S(1)}, f32[8,320]{1,0:T(8,128)S(1)}, u32[]{:S(2)}, u32[]{:S(2)}) collective-permute-start(f32[8,320]{1,0:T(8,128)S(1)} %get-tuple-element.399), channel_id=1, source_target_pairs={{0,1},{1,0},{2,3},{3,2},{4,5},{5,4},{6,7},{7,6},{8,9},{9,8},{10,11... | collective-permute-start | bytes 30728 | tf_op jit(solution)/shard_map/ppermute | solution.py:497
  107.1 6.8 %collective-permute-start.107 = (f32[8,320]{1,0:T(8,128)S(1)}, f32[8,320]{1,0:T(8,128)S(1)}, u32[]{:S(2)}, u32[]{:S(2)}) collective-permute-start(f32[8,320]{1,0:T(8,128)S(1)} %get-tuple-element.401), channel_id=1, source_target_pairs={{1,2},{3,4},{5,6},{7,8},{9,10},{11,12},{13,14},{15,16},{17,18},{19... | collective-permute-start | bytes 30728 | tf_op jit(solution)/shard_map/ppermute | solution.py:500
  120.6 0.6 copy-start.2
  121.2 2.3 %collective-permute-start.108 = (f32[8,320]{1,0:T(8,128)S(1)}, f32[8,320]{1,0:T(8,128)S(1)}, u32[]{:S(2)}, u32[]{:S(2)}) collective-permute-start(f32[8,320]{1,0:T(8,128)S(1)} %get-tuple-element.402), channel_id=1, source_target_pairs={{0,1},{1,0},{2,3},{3,2},{4,5},{5,4},{6,7},{7,6},{8,9},{9,8},{10,11... | collective-permute-start | bytes 30728 | tf_op jit(solution)/shard_map/ppermute | solution.py:497
  121.2 6.8 %collective-permute-start.109 = (f32[8,320]{1,0:T(8,128)S(1)}, f32[8,320]{1,0:T(8,128)S(1)}, u32[]{:S(2)}, u32[]{:S(2)}) collective-permute-start(f32[8,320]{1,0:T(8,128)S(1)} %get-tuple-element.404), channel_id=1, source_target_pairs={{1,2},{3,4},{5,6},{7,8},{9,10},{11,12},{13,14},{15,16},{17,18},{19... | collective-permute-start | bytes 30728 | tf_op jit(solution)/shard_map/ppermute | solution.py:500
  123.5 4.5 %copy-start.21 = (f32[8,320]{1,0:T(8,128)}, f32[8,320]{1,0:T(8,128)S(1)}, u32[]{:S(2)}) copy-start(f32[8,320]{1,0:T(8,128)S(1)} %collective-permute-done.108.side) | copy-start | bytes 30724
  128.0 0.6 copy-start.22

commit v5 on v4

--- a/solution.py
+++ b/solution.py
@@ -18,6 +18,7 @@
 ROOMY = pltpu.CompilerParams(vmem_limit_bytes=57 << 20)
 FACING = pltpu.CompilerParams(vmem_limit_bytes=50 << 20)
 SNUG = pltpu.CompilerParams(vmem_limit_bytes=52 << 20)
+PLAIN = pltpu.CompilerParams(vmem_limit_bytes=16 << 20)
 SMALL = pl.CostEstimate(flops=1 << 20, bytes_accessed=1 << 20, transcendentals=0)
 NT = (((1,), (1,)), ((), ()))
 
@@ -30,31 +31,17 @@
     return jnp.dot(a, b, preferred_element_type=jnp.float32)
 
 
-def product(block, pivot):
-    return dot_nt(block.T, pivot).astype(jnp.bfloat16)
-
-
-def put(got, out, half):
-    width = got.shape[1]
-    tail = width - WIDE
-    out[:, pl.ds(pl.multiple_of(half * WIDE, WIDE), WIDE)] = got[:, :WIDE]
-
-    @pl.when(half == 0)
-    def _():
-        out[:, 2 * WIDE : 2 * WIDE + tail] = got[:, WIDE:]
-
-    @pl.when(half == 1)
-    def _():
-        out[:, 2 * WIDE + tail :] = got[:, WIDE:]
+def put_pair(first, second, out):
+    out[:, :WIDE] = first[:, :WIDE]
+    out[:, WIDE : 2 * WIDE] = second[:, :WIDE]
+    out[:, 2 * WIDE :] = jnp.concatenate([first[:, WIDE:], second[:, WIDE:]], axis=1)
 
 
 def pair_product(pivot, lower, upper, out):
     both = jnp.concatenate([lower.T, upper.T], axis=0)
     got = dot_nt(both, pivot).astype(jnp.bfloat16)
     width = pivot.shape[0]
-    out[:, :WIDE] = got[:width, :WIDE]
-    out[:, WIDE : 2 * WIDE] = got[width:, :WIDE]
-    out[:, 2 * WIDE :] = jnp.concatenate([got[:width, WIDE:], got[width:, WIDE:]], axis=1)
+    put_pair(got[:width], got[width:], out)
 
 
 def places_taken(slots, owner, slot_count, taken):
@@ -85,19 +72,28 @@
     def pair_copies(at):
         return [pltpu.make_async_copy(stage.at[at], out, outsem.at[at]) for out in outs]
 
-    def step(m, carry):
-        pltpu.make_async_copy(piv.at[0], pb.at[m], insem.at[0, m]).wait()
-        pltpu.make_async_copy(piv.at[0], mb.at[m], insem.at[1, m]).wait()
-        put(product(mb[m], pb[m]), stage.at[m // 2], m % 2)
-        for j, copy in enumerate(pair_copies(m // 2)):
-
-            @pl.when((m // 2 == j) & ((m % 2 == 1) | (m == count - 1)))
+    def step(j, carry):
+        def arrived(m):
+            pltpu.make_async_copy(piv.at[0], pb.at[m], insem.at[0, m]).wait()
+            pltpu.make_async_copy(piv.at[0], mb.at[m], insem.at[1, m]).wait()
+
+        arrived(2 * j)
+
+        @pl.when(2 * j + 1 < count)
+        def _():
+            arrived(2 * j + 1)
+
+        first, second = [dot_nt(mb[m].T, pb[m]).astype(jnp.bfloat16) for m in (2 * j, 2 * j + 1)]
+        put_pair(first, second, stage.at[j])
+        for i, copy in enumerate(pair_copies(j)):
+
+            @pl.when(j == i)
             def _(copy=copy):
                 copy.start()
 
         return carry
 
-    lax.fori_loop(0, count, step, 0)
+    lax.fori_loop(0, (count + 1) // 2, step, 0)
     for j in range(len(outs)):
 
         @pl.when(2 * j < count)
@@ -536,6 +532,10 @@
         cost_estimate=SMALL,
         name="first",
     )(element_slot, across[None], pivot_inverse, lower_block, upper_block)
+    pivot_inverse, lower_block, upper_block, face_blocks = [
+        pltpu.with_memory_space_constraint(array, pltpu.HBM)
+        for array in (pivot_inverse, lower_block, upper_block, face_blocks)
+    ]
     first, halo_across, halo_side, pivot_inverse, face_blocks = lax.optimization_barrier(
         (first, halo_across, halo_side, pivot_inverse, face_blocks)
     )
@@ -567,6 +567,7 @@
         out_shape=[whole] * 4 + [some] * 2 + [jax.ShapeDtypeStruct((2,), jnp.int32)],
         in_specs=[SMEM] * 5,
         out_specs=[SMEM] * 7,
+        compiler_params=PLAIN,
         cost_estimate=SMALL,
         name="plan",
     )(element_slot, slot_side, slot_across, slot_far, ids)
@@ -668,7 +669,11 @@
         unused = len(blocks) - len(got)
         if unused:
             got += pl.pallas_call(
-                nothing_kernel, out_shape=[jax.ShapeDtypeStruct(pair, bf16)] * unused, out_specs=[HBM] * unused, name="unused"
+                nothing_kernel,
+                out_shape=[jax.ShapeDtypeStruct(pair, bf16)] * unused,
+                out_specs=[HBM] * unused,
+                compiler_params=PLAIN,
+                name="unused",
             )()
         return (*got, to_across(vectors))
 
@@ -709,6 +714,7 @@
         in_specs=[SMEM, VMEM, VMEM, VMEM],
         out_specs=VMEM,
         scratch_shapes=[pltpu.VMEM((slot_count, width), f32)],
+        compiler_params=PLAIN,
         name="place",
     )(item_of_own, back_side, back_own, back_across)
 

time: 132 us -> 125 us (0.947)
  the two profiles are of different devices: /device:TPU:23 before, /device:TPU:8 now
where the time goes in v5:
time: 125 us; the launch traced here: 126 us
  Pallas kernels  55.8 us (45%)
  starting transfers between devices  39.4 us (32%)
  waiting for transfers between devices  23.6 us (19%)
  between operations  2.97 us (2%)
  local copies, waits for them, and re-layouts  2.1 us (2%)
  other arithmetic  2.08 us (2%)
    ppermute x10, starting transfers between devices, to_side(): return lax.ppermute(array, 'dom', side_pairs)  21.5 us
    pallas_call x2, Pallas kernels, face_part(): pl.pallas_call(functools.partial(face_kernel, counts), out_shape=[jax.Sha...  20.7 us
    ppermute x6, waiting for transfers between devices, to_across(): return lax.ppermute(array, 'dom', across_pairs)  20.4 us
    ppermute x6, starting transfers between devices, to_across(): return lax.ppermute(array, 'dom', across_pairs)  17.9 us
    pallas_call x2, Pallas kernels, solve(): pl.pallas_call(functools.partial(solve_kernel, last, rests), out_shape=ou...  13.5 us
    pallas_call x1, Pallas kernels, body(): pl.pallas_call(functools.partial(rest_kernel, blind, SIDES, slot_count),...  8.21 us
    pallas_call x1, Pallas kernels, body(): pl.pallas_call(functools.partial(staying_kernel, slot_count), out_shape=j...  8.09 us
    ppermute x10, waiting for transfers between devices, to_side(): return lax.ppermute(array, 'dom', side_pairs)  3.13 us
  transfers between devices with their start and end apart: 16, of which 8 were waited for; matrix products, arithmetic and copies ran while one was open for 1% of the time, Pallas kernels for 24%

profile of v5, /device:TPU:8, one launch (start us, length us, event | category | flops | bytes accessed | tf_op | source)
XLA Modules:
  0.0 125.9 jit_solution(15460697753667249708)
XLA Ops:
  0.0 0.7 convert_element_type.18.refs_1_
  0.7 0.7 subtract_convert_fusion
  1.4 0.1 broadcast_in_dim.62
  1.5 0.1 pad_maximum_fusion
  1.6 1.2 collective-permute-done.95
  2.7 0.2 slice_reduce_fusion
  2.9 0.1 broadcast_select_fusion
  3.0 0.1 pad_maximum_fusion.1
  3.1 4.0 %collective-permute-start.96 = (bf16[16,384]{1,0:T(8,128)(2,1)S(1)}, bf16[16,384]{1,0:T(8,128)(2,1)S(1)}, u32[]{:S(2)}, u32[]{:S(2)}) collective-permute-start(bf16[16,384]{1,0:T(8,128)(2,1)S(1)} %pad_maximum_fusion.1), channel_id=1, source_target_pairs={{1,2},{3,4},{5,6},{7,8},{9,10},{11,12},{13,14},{15,16},{17,18},{19... | collective-permute-start | bytes 36872 | tf_op jit(solution)/shard_map/ppermute | solution.py:496
  7.1 1.3 %first.1 = bf16[4,320,640]{2,1,0:T(8,128)(2,1)} custom-call(s32[16]{0:T(128)} %slots.7, s32[1]{0:T(128)} %bitcast.across, bf16[16,320,320]{2,1,0:T(8,128)(2,1)} %refs_5_, bf16[16,320,320]{2,1,0:T(8,128)(2,1)} %low.5, bf16[16,320,320]{2,1,0:T(8,128)(2,1)} %upp.5), custom_call_target="tpu_custom_call" | custom-call | flops 1048576 | bytes 1048576 | tf_op jit(solution)/shard_map/first/pallas_call | solution.py:524
  8.4 1.4 %collective-permute-done.96 = bf16[16,384]{1,0:T(8,128)(2,1)S(1)} collective-permute-done((bf16[16,384]{1,0:T(8,128)(2,1)S(1)}, bf16[16,384]{1,0:T(8,128)(2,1)S(1)}, u32[]{:S(2)}, u32[]{:S(2)}) %collective-permute-start.96) | collective-permute-done | bytes 12320 | tf_op jit(solution)/shard_map/ppermute | solution.py:496
  9.9 6.1 %collective-permute-start.97 = (bf16[4,320,640]{2,1,0:T(8,128)(2,1)}, bf16[4,320,640]{2,1,0:T(8,128)(2,1)S(1)}, u32[]{:S(2)}, u32[]{:S(2)}) collective-permute-start(bf16[4,320,640]{2,1,0:T(8,128)(2,1)} %first.1), channel_id=1, source_target_pairs={{1,2},{3,4},{5,6},{7,8},{9,10},{11,12},{13,14},{15,16},{17,18},{19... | collective-permute-start | bytes 4915208 | tf_op jit(solution)/shard_map/ppermute | solution.py:496
  16.1 0.1 reshape.34.index
  16.2 0.1 pad_add_fusion.ids
  16.2 0.2 select_reduce_fusion
  16.5 2.8 %plan.1 = (s32[32]{0:T(128)S(1)}, s32[32]{0:T(128)S(1)}, s32[32]{0:T(128)S(1)}, s32[32]{0:T(128)S(1)}, s32[16]{0:T(128)S(1)}, /*index=5*/s32[16]{0:T(128)S(1)}, s32[2]{0:T(128)S(1)}) custom-call(s32[16]{0:T(128)S(1)} %copy-done.1, s32[16]{0:T(128)S(1)} %get-tuple-element.411.side_slots, s32[16]{0:T(128)S(1)} %get-tuple-element.406.across_slots, ...), custom_call_target="tpu_custom_call" | custom-call | flops 1048576 | bytes 1048576 | tf_op jit(solution)/shard_map/plan/pallas_call | solution.py:565
  19.3 10.3 %faces.2 = (f32[8,320]{1,0:T(8,128)S(1)}, f32[8,320]{1,0:T(8,128)S(1)}, f32[16,320]{1,0:T(8,128)S(1)}) custom-call(s32[16]{0:T(128)S(1)} %get-tuple-element.370.send, s32[64,1]{1,0:T(8,128)S(1)} %reshape.34.index, f32[16,320]{1,0:T(8,128)S(1)} %copy-done, bf16[16,320]{1,0:T(8,128)(2,1)S(1)} %bitcast.8, bf16[16,320]{1,0:T(8,128)(2,1)S(1)} %convert_element_type.18.refs_1_, ...), custom_call_target="tpu_custom_call" | custom-call | flops 1048576 | bytes 1048576 | tf_op jit(solution)/shard_map/faces/pallas_call | solution.py:611
  29.7 0.1 collective-permute-start.102
  29.8 8.2 %rest.1 = (bf16[2,320,640]{2,1,0:T(8,128)(2,1)}, bf16[2,320,640]{2,1,0:T(8,128)(2,1)}, bf16[2,320,640]{2,1,0:T(8,128)(2,1)}, bf16[2,320,640]{2,1,0:T(8,128)(2,1)...) custom-call(s32[16]{0:T(128)} %slots.7, ...), custom_call_target="tpu_custom_call" | custom-call | flops 1048576 | bytes 1048576 | tf_op jit(solution)/shard_map/rest/pallas_call | solution.py:547
  38.0 0.1 collective-permute-start.98
  38.1 0.5 collective-permute-start.99
  38.6 0.1 collective-permute-start.100
  38.6 0.4 collective-permute-start.101
  39.1 0.1 reshape.26
  39.2 8.1 %staying.1.refs_4_ = bf16[16,320,640]{2,1,0:T(8,128)(2,1)} custom-call(s32[16]{0:T(128)} %slots.7, s32[1]{0:T(128)} %bitcast.2.me, bf16[16,320,320]{2,1,0:T(8,128)(2,1)} %refs_5_, bf16[16,320,320]{2,1,0:T(8,128)(2,1)} %low.5, bf16[16,320,320]{2,1,0:T(8,128)(2,1)} %upp.5), custom_call_target="tpu_custom_call" | custom-call | flops 1048576 | bytes 1048576 | tf_op jit(solution)/shard_map/staying/pallas_call | solution.py:575
  47.3 0.7 fusion.18
  50.6 6.9 %conditional.1 = (bf16[320,640]{1,0:T(8,128)(2,1)}, bf16[320,640]{1,0:T(8,128)(2,1)}, bf16[320,640]{1,0:T(8,128)(2,1)}, bf16[320,640]{1,0:T(8,128)(2,1)}, f32[8,320]{1,0:T(8,128)}) conditional(s32[]{:T(128)} %clamp.3, f32[8,320]{1,0:T(8,128)S(1)} %get-tuple-element.387, (bf16[320,640]{1,0:T(8,128)(2,1)}, ...), branch_computations={%region_0.1_spmd, %region_1.2_spmd, %region_2.3_spmd, %region_3.4_... | conditional | bytes 6594800 | solution.py:694
  50.6 1.9 %collective-permute-start = (f32[8,320]{1,0:T(8,128)S(1)}, f32[8,320]{1,0:T(8,128)}, u32[]{:S(2)}, u32[]{:S(2)}) collective-permute-start(f32[8,320]{1,0:T(8,128)S(1)} %param), channel_id=1, source_target_pairs={{1,2},{3,4},{5,6},{7,8},{9,10},{11,12},{13,14},{15,16},{17,18},{19... | collective-permute-start | bytes 30728 | tf_op jit(solution)/shard_map/cond/branch_0_fun/ppermute | solution.py:496
  52.6 5.0 %collective-permute-done = f32[8,320]{1,0:T(8,128)} collective-permute-done((f32[8,320]{1,0:T(8,128)S(1)}, f32[8,320]{1,0:T(8,128)}, u32[]{:S(2)}, u32[]{:S(2)}) %collective-permute-start) | collective-permute-done | bytes 10272 | tf_op jit(solution)/shard_map/cond/branch_0_fun/ppermute | solution.py:496
  57.5 6.8 %solve.2.refs_0_ = bf16[32,320]{1,0:T(8,128)(2,1)S(1)} custom-call(s32[32]{0:T(128)S(1)} %get-tuple-element.361.table, s32[32]{0:T(128)S(1)} %get-tuple-element.362.lower_at, s32[32]{0:T(128)S(1)} %get-tuple-element.363.upper_at, s32[32]{0:T(128)S(1)} %get-tuple-element.364.back, s32[2]{0:T(128)S(1)} %get-tuple-element.380.counts, ...), custom_call_target="tpu_custom_call" | custom-call | flops 1048576 | bytes 1048576 | tf_op jit(solution)/shard_map/solve/pallas_call | solution.py:643
  64.4 20.0 %collective-permute-start.103 = (bf16[32,320]{1,0:T(8,128)(2,1)S(1)}, bf16[32,320]{1,0:T(8,128)(2,1)S(1)}, u32[]{:S(2)}, u32[]{:S(2)}) collective-permute-start(bf16[32,320]{1,0:T(8,128)(2,1)S(1)} %solve.2.refs_0_), channel_id=1, source_target_pairs={{0,1},{1,0},{2,3},{3,2},{4,5},{5,4},{6,7},{7,6},{8,9},{9,8},{10,11... | collective-permute-start | bytes 61448 | tf_op jit(solution)/shard_map/ppermute | solution.py:493
  84.4 0.8 collective-permute-done.103.refs_1_
  85.3 1.9 %collective-permute-start.104 = (bf16[64,320]{1,0:T(8,128)(2,1)S(1)}, bf16[64,320]{1,0:T(8,128)(2,1)S(1)}, u32[]{:S(2)}, u32[]{:S(2)}) collective-permute-start(bf16[64,320]{1,0:T(8,128)(2,1)S(1)} %maximum_select_fusion), channel_id=1, source_target_pairs={{1,2},{3,4},{5,6},{7,8},{9,10},{11,12},{13,14},{15,16},{17,18},{19... | collective-permute-start | bytes 122888 | tf_op jit(solution)/shard_map/ppermute | solution.py:496
  87.2 0.1 pad_add_fusion.1
  87.3 0.8 gather_fusion
  88.1 0.1 reshape.25
  88.2 4.4 %collective-permute-done.104.refs_2_ = bf16[64,320]{1,0:T(8,128)(2,1)S(1)} collective-permute-done((bf16[64,320]{1,0:T(8,128)(2,1)S(1)}, bf16[64,320]{1,0:T(8,128)(2,1)S(1)}, u32[]{:S(2)}, u32[]{:S(2)}) %collective-permute-start.104) | collective-permute-done | bytes 40992 | tf_op jit(solution)/shard_map/ppermute | solution.py:496
  92.6 0.1 reshape.35.index
  92.6 1.1 collective-permute-done.105.refs_3_
  93.8 10.4 %faces.3 = (f32[8,320]{1,0:T(8,128)S(1)}, f32[8,320]{1,0:T(8,128)S(1)}, f32[16,320]{1,0:T(8,128)S(1)}) custom-call(s32[16]{0:T(128)S(1)} %get-tuple-element.370.send, s32[64,1]{1,0:T(8,128)S(1)} %reshape.35.index, f32[16,320]{1,0:T(8,128)S(1)} %copy-done, bf16[32,320]{1,0:T(8,128)(2,1)S(1)} %solve.2.refs_0_, ...), custom_call_target="tpu_custom_call" | custom-call | flops 1048576 | bytes 1048576 | tf_op jit(solution)/shard_map/faces/pallas_call | solution.py:611
  104.1 0.2 collective-permute-start.106
  104.4 1.9 %collective-permute-start.107 = (f32[8,320]{1,0:T(8,128)S(1)}, f32[8,320]{1,0:T(8,128)S(1)}, u32[]{:S(2)}, u32[]{:S(2)}) collective-permute-start(f32[8,320]{1,0:T(8,128)S(1)} %get-tuple-element.401), channel_id=1, source_target_pairs={{1,2},{3,4},{5,6},{7,8},{9,10},{11,12},{13,14},{15,16},{17,18},{19... | collective-permute-start | bytes 30728 | tf_op jit(solution)/shard_map/ppermute | solution.py:496
  106.3 4.9 %collective-permute-done.107.refs_12_ = f32[8,320]{1,0:T(8,128)S(1)} collective-permute-done((f32[8,320]{1,0:T(8,128)S(1)}, f32[8,320]{1,0:T(8,128)S(1)}, u32[]{:S(2)}, u32[]{:S(2)}) %collective-permute-start.107) | collective-permute-done | bytes 10272 | tf_op jit(solution)/shard_map/ppermute | solution.py:496
  111.2 6.7 %solve.3 = (f32[8,320]{1,0:T(8,128)S(1)}, f32[16,320]{1,0:T(8,128)S(1)}, f32[8,320]{1,0:T(8,128)S(1)}) custom-call(s32[32]{0:T(128)S(1)} %get-tuple-element.361.table, s32[32]{0:T(128)S(1)} %get-tuple-element.362.lower_at, s32[32]{0:T(128)S(1)} %get-tuple-element.363.upper_at, s32[32]{0:T(128)S(1)} %get-tuple-element.364.back, ...), custom_call_target="tpu_custom_call" | custom-call | flops 1048576 | bytes 1048576 | tf_op jit(solution)/shard_map/solve/pallas_call | solution.py:643
  117.9 0.1 collective-permute-start.108
  117.9 2.0 %collective-permute-start.109 = (f32[8,320]{1,0:T(8,128)S(1)}, f32[8,320]{1,0:T(8,128)S(1)}, u32[]{:S(2)}, u32[]{:S(2)}) collective-permute-start(f32[8,320]{1,0:T(8,128)S(1)} %get-tuple-element.404), channel_id=1, source_target_pairs={{1,2},{3,4},{5,6},{7,8},{9,10},{11,12},{13,14},{15,16},{17,18},{19... | collective-permute-start | bytes 30728 | tf_op jit(solution)/shard_map/ppermute | solution.py:496
  120.0 4.8 %collective-permute-done.109.across = f32[8,320]{1,0:T(8,128)S(1)} collective-permute-done((f32[8,320]{1,0:T(8,128)S(1)}, f32[8,320]{1,0:T(8,128)S(1)}, u32[]{:S(2)}, u32[]{:S(2)}) %collective-permute-start.109) | collective-permute-done | bytes 10272 | tf_op jit(solution)/shard_map/ppermute | solution.py:496
  124.8 1.2 place.1
  (34 shorter events, 0.1 us)
Async XLA Ops:
  1.6 1.2 collective-permute-start.95
  3.1 6.8 %collective-permute-start.96 = (bf16[16,384]{1,0:T(8,128)(2,1)S(1)}, bf16[16,384]{1,0:T(8,128)(2,1)S(1)}, u32[]{:S(2)}, u32[]{:S(2)}) collective-permute-start(bf16[16,384]{1,0:T(8,128)(2,1)S(1)} %pad_maximum_fusion.1), channel_id=1, source_target_pairs={{1,2},{3,4},{5,6},{7,8},{9,10},{11,12},{13,14},{15,16},{17,18},{19... | collective-permute-start | bytes 36872 | tf_op jit(solution)/shard_map/ppermute | solution.py:496
  7.1 8.9 %copy-start.8 = (s32[4,16]{1,0:T(4,128)S(1)}, s32[4,16]{1,0:T(4,128)}, u32[]{:S(2)}) copy-start(s32[4,16]{1,0:T(4,128)} %param.39) | copy-start | bytes 772
  7.1 9.4 %copy-start.1 = (s32[16]{0:T(128)S(1)}, s32[16]{0:T(128)}, u32[]{:S(2)}) copy-start(s32[16]{0:T(128)} %slots.7) | copy-start | bytes 196
  7.1 12.2 %copy-start = (f32[16,320]{1,0:T(8,128)S(1)}, f32[16,320]{1,0:T(8,128)}, u32[]{:S(2)}) copy-start(f32[16,320]{1,0:T(8,128)} %rhs.7) | copy-start | bytes 61444
  9.9 37.4 %collective-permute-start.97 = (bf16[4,320,640]{2,1,0:T(8,128)(2,1)}, bf16[4,320,640]{2,1,0:T(8,128)(2,1)S(1)}, u32[]{:S(2)}, u32[]{:S(2)}) collective-permute-start(bf16[4,320,640]{2,1,0:T(8,128)(2,1)} %first.1), channel_id=1, source_target_pairs={{1,2},{3,4},{5,6},{7,8},{9,10},{11,12},{13,14},{15,16},{17,18},{19... | collective-permute-start | bytes 4915208 | tf_op jit(solution)/shard_map/ppermute | solution.py:496
  16.2 13.4 %copy-start.6 = (s32[3]{0:T(128)}, s32[3]{0:T(128)S(1)}, u32[]{:S(2)}) copy-start(s32[3]{0:T(128)S(1)} %pad_add_fusion.ids) | copy-start | bytes 40
  16.5 13.2 %copy-start.3 = (s32[16]{0:T(128)}, s32[16]{0:T(128)S(1)}, u32[]{:S(2)}) copy-start(s32[16]{0:T(128)S(1)} %get-tuple-element.406.across_slots) | copy-start | bytes 196
  16.5 13.2 %copy-start.5 = (s32[16]{0:T(128)}, s32[16]{0:T(128)S(1)}, u32[]{:S(2)}) copy-start(s32[16]{0:T(128)S(1)} %get-tuple-element.405.far_slots) | copy-start | bytes 196
  29.7 9.0 %collective-permute-start.102 = (f32[8,320]{1,0:T(8,128)S(1)}, f32[8,320]{1,0:T(8,128)S(1)}, u32[]{:S(2)}, u32[]{:S(2)}) collective-permute-start(f32[8,320]{1,0:T(8,128)S(1)} %get-tuple-element.379), channel_id=1, source_target_pairs={{0,1},{1,0},{2,3},{3,2},{4,5},{5,4},{6,7},{7,6},{8,9},{9,8},{10,11... | collective-permute-start | bytes 30728 | tf_op jit(solution)/shard_map/ppermute | solution.py:493
  38.0 9.3 %collective-permute-start.98 = (bf16[2,320,640]{2,1,0:T(8,128)(2,1)}, bf16[2,320,640]{2,1,0:T(8,128)(2,1)S(1)}, u32[]{:S(2)}, u32[]{:S(2)}) collective-permute-start(bf16[2,320,640]{2,1,0:T(8,128)(2,1)} %get-tuple-element.375), channel_id=1, source_target_pairs={{0,1},{1,0},{2,3},{3,2},{4,5},{5,4},{6,7},{7,6},{8,9},{9,8},{10,11... | collective-permute-start | bytes 2457608 | tf_op jit(solution)/shard_map/ppermute | solution.py:493
  38.1 9.2 %collective-permute-start.99 = (bf16[2,320,640]{2,1,0:T(8,128)(2,1)}, bf16[2,320,640]{2,1,0:T(8,128)(2,1)S(1)}, u32[]{:S(2)}, u32[]{:S(2)}) collective-permute-start(bf16[2,320,640]{2,1,0:T(8,128)(2,1)} %get-tuple-element.376), channel_id=1, source_target_pairs={{0,1},{1,0},{2,3},{3,2},{4,5},{5,4},{6,7},{7,6},{8,9},{9,8},{10,11... | collective-permute-start | bytes 2457608 | tf_op jit(solution)/shard_map/ppermute | solution.py:493
  38.6 8.7 %collective-permute-start.100 = (bf16[2,320,640]{2,1,0:T(8,128)(2,1)}, bf16[2,320,640]{2,1,0:T(8,128)(2,1)}, u32[]{:S(2)}, u32[]{:S(2)}) collective-permute-start(bf16[2,320,640]{2,1,0:T(8,128)(2,1)} %get-tuple-element.377), channel_id=1, source_target_pairs={{0,1},{1,0},{2,3},{3,2},{4,5},{5,4},{6,7},{7,6},{8,9},{9,8},{10,11... | collective-permute-start | bytes 2457608 | tf_op jit(solution)/shard_map/ppermute | solution.py:493
  38.6 8.6 %collective-permute-start.101 = (bf16[2,320,640]{2,1,0:T(8,128)(2,1)}, bf16[2,320,640]{2,1,0:T(8,128)(2,1)}, u32[]{:S(2)}, u32[]{:S(2)}) collective-permute-start(bf16[2,320,640]{2,1,0:T(8,128)(2,1)} %get-tuple-element.378), channel_id=1, source_target_pairs={{0,1},{1,0},{2,3},{3,2},{4,5},{5,4},{6,7},{7,6},{8,9},{9,8},{10,11... | collective-permute-start | bytes 2457608 | tf_op jit(solution)/shard_map/ppermute | solution.py:493
  47.3 10.2 %copy-start.7 = (bf16[4,320,640]{2,1,0:T(8,128)(2,1)}, bf16[4,320,640]{2,1,0:T(8,128)(2,1)S(1)}, u32[]{:S(2)}) copy-start(bf16[4,320,640]{2,1,0:T(8,128)(2,1)S(1)} %collective-permute-done.97.refs_5_) | copy-start | bytes 4915204
  50.6 6.9 %collective-permute-start = (f32[8,320]{1,0:T(8,128)S(1)}, f32[8,320]{1,0:T(8,128)}, u32[]{:S(2)}, u32[]{:S(2)}) collective-permute-start(f32[8,320]{1,0:T(8,128)S(1)} %param), channel_id=1, source_target_pairs={{1,2},{3,4},{5,6},{7,8},{9,10},{11,12},{13,14},{15,16},{17,18},{19... | collective-permute-start | bytes 30728 | tf_op jit(solution)/shard_map/cond/branch_0_fun/ppermute | solution.py:496
  57.5 29.7 %copy-start.2 = (s32[16]{0:T(128)S(1)}, s32[16]{0:T(128)}, u32[]{:S(2)}) copy-start(s32[16]{0:T(128)} %slots.7) | copy-start | bytes 196
  57.5 29.7 %copy-start.4 = (s32[16]{0:T(128)S(1)}, s32[16]{0:T(128)}, u32[]{:S(2)}) copy-start(s32[16]{0:T(128)} %copy-done.3) | copy-start | bytes 196
  64.4 20.9 %collective-permute-start.103 = (bf16[32,320]{1,0:T(8,128)(2,1)S(1)}, bf16[32,320]{1,0:T(8,128)(2,1)S(1)}, u32[]{:S(2)}, u32[]{:S(2)}) collective-permute-start(bf16[32,320]{1,0:T(8,128)(2,1)S(1)} %solve.2.refs_0_), channel_id=1, source_target_pairs={{0,1},{1,0},{2,3},{3,2},{4,5},{5,4},{6,7},{7,6},{8,9},{9,8},{10,11... | collective-permute-start | bytes 61448 | tf_op jit(solution)/shard_map/ppermute | solution.py:493
  85.3 7.2 %collective-permute-start.104 = (bf16[64,320]{1,0:T(8,128)(2,1)S(1)}, bf16[64,320]{1,0:T(8,128)(2,1)S(1)}, u32[]{:S(2)}, u32[]{:S(2)}) collective-permute-start(bf16[64,320]{1,0:T(8,128)(2,1)S(1)} %maximum_select_fusion), channel_id=1, source_target_pairs={{1,2},{3,4},{5,6},{7,8},{9,10},{11,12},{13,14},{15,16},{17,18},{19... | collective-permute-start | bytes 122888 | tf_op jit(solution)/shard_map/ppermute | solution.py:496
  92.5 1.2 collective-permute-start.105
  104.1 2.2 %collective-permute-start.106 = (f32[8,320]{1,0:T(8,128)S(1)}, f32[8,320]{1,0:T(8,128)S(1)}, u32[]{:S(2)}, u32[]{:S(2)}) collective-permute-start(f32[8,320]{1,0:T(8,128)S(1)} %get-tuple-element.399), channel_id=1, source_target_pairs={{0,1},{1,0},{2,3},{3,2},{4,5},{5,4},{6,7},{7,6},{8,9},{9,8},{10,11... | collective-permute-start | bytes 30728 | tf_op jit(solution)/shard_map/ppermute | solution.py:493
  104.4 6.8 %collective-permute-start.107 = (f32[8,320]{1,0:T(8,128)S(1)}, f32[8,320]{1,0:T(8,128)S(1)}, u32[]{:S(2)}, u32[]{:S(2)}) collective-permute-start(f32[8,320]{1,0:T(8,128)S(1)} %get-tuple-element.401), channel_id=1, source_target_pairs={{1,2},{3,4},{5,6},{7,8},{9,10},{11,12},{13,14},{15,16},{17,18},{19... | collective-permute-start | bytes 30728 | tf_op jit(solution)/shard_map/ppermute | solution.py:496
  117.9 2.1 %collective-permute-start.108 = (f32[8,320]{1,0:T(8,128)S(1)}, f32[8,320]{1,0:T(8,128)S(1)}, u32[]{:S(2)}, u32[]{:S(2)}) collective-permute-start(f32[8,320]{1,0:T(8,128)S(1)} %get-tuple-element.402), channel_id=1, source_target_pairs={{0,1},{1,0},{2,3},{3,2},{4,5},{5,4},{6,7},{7,6},{8,9},{9,8},{10,11... | collective-permute-start | bytes 30728 | tf_op jit(solution)/shard_map/ppermute | solution.py:493
  117.9 6.8 %collective-permute-start.109 = (f32[8,320]{1,0:T(8,128)S(1)}, f32[8,320]{1,0:T(8,128)S(1)}, u32[]{:S(2)}, u32[]{:S(2)}) collective-permute-start(f32[8,320]{1,0:T(8,128)S(1)} %get-tuple-element.404), channel_id=1, source_target_pairs={{1,2},{3,4},{5,6},{7,8},{9,10},{11,12},{13,14},{15,16},{17,18},{19... | collective-permute-start | bytes 30728 | tf_op jit(solution)/shard_map/ppermute | solution.py:496
